TPU v7x, 256 devices: a whole 4x4x8 slice. The times are simulated.
256 devices in a mesh: section: 8 (over x, core), expert: 32 (over z, y).
Axes of the slice: x: 4, y: 4, z: 8, core: 2. Of those that a mesh axis runs over, the one named last changes fastest.
Arguments:
- fwd_handoff: bfloat16 [8, 4096, 1536], P('section', 'expert'), may hold values from -27 to 27
- saved_input: bfloat16 [8, 4096, 1536], P('section', 'expert'), may hold values from -27 to 27
- grad_handoff: bfloat16 [8, 4096, 1536], P('section', 'expert'), may hold values from -3 to 3
- gain: float32 [8, 1536], P('section'), may hold values from 0.1 to 1.9
- route_fwd: int32 [8, 4096, 2], P('section', 'expert'), may hold values from 0 to 7, as said below
- gate_fwd: float32 [8, 4096, 2], P('section', 'expert'), may hold values from 0.1 to 1
- route_bwd: int32 [8, 4096, 2], P('section', 'expert'), may hold values from 0 to 7, as said below
- slot_bwd: int32 [8, 4096, 2], P('section', 'expert'), may hold values from 0 to 31, as said below
- gate_bwd: float32 [8, 4096, 2], P('section', 'expert'), may hold values from 0.1 to 1
- w_in: bfloat16 [8, 1536, 24576], P('section', None, 'expert'), may hold values from -0.15625 to 0.15625
- w_out: bfloat16 [8, 24576, 1536], P('section', 'expert'), may hold values from -0.109375 to 0.109375
- saved_pre: bfloat16 [8, 32768, 768], P('section', 'expert'), may hold values from -5 to 5
Outputs:
- section_out: bfloat16 [8, 4096, 1536], P('section', 'expert')
- input_grad: bfloat16 [8, 4096, 1536], P('section', 'expert')
- grad_w_in: bfloat16 [8, 1536, 24576], P('section', None, 'expert')
- grad_w_out: bfloat16 [8, 24576, 1536], P('section', 'expert')
Inputs may be any that keep to these rules, and one draw needn't show every extreme that they name: `route_fwd`: each token names two different experts; in each aligned block of 128 tokens (the tokens of one device) every expert is named by exactly 32 token-choices. `route_bwd`: each token names two different experts; in each aligned block of 128 tokens (the tokens of one device) every expert is named by exactly 32 token-choices. `slot_bwd`: in each aligned block of 128 tokens, the token-choices that name one expert hold the slots 0 to 31, each once.
All inputs are finite; a program needn't handle non-finite values.
Results may differ from a plain program's by a relative error of at most 0.009.
Values may be sent and summed in bfloat16 or wider, within the bound.
No kernel may reach another device: no remote copies, remote signals or barrier semaphores. Data moves between devices by JAX's collectives and lax.ppermute only.
A program may use at most 128 MiB of HBM per device.

v0:
```python
import functools

import jax
import jax.numpy as jnp
from jax import lax
from jax.experimental import pallas as pl
from jax.experimental.pallas import tpu as pltpu
from jax.sharding import PartitionSpec as P

EXPERTS = 8


EPSILON = 1e-06
TANH_SCALE = 0.7978845608028654
CUBIC_COEF = 0.044715


def shifted(block, axis, distance):
    devices = range(lax.axis_size(axis))
    route = [((i - distance) % len(devices), i) for i in devices]
    return lax.ppermute(block, axis, route)


def turned(block, groups, distance):
    route = [
        (e * groups + g, e * groups + (g + distance) % groups)
        for e in range(EXPERTS)
        for g in range(groups)
    ]
    return lax.ppermute(block, "expert", route)


def exchange(block, groups):
    index_groups = [[e * groups + g for e in range(EXPERTS)] for g in range(groups)]
    return lax.all_to_all(
        block, "expert", split_axis=0, concat_axis=0, tiled=True, axis_index_groups=index_groups
    )


def gather_group(chunk, groups):
    half = chunk.shape[0] // 2
    from_left = turned(chunk, groups, 1)
    from_right = turned(chunk, groups, -1)
    opposite_top = turned(from_left[:half], groups, 1)
    opposite_bottom = turned(from_right[half:], groups, -1)
    return [chunk, from_left, from_right, opposite_top, opposite_bottom]


def after(value, *earlier):
    return lax.optimization_barrier((value, *earlier))[0]


def after(value, *earlier):
    return lax.optimization_barrier((value, *earlier))[0]


VMEM_BYTES = 30 * 1024 * 1024


def matmul(left, right, dims):
    return lax.dot_general(left, right, (dims, ((), ())), preferred_element_type=jnp.float32)


def call(kernel, out_shapes, operands, flops, in_specs=None, out_specs=None, **more):
    moved = sum(a.size * a.dtype.itemsize for a in operands)
    moved += sum(o.size * o.dtype.itemsize for o in out_shapes)
    if in_specs is None and "grid_spec" not in more:

        def whole(array):
            return pl.BlockSpec(array.shape, lambda i: (0,) * len(array.shape))

        more["grid"] = (1,)
        more["in_specs"] = [whole(a) for a in operands]
        more["out_specs"] = [whole(o) for o in out_shapes]
    elif in_specs is not None:
        more["in_specs"] = in_specs
        more["out_specs"] = out_specs
    return pl.pallas_call(
        kernel,
        out_shape=out_shapes,
        cost_estimate=pl.CostEstimate(flops=flops, bytes_accessed=moved, transcendentals=0),
        compiler_params=pltpu.CompilerParams(vmem_limit_bytes=VMEM_BYTES),
        **more,
    )(*operands)


def rms_scale(widened):
    return lax.rsqrt(jnp.mean(widened * widened, axis=-1, keepdims=True) + EPSILON)


def normed_of(tokens_ref, gain_ref):
    widened = tokens_ref[...].astype(jnp.float32)
    return (widened * rms_scale(widened) * gain_ref[...]).astype(jnp.bfloat16)


def hits_of(target, rows):
    ids = lax.broadcasted_iota(jnp.int32, (target.shape[0], rows), 1)
    return (target == ids).astype(jnp.float32).astype(jnp.bfloat16)


def forward_targets(route, cap_rows):
    tokens, choices = route.shape
    lanes = lax.broadcasted_iota(jnp.int32, (tokens, 128), 1)
    below = (
        lax.broadcasted_iota(jnp.int32, (tokens, tokens), 0)
        > lax.broadcasted_iota(jnp.int32, (tokens, tokens), 1)
    ).astype(jnp.float32)
    below = below.astype(jnp.bfloat16)
    ahead = jnp.zeros((1, 128), jnp.float32)
    targets = []
    for k in range(choices):
        expert = route[:, k : k + 1]
        named = (expert == lanes).astype(jnp.float32)
        count = matmul(below, named.astype(jnp.bfloat16), ((1,), (0,))) + ahead
        rank = jnp.sum(named * count, axis=1, keepdims=True).astype(jnp.int32)
        targets.append(expert * cap_rows + rank)
        ahead = ahead + jnp.sum(named, axis=0, keepdims=True)
    return targets


def backward_targets(route, slot, cap_rows):
    target = route * cap_rows + slot
    return [target[:, k : k + 1] for k in range(target.shape[1])]


def pick_forward_kernel(cap_rows, tokens_ref, gain_ref, route_ref, out_ref):
    normed = normed_of(tokens_ref, gain_ref)
    pick = sum(
        hits_of(t, out_ref.shape[0]).astype(jnp.float32)
        for t in forward_targets(route_ref[...], cap_rows)
    ).astype(jnp.bfloat16)
    out_ref[...] = matmul(pick, normed, ((0,), (0,))).astype(jnp.bfloat16)


def pick_backward_kernel(cap_rows, tokens_ref, gain_ref, route_ref, slot_ref, out_ref):
    normed = normed_of(tokens_ref, gain_ref)
    pick = sum(
        hits_of(t, out_ref.shape[0]).astype(jnp.float32)
        for t in backward_targets(route_ref[...], slot_ref[...], cap_rows)
    ).astype(jnp.bfloat16)
    out_ref[...] = matmul(pick, normed, ((0,), (0,))).astype(jnp.bfloat16)


def pick_grad_kernel(cap_rows, cot_ref, gate_ref, route_ref, slot_ref, out_ref):
    cot = cot_ref[...].astype(jnp.float32)
    total = None
    for k, t in enumerate(backward_targets(route_ref[...], slot_ref[...], cap_rows)):
        gated = (gate_ref[:, k : k + 1] * cot).astype(jnp.bfloat16)
        part = matmul(hits_of(t, out_ref.shape[0]), gated, ((0,), (0,)))
        total = part if total is None else total + part
    out_ref[...] = total.astype(jnp.bfloat16)


def backward_kernel(sizes, place_ref, w_in_ref, w_out_ref, *refs):
    chunks = len(sizes)
    pieces = sum(len(s) for s in sizes)
    grads = list(refs[:pieces])
    pres = refs[pieces : pieces + chunks]
    outs = refs[pieces + chunks :]
    hidden_refs = outs[:chunks]
    pre_grad_refs = outs[chunks : 2 * chunks]
    back_refs = outs[2 * chunks : 3 * chunks]
    wide = outs[3 * chunks]
    for c in range(chunks):
        row = 0
        for size in sizes[c]:
            wide[row : row + size, :] = matmul(grads.pop(0)[...], w_out_ref[...], ((1,), (1,)))
            row += size
        blocks, _, slots, _ = pres[c].shape
        for b in range(blocks):
            span = slice(b * slots, (b + 1) * slots)
            pre = pres[c][b, 0].astype(jnp.float32)
            square = pre * pre
            inner = TANH_SCALE * (pre + CUBIC_COEF * square * pre)
            tangent = jnp.tanh(inner)
            half = 0.5 * (1.0 + tangent)
            derivative = half + 0.5 * pre * (1.0 - tangent * tangent) * TANH_SCALE * (
                1.0 + 3.0 * CUBIC_COEF * square
            )
            hidden_refs[c][span, :] = (pre * half).astype(jnp.bfloat16)
            pre_grad_refs[c][span, :] = (wide[span, :] * derivative).astype(jnp.bfloat16)
        back_refs[c][...] = matmul(pre_grad_refs[c][...], w_in_ref[...], ((1,), (1,))).astype(
            jnp.bfloat16
        )


def forward_kernel(sizes, w_in_ref, w_out_ref, *refs):
    chunks = len(sizes)
    pieces = sum(len(s) for s in sizes)
    rows = list(refs[:pieces])
    outs = refs[pieces : pieces + chunks]
    wide, hidden = refs[pieces + chunks :]
    for c in range(chunks):
        row = 0
        for size in sizes[c]:
            wide[row : row + size, :] = matmul(rows.pop(0)[...], w_in_ref[...], ((1,), (0,)))
            row += size
        for b in range(row // 32):
            span = slice(b * 32, (b + 1) * 32)
            pre = wide[span, :]
            tangent = jnp.tanh(TANH_SCALE * (pre + CUBIC_COEF * pre * pre * pre))
            hidden[span, :] = (0.5 * pre * (1.0 + tangent)).astype(jnp.bfloat16)
        outs[c][...] = matmul(hidden[...], w_out_ref[...], ((1,), (0,))).astype(jnp.bfloat16)


def backward_chunks(place, grads, pre_blocks, w_in, w_out, sizes, shifts):
    experts, groups, cap_rows, hidden = pre_blocks.shape
    features = w_in.shape[0]
    rows = experts * cap_rows
    chunks = len(sizes)

    def whole(shape):
        return pl.BlockSpec(shape, lambda i, p: (0,) * len(shape))

    def shared(shift):
        return pl.BlockSpec(
            (experts, 1, cap_rows, hidden),
            lambda i, p: (0, lax.rem(p[0] + shift, groups), 0, 0),
        )

    out_shapes = (
        [jax.ShapeDtypeStruct((rows, hidden), jnp.bfloat16)] * (2 * chunks)
        + [jax.ShapeDtypeStruct((rows, features), jnp.bfloat16)] * chunks
    )
    outs = call(
        functools.partial(backward_kernel, sizes),
        out_shapes,
        [place, w_in, w_out, *grads] + [pre_blocks] * chunks,
        4 * chunks * rows * hidden * features,
        grid_spec=pltpu.PrefetchScalarGridSpec(
            num_scalar_prefetch=1,
            grid=(1,),
            in_specs=[whole(w_in.shape), whole(w_out.shape)]
            + [whole(g.shape) for g in grads]
            + [shared(s) for s in shifts],
            out_specs=[whole(o.shape) for o in out_shapes],
            scratch_shapes=[pltpu.VMEM((rows, hidden), jnp.float32)],
        ),
    )
    return outs[:chunks], outs[chunks : 2 * chunks], outs[2 * chunks :]


def forward_chunks(rows_list, w_in, w_out, sizes):
    features, hidden = w_in.shape
    rows = sum(sizes[0])
    return call(
        functools.partial(forward_kernel, sizes),
        [jax.ShapeDtypeStruct((rows, features), jnp.bfloat16)] * len(sizes),
        [w_in, w_out, *rows_list],
        4 * len(sizes) * rows * hidden * features,
        scratch_shapes=[
            pltpu.VMEM((rows, hidden), jnp.float32),
            pltpu.VMEM((rows, hidden), jnp.bfloat16),
        ],
    )


def weight_grad_kernel(lefts, rights, *refs):
    out_ref = refs[-1]

    def cut(pieces, sizes):
        spans, at = [], 0
        for ref, size in zip(pieces, sizes):
            spans.append((at, at + size, ref))
            at += size
        return spans

    left_spans = cut(refs[: len(lefts)], lefts)
    right_spans = cut(refs[len(lefts) : -1], rights)
    total = None
    for start, end, left in left_spans:
        for first, last, right in right_spans:
            low, high = max(start, first), min(end, last)
            if low >= high:
                continue
            part = matmul(
                left[low - start : high - start, :],
                right[low - first : high - first, :],
                ((0,), (0,)),
            )
            total = part if total is None else total + part
    out_ref[...] = total.astype(jnp.bfloat16)


def weight_grad(lefts, rights, tile):
    left_cols, right_cols = lefts[0].shape[1], rights[0].shape[1]
    rows = sum(a.shape[0] for a in lefts)
    return call(
        functools.partial(
            weight_grad_kernel, [a.shape[0] for a in lefts], [a.shape[0] for a in rights]
        ),
        [jax.ShapeDtypeStruct((left_cols, right_cols), jnp.bfloat16)],
        [*lefts, *rights],
        2 * rows * left_cols * right_cols,
        in_specs=[pl.BlockSpec((a.shape[0], tile), lambda i: (0, i)) for a in lefts]
        + [pl.BlockSpec(a.shape, lambda i: (0, 0)) for a in rights],
        out_specs=[pl.BlockSpec((tile, right_cols), lambda i: (i, 0))],
        grid=(left_cols // tile,),
    )[0]


def add_kernel(into_ref, more_ref, out_ref):
    out_ref[...] = (
        into_ref[...].astype(jnp.float32) + more_ref[...].astype(jnp.float32)
    ).astype(jnp.bfloat16)


def add_half(into, more, which):
    half, features = more.shape
    place = pl.BlockSpec((half, features), lambda i: (which, 0))
    return call(
        add_kernel,
        [jax.ShapeDtypeStruct(into.shape, into.dtype)],
        [into, more],
        more.size,
        in_specs=[place, pl.BlockSpec((half, features), lambda i: (0, 0))],
        out_specs=[place],
        grid=(1,),
        input_output_aliases={0: 0},
    )[0]


def sum_kernel(one_ref, two_ref, three_ref, out_ref):
    out_ref[...] = (
        one_ref[...].astype(jnp.float32)
        + two_ref[...].astype(jnp.float32)
        + three_ref[...].astype(jnp.float32)
    ).astype(jnp.bfloat16)


def sum_three(one, two, three):
    return call(
        sum_kernel, [jax.ShapeDtypeStruct(one.shape, one.dtype)], [one, two, three], 2 * one.size
    )[0]


def forward_out_kernel(cap_rows, arrival_ref, gate_ref, route_ref, returned_ref, out_ref):
    total = None
    for k, t in enumerate(forward_targets(route_ref[...], cap_rows)):
        part = gate_ref[:, k : k + 1] * matmul(
            hits_of(t, returned_ref.shape[0]), returned_ref[...], ((1,), (0,))
        )
        total = part if total is None else total + part
    out_ref[...] = (arrival_ref[...].astype(jnp.float32) + total).astype(jnp.bfloat16)


def backward_out_kernel(
    cap_rows, saved_ref, gain_ref, cot_ref, route_ref, slot_ref, returned_ref, out_ref
):
    pick = sum(
        hits_of(t, returned_ref.shape[0]).astype(jnp.float32)
        for t in backward_targets(route_ref[...], slot_ref[...], cap_rows)
    ).astype(jnp.bfloat16)
    scaled = gain_ref[...] * matmul(pick, returned_ref[...], ((1,), (0,)))
    plain = saved_ref[...].astype(jnp.float32)
    recip = rms_scale(plain)
    cubed = recip * recip * recip
    out_ref[...] = (
        cot_ref[...].astype(jnp.float32)
        + recip * scaled
        - plain * cubed * jnp.mean(scaled * plain, axis=-1, keepdims=True)
    ).astype(jnp.bfloat16)


def body(
    fwd_handoff,
    saved_input,
    grad_handoff,
    gain,
    route_fwd,
    gate_fwd,
    route_bwd,
    slot_bwd,
    gate_bwd,
    w_in,
    w_out,
    saved_pre,
):
    groups = lax.axis_size("expert") // EXPERTS
    tok_rows, features = fwd_handoff.shape[1:]
    choices = route_fwd.shape[2]
    cap_rows = tok_rows * choices // EXPERTS
    all_rows = EXPERTS * cap_rows
    half = all_rows // 2
    mine = jnp.asarray(lax.axis_index("expert") % groups, jnp.int32).reshape(1)
    w_in_local = w_in[0]
    w_out_local = w_out[0]
    pre_blocks = saved_pre[0].reshape(EXPERTS, groups, cap_rows, -1)
    rows_shape = [jax.ShapeDtypeStruct((all_rows, features), jnp.bfloat16)]
    token_shape = [jax.ShapeDtypeStruct((tok_rows, features), jnp.bfloat16)]
    pick_flops = 2 * tok_rows * all_rows * features

    def send(values):
        return exchange(values.reshape(EXPERTS, cap_rows, features), groups).reshape(
            all_rows, features
        )

    cotangent = shifted(grad_handoff, "section", -1)
    arrival = shifted(after(fwd_handoff, cotangent), "section", 1)[0]
    cotangent = cotangent[0]

    rows_bwd = call(
        functools.partial(pick_backward_kernel, cap_rows),
        rows_shape,
        [saved_input[0], gain, route_bwd[0], slot_bwd[0]],
        pick_flops,
    )[0]
    grad_rows = call(
        functools.partial(pick_grad_kernel, cap_rows),
        rows_shape,
        [cotangent, gate_bwd[0], route_bwd[0], slot_bwd[0]],
        2 * pick_flops,
    )[0]
    rows_fwd = call(
        functools.partial(pick_forward_kernel, cap_rows),
        rows_shape,
        [arrival, gain, route_fwd[0]],
        pick_flops,
    )[0]

    sent_grads = send(grad_rows)
    sent_fwd = send(after(rows_fwd, sent_grads))
    sent_rows = send(after(rows_bwd, sent_fwd))
    grads = gather_group(sent_grads, groups)
    rows = gather_group(after(sent_fwd, grads[1], grads[2]), groups)
    own_grads = after(grads[0], sent_fwd)

    def backward_of(pieces, sizes, shifts):
        return backward_chunks(
            mine, pieces, pre_blocks, w_in_local, w_out_local, sizes, shifts
        )

    whole = (all_rows,)
    halves = (half, half)
    hidden_a, pre_grad_a, back_a = backward_of(
        [own_grads, grads[1], grads[2]], [whole] * 3, (0, groups - 1, 1)
    )
    hidden_b, pre_grad_b, back_b = backward_of(
        [after(grads[3], *back_a), grads[4]], [halves], (2,)
    )
    back_opposite = back_b[0]
    back_top = turned(back_opposite[:half], groups, 1)
    back_bottom = turned(back_opposite[half:], groups, -1)

    grad_w_out = weight_grad([*hidden_a, *hidden_b], grads, 256)
    fwd_a = forward_chunks(
        [after(rows[0], grad_w_out), rows[1], rows[2]], w_in_local, w_out_local, [whole] * 3
    )
    back_left = turned(add_half(back_a[2], after(back_top, *fwd_a), 0), groups, 1)
    back_right = turned(add_half(back_a[1], back_bottom, 1), groups, -1)
    fwd_b = forward_chunks([after(rows[3], *fwd_a), rows[4]], w_in_local, w_out_local, [halves])
    fwd_opposite = fwd_b[0]
    fwd_top = turned(fwd_opposite[:half], groups, 1)
    fwd_bottom = turned(fwd_opposite[half:], groups, -1)

    back_sum = sum_three(back_a[0], back_left, back_right)
    return_bwd = send(after(back_sum, sent_rows))

    fwd_left = turned(add_half(fwd_a[2], fwd_top, 0), groups, 1)
    fwd_right = turned(add_half(fwd_a[1], fwd_bottom, 1), groups, -1)
    fwd_sum = sum_three(fwd_a[0], fwd_left, fwd_right)
    return_fwd = send(after(fwd_sum, return_bwd))
    row_chunks = gather_group(after(sent_rows, fwd_sum), groups)

    grad_w_in = weight_grad(row_chunks, [*pre_grad_a, *pre_grad_b], 256)

    section_out = call(
        functools.partial(forward_out_kernel, cap_rows),
        token_shape,
        [arrival, gate_fwd[0], route_fwd[0], return_fwd],
        2 * pick_flops,
    )[0]
    input_grad = call(
        functools.partial(backward_out_kernel, cap_rows),
        token_shape,
        [saved_input[0], gain, cotangent, route_bwd[0], slot_bwd[0], return_bwd],
        pick_flops,
    )[0]
    return (section_out[None], input_grad[None], grad_w_in[None], grad_w_out[None])


def solution(mesh):
    placed = (
        P("section", "expert", None),
        P("section", "expert", None),
        P("section", "expert", None),
        P("section", None),
        P("section", "expert", None),
        P("section", "expert", None),
        P("section", "expert", None),
        P("section", "expert", None),
        P("section", "expert", None),
        P("section", None, "expert"),
        P("section", "expert", None),
        P("section", "expert", None),
    )
    return jax.shard_map(
        body,
        mesh=mesh,
        in_specs=placed,
        out_specs=(
            P("section", "expert", None),
            P("section", "expert", None),
            P("section", None, "expert"),
            P("section", "expert", None),
        ),
        check_vma=False,
    )
```

profile of v0, /device:TPU:6, one launch (start us, length us, event | category | flops | bytes accessed | tf_op | source)
XLA Modules:
  0.0 236.5 jit_solution(4862438378830831199)
XLA Ops:
  3.3 3.2 %collective-permute-done = bf16[1,128,1536]{2,1,0:T(8,128)(2,1)S(1)} collective-permute-done((bf16[1,128,1536]{2,1,0:T(8,128)(2,1)}, bf16[1,128,1536]{2,1,0:T(8,128)(2,1)S(1)}, u32[]{:S(2)}, u32[]{:S(2)}) %collective-permute-start) | collective-permute-done | bytes 393248 | tf_op jit(solution)/shard_map/ppermute | solution.py:21
  8.1 8.5 %all-to-all-start = ((bf16[8,32,1536]{2,1,0:T(8,128)(2,1)}), bf16[8,32,1536]{2,1,0:T(8,128)(2,1)}, u32[]{:S(2)}, u32[]{:S(2)}) async-start(bf16[8,32,1536]{2,1,0:T(8,128)(2,1)} %bitcast.9), calls=%async_computation | async-start | bytes 1572864 | tf_op jit(solution)/shard_map/all_to_all | solution.py:35
  19.0 4.8 %collective-permute-done.1 = bf16[1,128,1536]{2,1,0:T(8,128)(2,1)S(1)} collective-permute-done((bf16[1,128,1536]{2,1,0:T(8,128)(2,1)S(1)}, bf16[1,128,1536]{2,1,0:T(8,128)(2,1)S(1)}, u32[]{:S(2)}, u32[]{:S(2)}) %collective-permute-start.1) | collective-permute-done | bytes 393248 | tf_op jit(solution)/shard_map/ppermute | solution.py:21
  25.5 15.6 %all-to-all-done = bf16[8,32,1536]{2,1,0:T(8,128)(2,1)} async-done(((bf16[8,32,1536]{2,1,0:T(8,128)(2,1)}), bf16[8,32,1536]{2,1,0:T(8,128)(2,1)}, u32[]{:S(2)}, u32[]{:S(2)}) %all-to-all-start) | async-done | bytes 786464 | tf_op jit(solution)/shard_map/all_to_all | solution.py:35
  41.1 4.2 %all-to-all-start.1 = ((bf16[8,32,1536]{2,1,0:T(8,128)(2,1)}), bf16[8,32,1536]{2,1,0:T(8,128)(2,1)}, u32[]{:S(2)}, u32[]{:S(2)}) async-start(bf16[8,32,1536]{2,1,0:T(8,128)(2,1)} %bitcast.11), calls=%async_computation.1 | async-start | bytes 1572864 | tf_op jit(solution)/shard_map/all_to_all | solution.py:35
  48.7 17.8 %collective-permute-done.2.refs_1_.refs_5_ = bf16[256,1536]{1,0:T(8,128)(2,1)S(1)} collective-permute-done((bf16[256,1536]{1,0:T(8,128)(2,1)}, bf16[256,1536]{1,0:T(8,128)(2,1)S(1)}, u32[]{:S(2)}, u32[]{:S(2)}) %collective-permute-start.2) | collective-permute-done | bytes 786464 | tf_op jit(solution)/shard_map/ppermute | solution.py:30
  73.0 3.2 %collective-permute-start.7 = (bf16[256,1536]{1,0:T(8,128)(2,1)}, bf16[256,1536]{1,0:T(8,128)(2,1)}, u32[]{:S(2)}, u32[]{:S(2)}) collective-permute-start(bf16[256,1536]{1,0:T(8,128)(2,1)} %bitcast.12.refs_0_), channel_id=1, source_target_pairs={{0,3},{1,0},{2,1},{3,2},{4,7},{5,4},{6,5},{7,6},{8,11},{9,8},{10,9... | collective-permute-start | bytes 2359304 | tf_op jit(solution)/shard_map/ppermute | solution.py:30
  81.6 6.0 %shard_map.149 = (bf16[256,768]{1,0:T(8,128)(2,1)S(1)}, bf16[256,768]{1,0:T(8,128)(2,1)S(1)}, bf16[256,768]{1,0:T(8,128)(2,1)S(1)}, bf16[256,768]{1,0:T(8,128)(2...) custom-call(s32[1]{0:T(128)} %bitcast.13.place_ref, ...), custom_call_target="tpu_custom_call" | custom-call | flops 3623878656 | bytes 16515076 | tf_op jit(solution)/shard_map/pallas_call | solution.py:78
  94.9 3.4 %shard_map.150 = (bf16[256,768]{1,0:T(8,128)(2,1)S(1)}, bf16[256,768]{1,0:T(8,128)(2,1)S(1)}, bf16[256,1536]{1,0:T(8,128)(2,1)S(1)}) custom-call(s32[1]{0:T(128)} %bitcast.13.place_ref, bf16[1536,768]{1,0:T(8,128)(2,1)S(1)} %bitcast.27, bf16[768,1536]{1,0:T(8,128)(2,1)S(1)} %bitcast.31, bf16[128,1536]{1,0:T(8,128)(2,1)S(1)} %copy-done.29, ...), custom_call_target="tpu_custom_call" | custom-call | flops 1207959552 | bytes 8650756 | tf_op jit(solution)/shard_map/pallas_call | solution.py:78
  100.9 6.7 %all-to-all-start.2 = ((bf16[8,32,1536]{2,1,0:T(8,128)(2,1)}), bf16[8,32,1536]{2,1,0:T(8,128)(2,1)}, u32[]{:S(2)}, u32[]{:S(2)}) async-start(bf16[8,32,1536]{2,1,0:T(8,128)(2,1)} %bitcast.16), calls=%async_computation.2 | async-start | bytes 1572864 | tf_op jit(solution)/shard_map/all_to_all | solution.py:35
  115.9 6.0 %shard_map.151 = bf16[768,1536]{1,0:T(8,128)(2,1)} custom-call(bf16[256,768]{1,0:T(8,128)(2,1)S(1)} %copy-done.48, bf16[256,768]{1,0:T(8,128)(2,1)S(1)} %copy-done.50, bf16[256,768]{1,0:T(8,128)(2,1)S(1)} %copy-done.52, bf16[256,768]{1,0:T(8,128)(2,1)S(1)} %copy-done.40, bf16[256,1536]{1,0:T(8,128)(2,1)} %bitcast.10.refs_0_.refs_4_, ...), custom_call_target="tpu_custom_call" | custom-call | flops 2415919104 | bytes 7077888 | tf_op jit(solution)/shard_map/pallas_call | solution.py:78
  124.8 5.8 %shard_map.152 = (bf16[256,1536]{1,0:T(8,128)(2,1)S(1)}, bf16[256,1536]{1,0:T(8,128)(2,1)S(1)}, bf16[256,1536]{1,0:T(8,128)(2,1)S(1)}) custom-call(bf16[1536,768]{1,0:T(8,128)(2,1)S(1)} %bitcast.28, bf16[768,1536]{1,0:T(8,128)(2,1)S(1)} %bitcast.32, bf16[256,1536]{1,0:T(8,128)(2,1)} %bitcast.12.refs_0_, bf16[256,1536]{1,0:T(8,128)(2,1)} %collective-permute-done.6.refs_1_, ...), custom_call_target="tpu_custom_call" | custom-call | flops 3623878656 | bytes 9437184 | tf_op jit(solution)/shard_map/pallas_call | solution.py:78
  134.3 3.0 %collective-permute-start.9 = (bf16[128,1536]{1,0:T(8,128)(2,1)S(1)}, bf16[128,1536]{1,0:T(8,128)(2,1)S(1)}, u32[]{:S(2)}, u32[]{:S(2)}) collective-permute-start(bf16[128,1536]{1,0:T(8,128)(2,1)S(1)} %slice.43), channel_id=1, source_target_pairs={{0,3},{1,0},{2,1},{3,2},{4,7},{5,4},{6,5},{7,6},{8,11},{9,8},{10,9... | collective-permute-start | bytes 1179656 | tf_op jit(solution)/shard_map/ppermute | solution.py:30
  137.3 19.9 %collective-permute-done.8.refs_0_ = bf16[128,1536]{1,0:T(8,128)(2,1)S(1)} collective-permute-done((bf16[128,1536]{1,0:T(8,128)(2,1)S(1)}, bf16[128,1536]{1,0:T(8,128)(2,1)S(1)}, u32[]{:S(2)}, u32[]{:S(2)}) %collective-permute-start.8) | collective-permute-done | bytes 393248 | tf_op jit(solution)/shard_map/ppermute | solution.py:30
  159.9 7.1 %all-to-all-start.3 = ((bf16[8,32,1536]{2,1,0:T(8,128)(2,1)}), bf16[8,32,1536]{2,1,0:T(8,128)(2,1)S(1)}, u32[]{:S(2)}, u32[]{:S(2)}) async-start(bf16[8,32,1536]{2,1,0:T(8,128)(2,1)} %bitcast.18), calls=%async_computation.3 | async-start | bytes 1572864 | tf_op jit(solution)/shard_map/all_to_all | solution.py:35
  167.1 3.2 %collective-permute-start.12 = (bf16[128,1536]{1,0:T(8,128)(2,1)S(1)}, bf16[128,1536]{1,0:T(8,128)(2,1)S(1)}, u32[]{:S(2)}, u32[]{:S(2)}) collective-permute-start(bf16[128,1536]{1,0:T(8,128)(2,1)S(1)} %get-tuple-element.60), channel_id=1, source_target_pairs={{0,3},{1,0},{2,1},{3,2},{4,7},{5,4},{6,5},{7,6},{8,11},{9,8},{10,9... | collective-permute-start | bytes 1179656 | tf_op jit(solution)/shard_map/ppermute | solution.py:30
  170.4 5.9 %collective-permute-done.10.more_ref = bf16[128,1536]{1,0:T(8,128)(2,1)S(1)} collective-permute-done((bf16[128,1536]{1,0:T(8,128)(2,1)S(1)}, bf16[128,1536]{1,0:T(8,128)(2,1)S(1)}, u32[]{:S(2)}, u32[]{:S(2)}) %collective-permute-start.10) | collective-permute-done | bytes 393248 | tf_op jit(solution)/shard_map/ppermute | solution.py:30
  178.1 3.3 %collective-permute-start.13 = (bf16[256,1536]{1,0:T(8,128)(2,1)S(1)}, bf16[256,1536]{1,0:T(8,128)(2,1)S(1)}, u32[]{:S(2)}, u32[]{:S(2)}) collective-permute-start(bf16[256,1536]{1,0:T(8,128)(2,1)S(1)} %shard_map.155), channel_id=1, source_target_pairs={{0,3},{1,0},{2,1},{3,2},{4,7},{5,4},{6,5},{7,6},{8,11},{9,8},{10,9... | collective-permute-start | bytes 2359304 | tf_op jit(solution)/shard_map/ppermute | solution.py:30
  181.4 12.3 %collective-permute-done.11.two_ref = bf16[256,1536]{1,0:T(8,128)(2,1)S(1)} collective-permute-done((bf16[256,1536]{1,0:T(8,128)(2,1)S(1)}, bf16[256,1536]{1,0:T(8,128)(2,1)S(1)}, u32[]{:S(2)}, u32[]{:S(2)}) %collective-permute-start.11) | collective-permute-done | bytes 786464 | tf_op jit(solution)/shard_map/ppermute | solution.py:30
  195.3 3.6 %collective-permute-start.19 = (bf16[256,1536]{1,0:T(8,128)(2,1)}, bf16[256,1536]{1,0:T(8,128)(2,1)}, u32[]{:S(2)}, u32[]{:S(2)}) collective-permute-start(bf16[256,1536]{1,0:T(8,128)(2,1)} %bitcast.17.refs_0_), channel_id=1, source_target_pairs={{0,3},{1,0},{2,1},{3,2},{4,7},{5,4},{6,5},{7,6},{8,11},{9,8},{10,9... | collective-permute-start | bytes 2359304 | tf_op jit(solution)/shard_map/ppermute | solution.py:30
  198.9 7.2 %all-to-all-start.4 = ((bf16[8,32,1536]{2,1,0:T(8,128)(2,1)}), bf16[8,32,1536]{2,1,0:T(8,128)(2,1)S(1)}, u32[]{:S(2)}, u32[]{:S(2)}) async-start(bf16[8,32,1536]{2,1,0:T(8,128)(2,1)} %bitcast.20), calls=%async_computation.4 | async-start | bytes 1572864 | tf_op jit(solution)/shard_map/all_to_all | solution.py:35
  206.1 6.4 %collective-permute-done.18.refs_1_ = bf16[256,1536]{1,0:T(8,128)(2,1)S(1)} collective-permute-done((bf16[256,1536]{1,0:T(8,128)(2,1)}, bf16[256,1536]{1,0:T(8,128)(2,1)S(1)}, u32[]{:S(2)}, u32[]{:S(2)}) %collective-permute-start.18) | collective-permute-done | bytes 786464 | tf_op jit(solution)/shard_map/ppermute | solution.py:30
  215.1 3.2 %collective-permute-start.21 = (bf16[128,1536]{1,0:T(8,128)(2,1)}, bf16[128,1536]{1,0:T(8,128)(2,1)}, u32[]{:S(2)}, u32[]{:S(2)}) collective-permute-start(bf16[128,1536]{1,0:T(8,128)(2,1)} %slice.47), channel_id=1, source_target_pairs={{0,3},{1,0},{2,1},{3,2},{4,7},{5,4},{6,5},{7,6},{8,11},{9,8},{10,9... | collective-permute-start | bytes 1179656 | tf_op jit(solution)/shard_map/ppermute | solution.py:30
  227.9 7.1 %shard_map.163 = bf16[1536,768]{1,0:T(8,128)(2,1)} custom-call(bf16[256,1536]{1,0:T(8,128)(2,1)} %bitcast.17.refs_0_, bf16[256,1536]{1,0:T(8,128)(2,1)S(1)} %collective-permute-done.18.refs_1_, bf16[256,1536]{1,0:T(8,128)(2,1)} %collective-permute-done.19.refs_2_, bf16[128,1536]{1,0:T(8,128)(2,1)} %collective-permute-done.20.refs_3_, ...), custom_call_target="tpu_custom_call" | custom-call | flops 2415919104 | bytes 7077888 | tf_op jit(solution)/shard_map/pallas_call | solution.py:78
  (172 shorter events, 67.9 us)
Async XLA Ops:
  8.1 33.0 %all-to-all-start = ((bf16[8,32,1536]{2,1,0:T(8,128)(2,1)}), bf16[8,32,1536]{2,1,0:T(8,128)(2,1)}, u32[]{:S(2)}, u32[]{:S(2)}) async-start(bf16[8,32,1536]{2,1,0:T(8,128)(2,1)} %bitcast.9), calls=%async_computation | async-start | bytes 1572864 | tf_op jit(solution)/shard_map/all_to_all | solution.py:35
  41.1 31.9 %all-to-all-start.1 = ((bf16[8,32,1536]{2,1,0:T(8,128)(2,1)}), bf16[8,32,1536]{2,1,0:T(8,128)(2,1)}, u32[]{:S(2)}, u32[]{:S(2)}) async-start(bf16[8,32,1536]{2,1,0:T(8,128)(2,1)} %bitcast.11), calls=%async_computation.1 | async-start | bytes 1572864 | tf_op jit(solution)/shard_map/all_to_all | solution.py:35
  45.3 21.1 %collective-permute-start.2 = (bf16[256,1536]{1,0:T(8,128)(2,1)}, bf16[256,1536]{1,0:T(8,128)(2,1)S(1)}, u32[]{:S(2)}, u32[]{:S(2)}) collective-permute-start(bf16[256,1536]{1,0:T(8,128)(2,1)} %bitcast.10.refs_0_.refs_4_), channel_id=1, source_target_pairs={{0,1},{1,2},{2,3},{3,0},{4,5},{5,6},{6,7},{7,4},{8,9},{9,10},{10,1... | collective-permute-start | bytes 2359304 | tf_op jit(solution)/shard_map/ppermute | solution.py:30
  47.0 21.5 %collective-permute-start.3 = (bf16[256,1536]{1,0:T(8,128)(2,1)}, bf16[256,1536]{1,0:T(8,128)(2,1)S(1)}, u32[]{:S(2)}, u32[]{:S(2)}) collective-permute-start(bf16[256,1536]{1,0:T(8,128)(2,1)} %bitcast.10.refs_0_.refs_4_), channel_id=1, source_target_pairs={{0,3},{1,0},{2,1},{3,2},{4,7},{5,4},{6,5},{7,6},{8,11},{9,8},{10,9... | collective-permute-start | bytes 2359304 | tf_op jit(solution)/shard_map/ppermute | solution.py:30
  68.1 25.0 %collective-permute-start.4 = (bf16[128,1536]{1,0:T(8,128)(2,1)}, bf16[128,1536]{1,0:T(8,128)(2,1)S(1)}, u32[]{:S(2)}, u32[]{:S(2)}) collective-permute-start(bf16[128,1536]{1,0:T(8,128)(2,1)} %slice.40), channel_id=1, source_target_pairs={{0,1},{1,2},{2,3},{3,0},{4,5},{5,6},{6,7},{7,4},{8,9},{9,10},{10,1... | collective-permute-start | bytes 1179656 | tf_op jit(solution)/shard_map/ppermute | solution.py:30
  70.1 23.8 %collective-permute-start.5 = (bf16[128,1536]{1,0:T(8,128)(2,1)}, bf16[128,1536]{1,0:T(8,128)(2,1)}, u32[]{:S(2)}, u32[]{:S(2)}) collective-permute-start(bf16[128,1536]{1,0:T(8,128)(2,1)} %slice.41), channel_id=1, source_target_pairs={{0,3},{1,0},{2,1},{3,2},{4,7},{5,4},{6,5},{7,6},{8,11},{9,8},{10,9... | collective-permute-start | bytes 1179656 | tf_op jit(solution)/shard_map/ppermute | solution.py:30
  73.0 51.8 %collective-permute-start.6 = (bf16[256,1536]{1,0:T(8,128)(2,1)}, bf16[256,1536]{1,0:T(8,128)(2,1)}, u32[]{:S(2)}, u32[]{:S(2)}) collective-permute-start(bf16[256,1536]{1,0:T(8,128)(2,1)} %bitcast.12.refs_0_), channel_id=1, source_target_pairs={{0,1},{1,2},{2,3},{3,0},{4,5},{5,6},{6,7},{7,4},{8,9},{9,10},{10,1... | collective-permute-start | bytes 2359304 | tf_op jit(solution)/shard_map/ppermute | solution.py:30
  73.0 51.8 %collective-permute-start.7 = (bf16[256,1536]{1,0:T(8,128)(2,1)}, bf16[256,1536]{1,0:T(8,128)(2,1)}, u32[]{:S(2)}, u32[]{:S(2)}) collective-permute-start(bf16[256,1536]{1,0:T(8,128)(2,1)} %bitcast.12.refs_0_), channel_id=1, source_target_pairs={{0,3},{1,0},{2,1},{3,2},{4,7},{5,4},{6,5},{7,6},{8,11},{9,8},{10,9... | collective-permute-start | bytes 2359304 | tf_op jit(solution)/shard_map/ppermute | solution.py:30
  99.4 22.5 %collective-permute-start.16 = (bf16[128,1536]{1,0:T(8,128)(2,1)}, bf16[128,1536]{1,0:T(8,128)(2,1)}, u32[]{:S(2)}, u32[]{:S(2)}) collective-permute-start(bf16[128,1536]{1,0:T(8,128)(2,1)} %get-tuple-element.58), channel_id=1, source_target_pairs={{0,3},{1,0},{2,1},{3,2},{4,7},{5,4},{6,5},{7,6},{8,11},{9,8},{10,9... | collective-permute-start | bytes 1179656 | tf_op jit(solution)/shard_map/ppermute | solution.py:30
  100.9 59.0 %all-to-all-start.2 = ((bf16[8,32,1536]{2,1,0:T(8,128)(2,1)}), bf16[8,32,1536]{2,1,0:T(8,128)(2,1)}, u32[]{:S(2)}, u32[]{:S(2)}) async-start(bf16[8,32,1536]{2,1,0:T(8,128)(2,1)} %bitcast.16), calls=%async_computation.2 | async-start | bytes 1572864 | tf_op jit(solution)/shard_map/all_to_all | solution.py:35
  107.7 23.0 %collective-permute-start.14 = (bf16[128,1536]{1,0:T(8,128)(2,1)}, bf16[128,1536]{1,0:T(8,128)(2,1)S(1)}, u32[]{:S(2)}, u32[]{:S(2)}) collective-permute-start(bf16[128,1536]{1,0:T(8,128)(2,1)} %get-tuple-element.59), channel_id=1, source_target_pairs={{0,1},{1,2},{2,3},{3,0},{4,5},{5,6},{6,7},{7,4},{8,9},{9,10},{10,1... | collective-permute-start | bytes 1179656 | tf_op jit(solution)/shard_map/ppermute | solution.py:30
  123.3 35.5 %collective-permute-start.17 = (bf16[256,1536]{1,0:T(8,128)(2,1)S(1)}, bf16[256,1536]{1,0:T(8,128)(2,1)S(1)}, u32[]{:S(2)}, u32[]{:S(2)}) collective-permute-start(bf16[256,1536]{1,0:T(8,128)(2,1)S(1)} %shard_map.158), channel_id=1, source_target_pairs={{0,3},{1,0},{2,1},{3,2},{4,7},{5,4},{6,5},{7,6},{8,11},{9,8},{10,9... | collective-permute-start | bytes 2359304 | tf_op jit(solution)/shard_map/ppermute | solution.py:30
  131.0 27.7 %collective-permute-start.15 = (bf16[256,1536]{1,0:T(8,128)(2,1)S(1)}, bf16[256,1536]{1,0:T(8,128)(2,1)S(1)}, u32[]{:S(2)}, u32[]{:S(2)}) collective-permute-start(bf16[256,1536]{1,0:T(8,128)(2,1)S(1)} %shard_map.157), channel_id=1, source_target_pairs={{0,1},{1,2},{2,3},{3,0},{4,5},{5,6},{6,7},{7,4},{8,9},{9,10},{10,1... | collective-permute-start | bytes 2359304 | tf_op jit(solution)/shard_map/ppermute | solution.py:30
  132.9 24.3 %collective-permute-start.8 = (bf16[128,1536]{1,0:T(8,128)(2,1)S(1)}, bf16[128,1536]{1,0:T(8,128)(2,1)S(1)}, u32[]{:S(2)}, u32[]{:S(2)}) collective-permute-start(bf16[128,1536]{1,0:T(8,128)(2,1)S(1)} %slice.42), channel_id=1, source_target_pairs={{0,1},{1,2},{2,3},{3,0},{4,5},{5,6},{6,7},{7,4},{8,9},{9,10},{10,1... | collective-permute-start | bytes 1179656 | tf_op jit(solution)/shard_map/ppermute | solution.py:30
  134.3 22.9 %collective-permute-start.9 = (bf16[128,1536]{1,0:T(8,128)(2,1)S(1)}, bf16[128,1536]{1,0:T(8,128)(2,1)S(1)}, u32[]{:S(2)}, u32[]{:S(2)}) collective-permute-start(bf16[128,1536]{1,0:T(8,128)(2,1)S(1)} %slice.43), channel_id=1, source_target_pairs={{0,3},{1,0},{2,1},{3,2},{4,7},{5,4},{6,5},{7,6},{8,11},{9,8},{10,9... | collective-permute-start | bytes 1179656 | tf_op jit(solution)/shard_map/ppermute | solution.py:30
  159.9 39.0 %all-to-all-start.3 = ((bf16[8,32,1536]{2,1,0:T(8,128)(2,1)}), bf16[8,32,1536]{2,1,0:T(8,128)(2,1)S(1)}, u32[]{:S(2)}, u32[]{:S(2)}) async-start(bf16[8,32,1536]{2,1,0:T(8,128)(2,1)} %bitcast.18), calls=%async_computation.3 | async-start | bytes 1572864 | tf_op jit(solution)/shard_map/all_to_all | solution.py:35
  167.0 9.2 %collective-permute-start.10 = (bf16[128,1536]{1,0:T(8,128)(2,1)S(1)}, bf16[128,1536]{1,0:T(8,128)(2,1)S(1)}, u32[]{:S(2)}, u32[]{:S(2)}) collective-permute-start(bf16[128,1536]{1,0:T(8,128)(2,1)S(1)} %get-tuple-element.61), channel_id=1, source_target_pairs={{0,1},{1,2},{2,3},{3,0},{4,5},{5,6},{6,7},{7,4},{8,9},{9,10},{10,1... | collective-permute-start | bytes 1179656 | tf_op jit(solution)/shard_map/ppermute | solution.py:30
  167.1 10.7 %collective-permute-start.12 = (bf16[128,1536]{1,0:T(8,128)(2,1)S(1)}, bf16[128,1536]{1,0:T(8,128)(2,1)S(1)}, u32[]{:S(2)}, u32[]{:S(2)}) collective-permute-start(bf16[128,1536]{1,0:T(8,128)(2,1)S(1)} %get-tuple-element.60), channel_id=1, source_target_pairs={{0,3},{1,0},{2,1},{3,2},{4,7},{5,4},{6,5},{7,6},{8,11},{9,8},{10,9... | collective-permute-start | bytes 1179656 | tf_op jit(solution)/shard_map/ppermute | solution.py:30
  177.7 16.1 %collective-permute-start.11 = (bf16[256,1536]{1,0:T(8,128)(2,1)S(1)}, bf16[256,1536]{1,0:T(8,128)(2,1)S(1)}, u32[]{:S(2)}, u32[]{:S(2)}) collective-permute-start(bf16[256,1536]{1,0:T(8,128)(2,1)S(1)} %shard_map.154), channel_id=1, source_target_pairs={{0,1},{1,2},{2,3},{3,0},{4,5},{5,6},{6,7},{7,4},{8,9},{9,10},{10,1... | collective-permute-start | bytes 2359304 | tf_op jit(solution)/shard_map/ppermute | solution.py:30
  178.1 15.6 %collective-permute-start.13 = (bf16[256,1536]{1,0:T(8,128)(2,1)S(1)}, bf16[256,1536]{1,0:T(8,128)(2,1)S(1)}, u32[]{:S(2)}, u32[]{:S(2)}) collective-permute-start(bf16[256,1536]{1,0:T(8,128)(2,1)S(1)} %shard_map.155), channel_id=1, source_target_pairs={{0,3},{1,0},{2,1},{3,2},{4,7},{5,4},{6,5},{7,6},{8,11},{9,8},{10,9... | collective-permute-start | bytes 2359304 | tf_op jit(solution)/shard_map/ppermute | solution.py:30
  195.0 17.6 %collective-permute-start.18 = (bf16[256,1536]{1,0:T(8,128)(2,1)}, bf16[256,1536]{1,0:T(8,128)(2,1)S(1)}, u32[]{:S(2)}, u32[]{:S(2)}) collective-permute-start(bf16[256,1536]{1,0:T(8,128)(2,1)} %bitcast.17.refs_0_), channel_id=1, source_target_pairs={{0,1},{1,2},{2,3},{3,0},{4,5},{5,6},{6,7},{7,4},{8,9},{9,10},{10,1... | collective-permute-start | bytes 2359304 | tf_op jit(solution)/shard_map/ppermute | solution.py:30
  195.3 18.0 %collective-permute-start.19 = (bf16[256,1536]{1,0:T(8,128)(2,1)}, bf16[256,1536]{1,0:T(8,128)(2,1)}, u32[]{:S(2)}, u32[]{:S(2)}) collective-permute-start(bf16[256,1536]{1,0:T(8,128)(2,1)} %bitcast.17.refs_0_), channel_id=1, source_target_pairs={{0,3},{1,0},{2,1},{3,2},{4,7},{5,4},{6,5},{7,6},{8,11},{9,8},{10,9... | collective-permute-start | bytes 2359304 | tf_op jit(solution)/shard_map/ppermute | solution.py:30
  198.9 36.1 %all-to-all-start.4 = ((bf16[8,32,1536]{2,1,0:T(8,128)(2,1)}), bf16[8,32,1536]{2,1,0:T(8,128)(2,1)S(1)}, u32[]{:S(2)}, u32[]{:S(2)}) async-start(bf16[8,32,1536]{2,1,0:T(8,128)(2,1)} %bitcast.20), calls=%async_computation.4 | async-start | bytes 1572864 | tf_op jit(solution)/shard_map/all_to_all | solution.py:35
  213.3 9.3 %collective-permute-start.20 = (bf16[128,1536]{1,0:T(8,128)(2,1)}, bf16[128,1536]{1,0:T(8,128)(2,1)}, u32[]{:S(2)}, u32[]{:S(2)}) collective-permute-start(bf16[128,1536]{1,0:T(8,128)(2,1)} %slice.46), channel_id=1, source_target_pairs={{0,1},{1,2},{2,3},{3,0},{4,5},{5,6},{6,7},{7,4},{8,9},{9,10},{10,1... | collective-permute-start | bytes 1179656 | tf_op jit(solution)/shard_map/ppermute | solution.py:30
  (59 other events, 808.7 us)
where the time goes:
time: 239 us; the launch traced here: 237 us
  waiting for transfers between devices  90.3 us (38%)
  starting transfers between devices  67.7 us (28%)
  Pallas kernels  41.9 us (18%)
  local copies, waits for them, and re-layouts  35.6 us (15%)
    ppermute x20, waiting for transfers between devices, turned(): return lax.ppermute(block, 'expert', route)  66.7 us
    pallas_call x17, Pallas kernels, call(): pl.pallas_call(kernel, out_shape=out_shapes, cost_estimate=pl.CostEstimat...  41.9 us
    all_to_all x5, starting transfers between devices, exchange(): lax.all_to_all(block, 'expert', split_axis=0, concat_axis=0, tiled=True,...  33.7 us
    ppermute x20, starting transfers between devices, turned(): return lax.ppermute(block, 'expert', route)  31.4 us
    unnamed x117, local copies, waits for them, and re-layouts  28.4 us
    all_to_all x5, waiting for transfers between devices, exchange(): lax.all_to_all(block, 'expert', split_axis=0, concat_axis=0, tiled=True,...  15.6 us
    ppermute x2, waiting for transfers between devices, shifted(): return lax.ppermute(block, axis, route)  8.01 us
  transfers between devices with their start and end apart: 27, of which 10 were waited for; matrix products, arithmetic and copies ran while one was open for 4% of the time, Pallas kernels for 16%

commit v1 on v0

--- a/solution.py
+++ b/solution.py
@@ -35,15 +35,6 @@
     return lax.all_to_all(
         block, "expert", split_axis=0, concat_axis=0, tiled=True, axis_index_groups=index_groups
     )
-
-
-def gather_group(chunk, groups):
-    half = chunk.shape[0] // 2
-    from_left = turned(chunk, groups, 1)
-    from_right = turned(chunk, groups, -1)
-    opposite_top = turned(from_left[:half], groups, 1)
-    opposite_bottom = turned(from_right[half:], groups, -1)
-    return [chunk, from_left, from_right, opposite_top, opposite_bottom]
 
 
 def after(value, *earlier):
@@ -151,7 +142,7 @@
     out_ref[...] = total.astype(jnp.bfloat16)
 
 
-def backward_kernel(sizes, place_ref, w_in_ref, w_out_ref, *refs):
+def backward_kernel(sizes, split, place_ref, w_in_ref, w_out_ref, *refs):
     chunks = len(sizes)
     pieces = sum(len(s) for s in sizes)
     grads = list(refs[:pieces])
@@ -159,8 +150,8 @@
     outs = refs[pieces + chunks :]
     hidden_refs = outs[:chunks]
     pre_grad_refs = outs[chunks : 2 * chunks]
-    back_refs = outs[2 * chunks : 3 * chunks]
-    wide = outs[3 * chunks]
+    back_refs = outs[2 * chunks : -1]
+    wide = outs[-1]
     for c in range(chunks):
         row = 0
         for size in sizes[c]:
@@ -179,17 +170,20 @@
             )
             hidden_refs[c][span, :] = (pre * half).astype(jnp.bfloat16)
             pre_grad_refs[c][span, :] = (wide[span, :] * derivative).astype(jnp.bfloat16)
-        back_refs[c][...] = matmul(pre_grad_refs[c][...], w_in_ref[...], ((1,), (1,))).astype(
-            jnp.bfloat16
-        )
-
-
-def forward_kernel(sizes, w_in_ref, w_out_ref, *refs):
+        parts = 2 if split else 1
+        for h in range(parts):
+            span = slice(h * row // parts, (h + 1) * row // parts)
+            back_refs[parts * c + h][...] = matmul(
+                pre_grad_refs[c][span, :], w_in_ref[...], ((1,), (1,))
+            ).astype(jnp.bfloat16)
+
+
+def forward_kernel(sizes, split, w_in_ref, w_out_ref, *refs):
     chunks = len(sizes)
     pieces = sum(len(s) for s in sizes)
     rows = list(refs[:pieces])
-    outs = refs[pieces : pieces + chunks]
-    wide, hidden = refs[pieces + chunks :]
+    outs = refs[pieces:-2]
+    wide, hidden = refs[-2:]
     for c in range(chunks):
         row = 0
         for size in sizes[c]:
@@ -200,14 +194,20 @@
             pre = wide[span, :]
             tangent = jnp.tanh(TANH_SCALE * (pre + CUBIC_COEF * pre * pre * pre))
             hidden[span, :] = (0.5 * pre * (1.0 + tangent)).astype(jnp.bfloat16)
-        outs[c][...] = matmul(hidden[...], w_out_ref[...], ((1,), (0,))).astype(jnp.bfloat16)
-
-
-def backward_chunks(place, grads, pre_blocks, w_in, w_out, sizes, shifts):
+        parts = 2 if split else 1
+        for h in range(parts):
+            span = slice(h * row // parts, (h + 1) * row // parts)
+            outs[parts * c + h][...] = matmul(
+                hidden[span, :], w_out_ref[...], ((1,), (0,))
+            ).astype(jnp.bfloat16)
+
+
+def backward_chunks(place, grads, pre_blocks, w_in, w_out, sizes, shifts, split=False):
     experts, groups, cap_rows, hidden = pre_blocks.shape
     features = w_in.shape[0]
     rows = experts * cap_rows
-    chunks = len(sizes)
+    chunks = len(shifts)
+    parts = 2 if split else 1
 
     def whole(shape):
         return pl.BlockSpec(shape, lambda i, p: (0,) * len(shape))
@@ -218,12 +218,11 @@
             lambda i, p: (0, lax.rem(p[0] + shift, groups), 0, 0),
         )
 
-    out_shapes = (
-        [jax.ShapeDtypeStruct((rows, hidden), jnp.bfloat16)] * (2 * chunks)
-        + [jax.ShapeDtypeStruct((rows, features), jnp.bfloat16)] * chunks
-    )
+    out_shapes = [jax.ShapeDtypeStruct((rows, hidden), jnp.bfloat16)] * (2 * chunks) + [
+        jax.ShapeDtypeStruct((rows // parts, features), jnp.bfloat16)
+    ] * (parts * chunks)
     outs = call(
-        functools.partial(backward_kernel, sizes),
+        functools.partial(backward_kernel, sizes, split),
         out_shapes,
         [place, w_in, w_out, *grads] + [pre_blocks] * chunks,
         4 * chunks * rows * hidden * features,
@@ -240,12 +239,13 @@
     return outs[:chunks], outs[chunks : 2 * chunks], outs[2 * chunks :]
 
 
-def forward_chunks(rows_list, w_in, w_out, sizes):
+def forward_chunks(rows_list, w_in, w_out, sizes, split=False):
     features, hidden = w_in.shape
     rows = sum(sizes[0])
+    parts = 2 if split else 1
     return call(
-        functools.partial(forward_kernel, sizes),
-        [jax.ShapeDtypeStruct((rows, features), jnp.bfloat16)] * len(sizes),
+        functools.partial(forward_kernel, sizes, split),
+        [jax.ShapeDtypeStruct((rows // parts, features), jnp.bfloat16)] * (parts * len(sizes)),
         [w_in, w_out, *rows_list],
         4 * len(sizes) * rows * hidden * features,
         scratch_shapes=[
@@ -296,6 +296,67 @@
         + [pl.BlockSpec(a.shape, lambda i: (0, 0)) for a in rights],
         out_specs=[pl.BlockSpec((tile, right_cols), lambda i: (i, 0))],
         grid=(left_cols // tile,),
+    )[0]
+
+
+def exchanged_grad_kernel(rows_ref, *refs):
+    out_ref = refs[-1]
+    blocks, chunks, slots, tile = rows_ref.shape
+    total = None
+    for c in range(chunks):
+        rows = rows_ref[:, c].reshape(blocks * slots, tile)
+        part = matmul(rows, refs[c][...], ((0,), (0,)))
+        total = part if total is None else total + part
+    out_ref[...] = total.astype(jnp.bfloat16)
+
+
+def exchanged_grad(rows, rights, tile):
+    blocks, chunks, slots, features = rows.shape
+    hidden = rights[0].shape[1]
+    return call(
+        exchanged_grad_kernel,
+        [jax.ShapeDtypeStruct((features, hidden), jnp.bfloat16)],
+        [rows, *rights],
+        2 * blocks * chunks * slots * features * hidden,
+        in_specs=[pl.BlockSpec((blocks, chunks, slots, tile), lambda i: (0, 0, 0, i))]
+        + [pl.BlockSpec(a.shape, lambda i: (0, 0)) for a in rights],
+        out_specs=[pl.BlockSpec((tile, hidden), lambda i: (i, 0))],
+        grid=(features // tile,),
+    )[0]
+
+
+def assemble_kernel(own_ref, left_ref, right_ref, top_ref, bottom_ref, out_ref, sems):
+    upper = top_ref.shape[0]
+    copies = [
+        (own_ref, out_ref.at[:, 0]),
+        (left_ref, out_ref.at[:, 1]),
+        (right_ref, out_ref.at[:, 2]),
+        (top_ref, out_ref.at[:upper, 3]),
+        (bottom_ref, out_ref.at[upper:, 3]),
+    ]
+    started = [
+        pltpu.make_async_copy(source, target, sems.at[n])
+        for n, (source, target) in enumerate(copies)
+    ]
+    for copy in started:
+        copy.start()
+    for copy in started:
+        copy.wait()
+
+
+def assemble(pieces, cap_rows):
+    features = pieces[0].shape[1]
+    shaped = [p.reshape(-1, cap_rows, features) for p in pieces]
+    experts = shaped[0].shape[0]
+    anywhere = pl.BlockSpec(memory_space=pl.ANY)
+    return call(
+        assemble_kernel,
+        [jax.ShapeDtypeStruct((experts, 4, cap_rows, features), jnp.bfloat16)],
+        shaped,
+        0,
+        in_specs=[anywhere] * 5,
+        out_specs=[pl.BlockSpec(memory_space=pltpu.HBM)],
+        scratch_shapes=[pltpu.SemaphoreType.DMA((5,))],
     )[0]
 
 
@@ -391,9 +452,10 @@
     pick_flops = 2 * tok_rows * all_rows * features
 
     def send(values):
-        return exchange(values.reshape(EXPERTS, cap_rows, features), groups).reshape(
-            all_rows, features
-        )
+        return exchange(values.reshape(EXPERTS, -1, features), groups).reshape(-1, features)
+
+    def halves_of(chunk):
+        return chunk[:half], chunk[half:]
 
     cotangent = shifted(grad_handoff, "section", -1)
     arrival = shifted(after(fwd_handoff, cotangent), "section", 1)[0]
@@ -405,64 +467,99 @@
         [saved_input[0], gain, route_bwd[0], slot_bwd[0]],
         pick_flops,
     )[0]
+    rows_left, rows_right = turned(rows_bwd, groups, 1), turned(rows_bwd, groups, -1)
+    rows_left_top, rows_right_bottom = rows_left[:half], rows_right[half:]
+    rows_top = turned(rows_left_top, groups, 1)
+    rows_bottom = turned(rows_right_bottom, groups, -1)
+
     grad_rows = call(
         functools.partial(pick_grad_kernel, cap_rows),
         rows_shape,
-        [cotangent, gate_bwd[0], route_bwd[0], slot_bwd[0]],
+        [after(cotangent, rows_bwd), gate_bwd[0], route_bwd[0], slot_bwd[0]],
         2 * pick_flops,
     )[0]
     rows_fwd = call(
         functools.partial(pick_forward_kernel, cap_rows),
         rows_shape,
-        [arrival, gain, route_fwd[0]],
+        [after(arrival, rows_left_top, rows_right_bottom), gain, route_fwd[0]],
         pick_flops,
     )[0]
 
-    sent_grads = send(grad_rows)
-    sent_fwd = send(after(rows_fwd, sent_grads))
-    sent_rows = send(after(rows_bwd, sent_fwd))
-    grads = gather_group(sent_grads, groups)
-    rows = gather_group(after(sent_fwd, grads[1], grads[2]), groups)
-    own_grads = after(grads[0], sent_fwd)
-
-    def backward_of(pieces, sizes, shifts):
-        return backward_chunks(
-            mine, pieces, pre_blocks, w_in_local, w_out_local, sizes, shifts
-        )
-
-    whole = (all_rows,)
-    halves = (half, half)
-    hidden_a, pre_grad_a, back_a = backward_of(
-        [own_grads, grads[1], grads[2]], [whole] * 3, (0, groups - 1, 1)
-    )
-    hidden_b, pre_grad_b, back_b = backward_of(
-        [after(grads[3], *back_a), grads[4]], [halves], (2,)
-    )
-    back_opposite = back_b[0]
-    back_top = turned(back_opposite[:half], groups, 1)
-    back_bottom = turned(back_opposite[half:], groups, -1)
-
-    grad_w_out = weight_grad([*hidden_a, *hidden_b], grads, 256)
-    fwd_a = forward_chunks(
-        [after(rows[0], grad_w_out), rows[1], rows[2]], w_in_local, w_out_local, [whole] * 3
-    )
-    back_left = turned(add_half(back_a[2], after(back_top, *fwd_a), 0), groups, 1)
-    back_right = turned(add_half(back_a[1], back_bottom, 1), groups, -1)
-    fwd_b = forward_chunks([after(rows[3], *fwd_a), rows[4]], w_in_local, w_out_local, [halves])
-    fwd_opposite = fwd_b[0]
-    fwd_top = turned(fwd_opposite[:half], groups, 1)
-    fwd_bottom = turned(fwd_opposite[half:], groups, -1)
-
-    back_sum = sum_three(back_a[0], back_left, back_right)
-    return_bwd = send(after(back_sum, sent_rows))
-
-    fwd_left = turned(add_half(fwd_a[2], fwd_top, 0), groups, 1)
-    fwd_right = turned(add_half(fwd_a[1], fwd_bottom, 1), groups, -1)
-    fwd_sum = sum_three(fwd_a[0], fwd_left, fwd_right)
+    grads = send(grad_rows)
+    grads_left, grads_right = turned(grads, groups, 1), turned(grads, groups, -1)
+    sent_fwd = send(after(rows_fwd, grads))
+    whole, halves = (all_rows,), (half, half)
+    hidden_0, pre_grad_0, back_0 = backward_chunks(
+        mine, [after(grads, rows_top, rows_bottom)], pre_blocks, w_in_local, w_out_local, [whole], (0,)
+    )
+    grads_left_top, grads_right_bottom = grads_left[:half], grads_right[half:]
+    grads_top = turned(grads_left_top, groups, 1)
+    grads_bottom = turned(grads_right_bottom, groups, -1)
+    assembled = assemble(
+        [after(rows_bwd, grads_left_top, grads_right_bottom, *back_0), rows_left, rows_right, rows_top, rows_bottom], cap_rows
+    )
+    ready = after(sent_fwd, grads_left, grads_right)
+    left, right = turned(ready, groups, 1), turned(ready, groups, -1)
+    sent_rows = send(after(assembled, sent_fwd))
+
+    hidden_1, pre_grad_1, back_1 = backward_chunks(
+        mine,
+        [after(grads_left, sent_fwd), grads_right],
+        pre_blocks,
+        w_in_local,
+        w_out_local,
+        [whole] * 2,
+        (groups - 1, 1),
+    )
+    hidden_2, pre_grad_2, back_2 = backward_chunks(
+        mine,
+        [after(grads_top, *back_1), grads_bottom],
+        pre_blocks,
+        w_in_local,
+        w_out_local,
+        [halves],
+        (2,),
+        split=True,
+    )
+    back_top = turned(back_2[0], groups, 1)
+    back_bottom = turned(back_2[1], groups, -1)
+
+    left_top, right_bottom = left[:half], right[half:]
+    opposite_top = turned(left_top, groups, 1)
+    opposite_bottom = turned(right_bottom, groups, -1)
+    grad_w_out = weight_grad(
+        [*hidden_0, *hidden_1, *hidden_2],
+        [after(grads, left_top, right_bottom), grads_left, grads_right, grads_top, grads_bottom],
+        256,
+    )
+    fwd_0 = forward_chunks([after(sent_fwd, left_top, right_bottom)], w_in_local, w_out_local, [whole])
+
+    arrived = (grad_w_out, *fwd_0, opposite_top, opposite_bottom)
+    back_to_left = add_half(back_1[1], after(back_top, *arrived), 0)
+    back_to_right = add_half(back_1[0], after(back_bottom, *arrived), 1)
+    back_left = turned(back_to_left, groups, 1)
+    back_right = turned(back_to_right, groups, -1)
+    fwd_1 = forward_chunks(
+        [after(left, back_to_left, back_to_right), right], w_in_local, w_out_local, [whole] * 2
+    )
+    fwd_2 = forward_chunks(
+        [after(opposite_top, *fwd_1), opposite_bottom], w_in_local, w_out_local, [halves], split=True
+    )
+    fwd_top = turned(fwd_2[0], groups, 1)
+    fwd_bottom = turned(fwd_2[1], groups, -1)
+
+    back_sum = sum_three(after(back_0[0], *fwd_2), back_left, back_right)
+    fwd_to_left = add_half(fwd_1[1], fwd_top, 0)
+    fwd_to_right = add_half(fwd_1[0], fwd_bottom, 1)
+    return_bwd = send(after(back_sum, sent_rows, fwd_to_left, fwd_to_right))
+    grad_w_in = exchanged_grad(
+        sent_rows.reshape(assembled.shape), [*pre_grad_0, *pre_grad_1, *pre_grad_2], 256
+    )
+
+    fwd_left = turned(fwd_to_left, groups, 1)
+    fwd_right = turned(fwd_to_right, groups, -1)
+    fwd_sum = sum_three(fwd_0[0], after(fwd_left, grad_w_in), fwd_right)
     return_fwd = send(after(fwd_sum, return_bwd))
-    row_chunks = gather_group(after(sent_rows, fwd_sum), groups)
-
-    grad_w_in = weight_grad(row_chunks, [*pre_grad_a, *pre_grad_b], 256)
 
     section_out = call(
         functools.partial(forward_out_kernel, cap_rows),

time: 239 us -> 237 us (level)
  waiting for transfers between devices: 90.3 us -> 101 us
  local copies, waits for them, and re-layouts: 35.6 us -> 27.4 us
  starting transfers between devices: 67.7 us -> 63.1 us
    ppermute x20, waiting for transfers between devices: 66.7 us -> 83.2 us  [turned(): return lax.ppermute(block, 'expert', route)]
    unnamed x117 -> x81, local copies, waits for them, and re-layouts: 28.4 us -> 20 us
    ppermute x2, waiting for transfers between devices: 8.01 us -> 0.01 us  [shifted(): return lax.ppermute(block, axis, route)]
    ppermute x20, starting transfers between devices: 31.4 us -> 26.2 us  [turned(): return lax.ppermute(block, 'expert', route)]
    pallas_call x17 -> x20, Pallas kernels: 41.9 us -> 43 us  [call(): pl.pallas_call(kernel, out_shape=out_shapes, cost_estimate=pl.CostEstimat...]
    slice x8 -> x6, local copies, waits for them, and re-layouts: 7.23 us -> 7.43 us  [the longest x2 3.84 us: body(): grads_left_top, grads_right_bottom = (grads_left[:half], grads_right[half:])]
  transfers between devices with their start and end apart: 27 -> 27, of which waited for: 10 -> 11; matrix products, arithmetic and copies ran while one was open for 4% -> 5% of each run, Pallas kernels for 16% -> 17%
where the time goes in v1:
time: 237 us; the launch traced here: 236 us
  waiting for transfers between devices  101 us (43%)
  starting transfers between devices  63.1 us (27%)
  Pallas kernels  43 us (18%)
  local copies, waits for them, and re-layouts  27.4 us (12%)
    ppermute x20, waiting for transfers between devices, turned(): return lax.ppermute(block, 'expert', route)  83.2 us
    pallas_call x20, Pallas kernels, call(): pl.pallas_call(kernel, out_shape=out_shapes, cost_estimate=pl.CostEstimat...  43 us
    all_to_all x5, starting transfers between devices, exchange(): lax.all_to_all(block, 'expert', split_axis=0, concat_axis=0, tiled=True,...  34.6 us
    ppermute x20, starting transfers between devices, turned(): return lax.ppermute(block, 'expert', route)  26.2 us
    unnamed x81, local copies, waits for them, and re-layouts  20 us
    all_to_all x5, waiting for transfers between devices, exchange(): lax.all_to_all(block, 'expert', split_axis=0, concat_axis=0, tiled=True,...  17.9 us
  transfers between devices with their start and end apart: 27, of which 11 were waited for; matrix products, arithmetic and copies ran while one was open for 5% of the time, Pallas kernels for 17%

profile of v1, /device:TPU:6, one launch (start us, length us, event | category | flops | bytes accessed | tf_op | source)
XLA Modules:
  0.0 235.6 jit_solution(10107747036899107933)
XLA Ops:
  8.1 8.5 %all-to-all-start = ((bf16[8,32,1536]{2,1,0:T(8,128)(2,1)}), bf16[8,32,1536]{2,1,0:T(8,128)(2,1)S(1)}, u32[]{:S(2)}, u32[]{:S(2)}) async-start(bf16[8,32,1536]{2,1,0:T(8,128)(2,1)} %bitcast.10), calls=%async_computation | async-start | bytes 1572864 | tf_op jit(solution)/shard_map/all_to_all | solution.py:35
  16.6 3.1 %collective-permute-start.3 = (bf16[256,1536]{1,0:T(8,128)(2,1)}, bf16[256,1536]{1,0:T(8,128)(2,1)}, u32[]{:S(2)}, u32[]{:S(2)}) collective-permute-start(bf16[256,1536]{1,0:T(8,128)(2,1)} %copy-done.7), channel_id=1, source_target_pairs={{0,3},{1,0},{2,1},{3,2},{4,7},{5,4},{6,5},{7,6},{8,11},{9,8},{10,9... | collective-permute-start | bytes 2359304 | tf_op jit(solution)/shard_map/ppermute | solution.py:30
  22.4 14.1 %collective-permute-done.3 = bf16[256,1536]{1,0:T(8,128)(2,1)} collective-permute-done((bf16[256,1536]{1,0:T(8,128)(2,1)}, bf16[256,1536]{1,0:T(8,128)(2,1)}, u32[]{:S(2)}, u32[]{:S(2)}) %collective-permute-start.3) | collective-permute-done | bytes 786464 | tf_op jit(solution)/shard_map/ppermute | solution.py:30
  45.9 7.4 %all-to-all-start.1 = ((bf16[8,32,1536]{2,1,0:T(8,128)(2,1)}), bf16[8,32,1536]{2,1,0:T(8,128)(2,1)}, u32[]{:S(2)}, u32[]{:S(2)}) async-start(bf16[8,32,1536]{2,1,0:T(8,128)(2,1)} %bitcast.53), calls=%async_computation.1 | async-start | bytes 1572864 | tf_op jit(solution)/shard_map/all_to_all | solution.py:35
  55.4 2.7 %collective-permute-start.12 = (bf16[128,1536]{1,0:T(8,128)(2,1)}, bf16[128,1536]{1,0:T(8,128)(2,1)}, u32[]{:S(2)}, u32[]{:S(2)}) collective-permute-start(bf16[128,1536]{1,0:T(8,128)(2,1)} %slice.25), channel_id=1, source_target_pairs={{0,3},{1,0},{2,1},{3,2},{4,7},{5,4},{6,5},{7,6},{8,11},{9,8},{10,9... | collective-permute-start | bytes 1179656 | tf_op jit(solution)/shard_map/ppermute | solution.py:30
  58.0 23.5 %collective-permute-done.12 = bf16[128,1536]{1,0:T(8,128)(2,1)} collective-permute-done((bf16[128,1536]{1,0:T(8,128)(2,1)}, bf16[128,1536]{1,0:T(8,128)(2,1)}, u32[]{:S(2)}, u32[]{:S(2)}) %collective-permute-start.12) | collective-permute-done | bytes 393248 | tf_op jit(solution)/shard_map/ppermute | solution.py:30
  81.6 2.7 %collective-permute-done.11 = bf16[128,1536]{1,0:T(8,128)(2,1)} collective-permute-done((bf16[128,1536]{1,0:T(8,128)(2,1)}, bf16[128,1536]{1,0:T(8,128)(2,1)}, u32[]{:S(2)}, u32[]{:S(2)}) %collective-permute-start.11) | collective-permute-done | bytes 393248 | tf_op jit(solution)/shard_map/ppermute | solution.py:30
  96.6 6.9 %all-to-all-start.2 = ((bf16[8,128,1536]{2,1,0:T(8,128)(2,1)}), bf16[8,128,1536]{2,1,0:T(8,128)(2,1)}, u32[]{:S(2)}, u32[]{:S(2)}) async-start(bf16[8,128,1536]{2,1,0:T(8,128)(2,1)} %bitcast.47), calls=%async_computation.2 | async-start | bytes 6291456 | tf_op jit(solution)/shard_map/all_to_all | solution.py:35
  105.6 3.2 %collective-permute-start.9 = (bf16[128,1536]{1,0:T(8,128)(2,1)}, bf16[128,1536]{1,0:T(8,128)(2,1)S(1)}, u32[]{:S(2)}, u32[]{:S(2)}) collective-permute-start(bf16[128,1536]{1,0:T(8,128)(2,1)} %slice.29), channel_id=1, source_target_pairs={{0,3},{1,0},{2,1},{3,2},{4,7},{5,4},{6,5},{7,6},{8,11},{9,8},{10,9... | collective-permute-start | bytes 1179656 | tf_op jit(solution)/shard_map/ppermute | solution.py:30
  111.9 4.7 %shard_map.151 = (bf16[256,768]{1,0:T(8,128)(2,1)S(1)}, bf16[256,768]{1,0:T(8,128)(2,1)S(1)}, bf16[256,768]{1,0:T(8,128)(2,1)S(1)}, bf16[256,768]{1,0:T(8,128)(2...) custom-call(s32[1]{0:T(128)} %bitcast.14.place_ref, bf16[1536,768]{1,0:T(8,128)(2,1)S(1)} %bitcast.32, ...), custom_call_target="tpu_custom_call" | custom-call | flops 2415919104 | bytes 12582916 | tf_op jit(solution)/shard_map/pallas_call | solution.py:69
  117.4 14.7 %collective-permute-done.8.refs_0_.refs_7_ = bf16[128,1536]{1,0:T(8,128)(2,1)S(1)} collective-permute-done((bf16[128,1536]{1,0:T(8,128)(2,1)}, bf16[128,1536]{1,0:T(8,128)(2,1)S(1)}, u32[]{:S(2)}, u32[]{:S(2)}) %collective-permute-start.8) | collective-permute-done | bytes 393248 | tf_op jit(solution)/shard_map/ppermute | solution.py:30
  132.0 3.2 %shard_map.152 = (bf16[256,768]{1,0:T(8,128)(2,1)S(1)}, bf16[256,768]{1,0:T(8,128)(2,1)S(1)}, bf16[128,1536]{1,0:T(8,128)(2,1)S(1)}, bf16[128,1536]{1,0:T(8,128)(2,1)S(1)}) custom-call(s32[1]{0:T(128)} %bitcast.14.place_ref, bf16[1536,768]{1,0:T(8,128)(2,1)S(1)} %bitcast.33, bf16[768,1536]{1,0:T(8,128)(2,1)S(1)} %bitcast.39, ...), custom_call_target="tpu_custom_call" | custom-call | flops 1207959552 | bytes 8650756 | tf_op jit(solution)/shard_map/pallas_call | solution.py:69
  139.7 2.9 %shard_map.150.one_ref = bf16[256,1536]{1,0:T(8,128)(2,1)S(1)} custom-call(bf16[1536,768]{1,0:T(8,128)(2,1)S(1)} %bitcast.34, bf16[768,1536]{1,0:T(8,128)(2,1)S(1)} %bitcast.40, bf16[256,1536]{1,0:T(8,128)(2,1)} %bitcast.13.refs_0_), custom_call_target="tpu_custom_call" | custom-call | flops 1207959552 | bytes 6291456 | tf_op jit(solution)/shard_map/pallas_call | solution.py:69
  143.5 6.0 %shard_map.154 = bf16[768,1536]{1,0:T(8,128)(2,1)} custom-call(bf16[256,768]{1,0:T(8,128)(2,1)S(1)} %copy-done.35, bf16[256,768]{1,0:T(8,128)(2,1)S(1)} %get-tuple-element.54.refs_1_, bf16[256,768]{1,0:T(8,128)(2,1)S(1)} %get-tuple-element.55.refs_2_, bf16[256,768]{1,0:T(8,128)(2,1)S(1)} %get-tuple-element.56.refs_3_, bf16[256,1536]{1,0:T(8,128)(2,1)S(1)} %bitcast.51, ...), custom_call_target="tpu_custom_call" | custom-call | flops 2415919104 | bytes 7077888 | tf_op jit(solution)/shard_map/pallas_call | solution.py:69
  149.5 3.5 %collective-permute-done.14.refs_1_ = bf16[128,1536]{1,0:T(8,128)(2,1)S(1)} collective-permute-done((bf16[128,1536]{1,0:T(8,128)(2,1)S(1)}, bf16[128,1536]{1,0:T(8,128)(2,1)S(1)}, u32[]{:S(2)}, u32[]{:S(2)}) %collective-permute-start.14) | collective-permute-done | bytes 393248 | tf_op jit(solution)/shard_map/ppermute | solution.py:30
  157.5 3.0 %shard_map.157 = (bf16[256,1536]{1,0:T(8,128)(2,1)S(1)}, bf16[256,1536]{1,0:T(8,128)(2,1)S(1)}) custom-call(bf16[1536,768]{1,0:T(8,128)(2,1)S(1)} %bitcast.35, bf16[768,1536]{1,0:T(8,128)(2,1)S(1)} %bitcast.41, bf16[256,1536]{1,0:T(8,128)(2,1)S(1)} %collective-permute-done.6.refs_0_, bf16[256,1536]{1,0:T(8,128)(2,1)S(1)} %collective-permute-done.7.refs_1_), custom_call_target="tpu_custom_call" | custom-call | flops 2415919104 | bytes 7864320 | tf_op jit(solution)/shard_map/pallas_call | solution.py:69
  162.3 2.9 %collective-permute-start.18 = (bf16[128,1536]{1,0:T(8,128)(2,1)S(1)}, bf16[128,1536]{1,0:T(8,128)(2,1)S(1)}, u32[]{:S(2)}, u32[]{:S(2)}) collective-permute-start(bf16[128,1536]{1,0:T(8,128)(2,1)S(1)} %get-tuple-element.74), channel_id=1, source_target_pairs={{0,3},{1,0},{2,1},{3,2},{4,7},{5,4},{6,5},{7,6},{8,11},{9,8},{10,9... | collective-permute-start | bytes 1179656 | tf_op jit(solution)/shard_map/ppermute | solution.py:30
  165.3 16.8 %collective-permute-done.16.more_ref = bf16[128,1536]{1,0:T(8,128)(2,1)S(1)} collective-permute-done((bf16[128,1536]{1,0:T(8,128)(2,1)S(1)}, bf16[128,1536]{1,0:T(8,128)(2,1)S(1)}, u32[]{:S(2)}, u32[]{:S(2)}) %collective-permute-start.16) | collective-permute-done | bytes 393248 | tf_op jit(solution)/shard_map/ppermute | solution.py:30
  184.8 6.4 %all-to-all-start.3 = ((bf16[8,32,1536]{2,1,0:T(8,128)(2,1)}), bf16[8,32,1536]{2,1,0:T(8,128)(2,1)S(1)}, u32[]{:S(2)}, u32[]{:S(2)}) async-start(bf16[8,32,1536]{2,1,0:T(8,128)(2,1)} %bitcast.23), calls=%async_computation.3 | async-start | bytes 1572864 | tf_op jit(solution)/shard_map/all_to_all | solution.py:35
  191.2 3.2 %collective-permute-start.19 = (bf16[256,1536]{1,0:T(8,128)(2,1)S(1)}, bf16[256,1536]{1,0:T(8,128)(2,1)S(1)}, u32[]{:S(2)}, u32[]{:S(2)}) collective-permute-start(bf16[256,1536]{1,0:T(8,128)(2,1)S(1)} %copy-done.21), channel_id=1, source_target_pairs={{0,3},{1,0},{2,1},{3,2},{4,7},{5,4},{6,5},{7,6},{8,11},{9,8},{10,9... | collective-permute-start | bytes 2359304 | tf_op jit(solution)/shard_map/ppermute | solution.py:30
  196.4 6.8 %shard_map.161 = bf16[1536,768]{1,0:T(8,128)(2,1)} custom-call(bf16[8,4,32,1536]{3,2,1,0:T(8,128)(2,1)} %bitcast.22.rows_ref, bf16[256,768]{1,0:T(8,128)(2,1)S(1)} %copy-done.27, bf16[256,768]{1,0:T(8,128)(2,1)S(1)} %copy-done.29, bf16[256,768]{1,0:T(8,128)(2,1)S(1)} %copy-done.31, bf16[256,768]{1,0:T(8,128)(2,1)S(1)} %copy-done.33), custom_call_target="tpu_custom_call" | custom-call | flops 2415919104 | bytes 7077888 | tf_op jit(solution)/shard_map/pallas_call | solution.py:69
  203.2 4.0 %collective-permute-done.17.two_ref = bf16[256,1536]{1,0:T(8,128)(2,1)S(1)} collective-permute-done((bf16[256,1536]{1,0:T(8,128)(2,1)S(1)}, bf16[256,1536]{1,0:T(8,128)(2,1)S(1)}, u32[]{:S(2)}, u32[]{:S(2)}) %collective-permute-start.17) | collective-permute-done | bytes 786464 | tf_op jit(solution)/shard_map/ppermute | solution.py:30
  210.1 5.4 %all-to-all-start.4 = ((bf16[8,32,1536]{2,1,0:T(8,128)(2,1)}), bf16[8,32,1536]{2,1,0:T(8,128)(2,1)S(1)}, u32[]{:S(2)}, u32[]{:S(2)}) async-start(bf16[8,32,1536]{2,1,0:T(8,128)(2,1)} %bitcast.25), calls=%async_computation.4 | async-start | bytes 1572864 | tf_op jit(solution)/shard_map/all_to_all | solution.py:35
  216.9 16.2 %all-to-all-done.4 = bf16[8,32,1536]{2,1,0:T(8,128)(2,1)S(1)} async-done(((bf16[8,32,1536]{2,1,0:T(8,128)(2,1)}), bf16[8,32,1536]{2,1,0:T(8,128)(2,1)S(1)}, u32[]{:S(2)}, u32[]{:S(2)}) %all-to-all-start.4) | async-done | bytes 786464 | tf_op jit(solution)/shard_map/all_to_all | solution.py:35
  (137 shorter events, 62.9 us)
Async XLA Ops:
  8.1 37.8 %all-to-all-start = ((bf16[8,32,1536]{2,1,0:T(8,128)(2,1)}), bf16[8,32,1536]{2,1,0:T(8,128)(2,1)S(1)}, u32[]{:S(2)}, u32[]{:S(2)}) async-start(bf16[8,32,1536]{2,1,0:T(8,128)(2,1)} %bitcast.10), calls=%async_computation | async-start | bytes 1572864 | tf_op jit(solution)/shard_map/all_to_all | solution.py:35
  16.6 20.0 %collective-permute-start.3 = (bf16[256,1536]{1,0:T(8,128)(2,1)}, bf16[256,1536]{1,0:T(8,128)(2,1)}, u32[]{:S(2)}, u32[]{:S(2)}) collective-permute-start(bf16[256,1536]{1,0:T(8,128)(2,1)} %copy-done.7), channel_id=1, source_target_pairs={{0,3},{1,0},{2,1},{3,2},{4,7},{5,4},{6,5},{7,6},{8,11},{9,8},{10,9... | collective-permute-start | bytes 2359304 | tf_op jit(solution)/shard_map/ppermute | solution.py:30
  19.7 20.9 %collective-permute-start.2 = (bf16[256,1536]{1,0:T(8,128)(2,1)}, bf16[256,1536]{1,0:T(8,128)(2,1)}, u32[]{:S(2)}, u32[]{:S(2)}) collective-permute-start(bf16[256,1536]{1,0:T(8,128)(2,1)} %copy-done.7), channel_id=1, source_target_pairs={{0,1},{1,2},{2,3},{3,0},{4,5},{5,6},{6,7},{7,4},{8,9},{9,10},{10,1... | collective-permute-start | bytes 2359304 | tf_op jit(solution)/shard_map/ppermute | solution.py:30
  19.7 22.7 %collective-permute-start.1 = (bf16[1,128,1536]{2,1,0:T(8,128)(2,1)}, bf16[1,128,1536]{2,1,0:T(8,128)(2,1)}, u32[]{:S(2)}, u32[]{:S(2)}) collective-permute-start(bf16[1,128,1536]{2,1,0:T(8,128)(2,1)} %param.12), channel_id=1, source_target_pairs={{224,0},{0,32},{32,64},{64,96},{96,128},{128,160},{160,192},{192,2... | collective-permute-start | bytes 1179656 | tf_op jit(solution)/shard_map/ppermute | solution.py:21
  45.9 50.7 %all-to-all-start.1 = ((bf16[8,32,1536]{2,1,0:T(8,128)(2,1)}), bf16[8,32,1536]{2,1,0:T(8,128)(2,1)}, u32[]{:S(2)}, u32[]{:S(2)}) async-start(bf16[8,32,1536]{2,1,0:T(8,128)(2,1)} %bitcast.53), calls=%async_computation.1 | async-start | bytes 1572864 | tf_op jit(solution)/shard_map/all_to_all | solution.py:35
  53.3 36.0 %collective-permute-start.5 = (bf16[256,1536]{1,0:T(8,128)(2,1)S(1)}, bf16[256,1536]{1,0:T(8,128)(2,1)}, u32[]{:S(2)}, u32[]{:S(2)}) collective-permute-start(bf16[256,1536]{1,0:T(8,128)(2,1)S(1)} %bitcast.48), channel_id=1, source_target_pairs={{0,3},{1,0},{2,1},{3,2},{4,7},{5,4},{6,5},{7,6},{8,11},{9,8},{10,9... | collective-permute-start | bytes 2359304 | tf_op jit(solution)/shard_map/ppermute | solution.py:30
  54.8 36.6 %collective-permute-start.4 = (bf16[256,1536]{1,0:T(8,128)(2,1)S(1)}, bf16[256,1536]{1,0:T(8,128)(2,1)}, u32[]{:S(2)}, u32[]{:S(2)}) collective-permute-start(bf16[256,1536]{1,0:T(8,128)(2,1)S(1)} %bitcast.49), channel_id=1, source_target_pairs={{0,1},{1,2},{2,3},{3,0},{4,5},{5,6},{6,7},{7,4},{8,9},{9,10},{10,1... | collective-permute-start | bytes 2359304 | tf_op jit(solution)/shard_map/ppermute | solution.py:30
  55.4 26.2 %collective-permute-start.12 = (bf16[128,1536]{1,0:T(8,128)(2,1)}, bf16[128,1536]{1,0:T(8,128)(2,1)}, u32[]{:S(2)}, u32[]{:S(2)}) collective-permute-start(bf16[128,1536]{1,0:T(8,128)(2,1)} %slice.25), channel_id=1, source_target_pairs={{0,3},{1,0},{2,1},{3,2},{4,7},{5,4},{6,5},{7,6},{8,11},{9,8},{10,9... | collective-permute-start | bytes 1179656 | tf_op jit(solution)/shard_map/ppermute | solution.py:30
  58.0 26.2 %collective-permute-start.11 = (bf16[128,1536]{1,0:T(8,128)(2,1)}, bf16[128,1536]{1,0:T(8,128)(2,1)}, u32[]{:S(2)}, u32[]{:S(2)}) collective-permute-start(bf16[128,1536]{1,0:T(8,128)(2,1)} %slice.24), channel_id=1, source_target_pairs={{0,1},{1,2},{2,3},{3,0},{4,5},{5,6},{6,7},{7,4},{8,9},{9,10},{10,1... | collective-permute-start | bytes 1179656 | tf_op jit(solution)/shard_map/ppermute | solution.py:30
  96.6 88.2 %all-to-all-start.2 = ((bf16[8,128,1536]{2,1,0:T(8,128)(2,1)}), bf16[8,128,1536]{2,1,0:T(8,128)(2,1)}, u32[]{:S(2)}, u32[]{:S(2)}) async-start(bf16[8,128,1536]{2,1,0:T(8,128)(2,1)} %bitcast.47), calls=%async_computation.2 | async-start | bytes 6291456 | tf_op jit(solution)/shard_map/all_to_all | solution.py:35
  103.5 32.1 %collective-permute-start.7 = (bf16[256,1536]{1,0:T(8,128)(2,1)}, bf16[256,1536]{1,0:T(8,128)(2,1)S(1)}, u32[]{:S(2)}, u32[]{:S(2)}) collective-permute-start(bf16[256,1536]{1,0:T(8,128)(2,1)} %bitcast.13.refs_0_), channel_id=1, source_target_pairs={{0,3},{1,0},{2,1},{3,2},{4,7},{5,4},{6,5},{7,6},{8,11},{9,8},{10,9... | collective-permute-start | bytes 2359304 | tf_op jit(solution)/shard_map/ppermute | solution.py:30
  103.8 32.8 %collective-permute-start.6 = (bf16[256,1536]{1,0:T(8,128)(2,1)}, bf16[256,1536]{1,0:T(8,128)(2,1)S(1)}, u32[]{:S(2)}, u32[]{:S(2)}) collective-permute-start(bf16[256,1536]{1,0:T(8,128)(2,1)} %bitcast.13.refs_0_), channel_id=1, source_target_pairs={{0,1},{1,2},{2,3},{3,0},{4,5},{5,6},{6,7},{7,4},{8,9},{9,10},{10,1... | collective-permute-start | bytes 2359304 | tf_op jit(solution)/shard_map/ppermute | solution.py:30
  105.6 26.4 %collective-permute-start.8 = (bf16[128,1536]{1,0:T(8,128)(2,1)}, bf16[128,1536]{1,0:T(8,128)(2,1)S(1)}, u32[]{:S(2)}, u32[]{:S(2)}) collective-permute-start(bf16[128,1536]{1,0:T(8,128)(2,1)} %slice.28), channel_id=1, source_target_pairs={{0,1},{1,2},{2,3},{3,0},{4,5},{5,6},{6,7},{7,4},{8,9},{9,10},{10,1... | collective-permute-start | bytes 1179656 | tf_op jit(solution)/shard_map/ppermute | solution.py:30
  105.6 26.4 %collective-permute-start.9 = (bf16[128,1536]{1,0:T(8,128)(2,1)}, bf16[128,1536]{1,0:T(8,128)(2,1)S(1)}, u32[]{:S(2)}, u32[]{:S(2)}) collective-permute-start(bf16[128,1536]{1,0:T(8,128)(2,1)} %slice.29), channel_id=1, source_target_pairs={{0,3},{1,0},{2,1},{3,2},{4,7},{5,4},{6,5},{7,6},{8,11},{9,8},{10,9... | collective-permute-start | bytes 1179656 | tf_op jit(solution)/shard_map/ppermute | solution.py:30
  135.7 17.3 %collective-permute-start.14 = (bf16[128,1536]{1,0:T(8,128)(2,1)S(1)}, bf16[128,1536]{1,0:T(8,128)(2,1)S(1)}, u32[]{:S(2)}, u32[]{:S(2)}) collective-permute-start(bf16[128,1536]{1,0:T(8,128)(2,1)S(1)} %slice.27), channel_id=1, source_target_pairs={{0,3},{1,0},{2,1},{3,2},{4,7},{5,4},{6,5},{7,6},{8,11},{9,8},{10,9... | collective-permute-start | bytes 1179656 | tf_op jit(solution)/shard_map/ppermute | solution.py:30
  136.7 16.3 %collective-permute-start.13 = (bf16[128,1536]{1,0:T(8,128)(2,1)S(1)}, bf16[128,1536]{1,0:T(8,128)(2,1)S(1)}, u32[]{:S(2)}, u32[]{:S(2)}) collective-permute-start(bf16[128,1536]{1,0:T(8,128)(2,1)S(1)} %slice.26), channel_id=1, source_target_pairs={{0,1},{1,2},{2,3},{3,0},{4,5},{5,6},{6,7},{7,4},{8,9},{9,10},{10,1... | collective-permute-start | bytes 1179656 | tf_op jit(solution)/shard_map/ppermute | solution.py:30
  137.9 17.0 %collective-permute-start.10 = (bf16[128,1536]{1,0:T(8,128)(2,1)S(1)}, bf16[128,1536]{1,0:T(8,128)(2,1)S(1)}, u32[]{:S(2)}, u32[]{:S(2)}) collective-permute-start(bf16[128,1536]{1,0:T(8,128)(2,1)S(1)} %get-tuple-element.51), channel_id=1, source_target_pairs={{0,1},{1,2},{2,3},{3,0},{4,5},{5,6},{6,7},{7,4},{8,9},{9,10},{10,1... | collective-permute-start | bytes 1179656 | tf_op jit(solution)/shard_map/ppermute | solution.py:30
  154.9 28.7 %collective-permute-start.21 = (bf16[256,1536]{1,0:T(8,128)(2,1)S(1)}, bf16[256,1536]{1,0:T(8,128)(2,1)S(1)}, u32[]{:S(2)}, u32[]{:S(2)}) collective-permute-start(bf16[256,1536]{1,0:T(8,128)(2,1)S(1)} %shard_map.156), channel_id=1, source_target_pairs={{0,3},{1,0},{2,1},{3,2},{4,7},{5,4},{6,5},{7,6},{8,11},{9,8},{10,9... | collective-permute-start | bytes 2359304 | tf_op jit(solution)/shard_map/ppermute | solution.py:30
  155.8 27.8 %collective-permute-start.20 = (bf16[256,1536]{1,0:T(8,128)(2,1)S(1)}, bf16[256,1536]{1,0:T(8,128)(2,1)S(1)}, u32[]{:S(2)}, u32[]{:S(2)}) collective-permute-start(bf16[256,1536]{1,0:T(8,128)(2,1)S(1)} %shard_map.155), channel_id=1, source_target_pairs={{0,1},{1,2},{2,3},{3,0},{4,5},{5,6},{6,7},{7,4},{8,9},{9,10},{10,1... | collective-permute-start | bytes 2359304 | tf_op jit(solution)/shard_map/ppermute | solution.py:30
  161.9 20.1 %collective-permute-start.16 = (bf16[128,1536]{1,0:T(8,128)(2,1)S(1)}, bf16[128,1536]{1,0:T(8,128)(2,1)S(1)}, u32[]{:S(2)}, u32[]{:S(2)}) collective-permute-start(bf16[128,1536]{1,0:T(8,128)(2,1)S(1)} %get-tuple-element.65), channel_id=1, source_target_pairs={{0,1},{1,2},{2,3},{3,0},{4,5},{5,6},{6,7},{7,4},{8,9},{9,10},{10,1... | collective-permute-start | bytes 1179656 | tf_op jit(solution)/shard_map/ppermute | solution.py:30
  162.3 20.1 %collective-permute-start.18 = (bf16[128,1536]{1,0:T(8,128)(2,1)S(1)}, bf16[128,1536]{1,0:T(8,128)(2,1)S(1)}, u32[]{:S(2)}, u32[]{:S(2)}) collective-permute-start(bf16[128,1536]{1,0:T(8,128)(2,1)S(1)} %get-tuple-element.74), channel_id=1, source_target_pairs={{0,3},{1,0},{2,1},{3,2},{4,7},{5,4},{6,5},{7,6},{8,11},{9,8},{10,9... | collective-permute-start | bytes 1179656 | tf_op jit(solution)/shard_map/ppermute | solution.py:30
  184.8 25.4 %all-to-all-start.3 = ((bf16[8,32,1536]{2,1,0:T(8,128)(2,1)}), bf16[8,32,1536]{2,1,0:T(8,128)(2,1)S(1)}, u32[]{:S(2)}, u32[]{:S(2)}) async-start(bf16[8,32,1536]{2,1,0:T(8,128)(2,1)} %bitcast.23), calls=%async_computation.3 | async-start | bytes 1572864 | tf_op jit(solution)/shard_map/all_to_all | solution.py:35
  191.2 16.0 %collective-permute-start.17 = (bf16[256,1536]{1,0:T(8,128)(2,1)S(1)}, bf16[256,1536]{1,0:T(8,128)(2,1)S(1)}, u32[]{:S(2)}, u32[]{:S(2)}) collective-permute-start(bf16[256,1536]{1,0:T(8,128)(2,1)S(1)} %shard_map.159), channel_id=1, source_target_pairs={{0,1},{1,2},{2,3},{3,0},{4,5},{5,6},{6,7},{7,4},{8,9},{9,10},{10,1... | collective-permute-start | bytes 2359304 | tf_op jit(solution)/shard_map/ppermute | solution.py:30
  210.1 23.0 %all-to-all-start.4 = ((bf16[8,32,1536]{2,1,0:T(8,128)(2,1)}), bf16[8,32,1536]{2,1,0:T(8,128)(2,1)S(1)}, u32[]{:S(2)}, u32[]{:S(2)}) async-start(bf16[8,32,1536]{2,1,0:T(8,128)(2,1)} %bitcast.25), calls=%async_computation.4 | async-start | bytes 1572864 | tf_op jit(solution)/shard_map/all_to_all | solution.py:35
  (41 other events, 381.7 us)

commit v2 on v1

--- a/solution.py
+++ b/solution.py
@@ -123,13 +123,57 @@
     out_ref[...] = matmul(pick, normed, ((0,), (0,))).astype(jnp.bfloat16)
 
 
-def pick_backward_kernel(cap_rows, tokens_ref, gain_ref, route_ref, slot_ref, out_ref):
-    normed = normed_of(tokens_ref, gain_ref)
-    pick = sum(
-        hits_of(t, out_ref.shape[0]).astype(jnp.float32)
-        for t in backward_targets(route_ref[...], slot_ref[...], cap_rows)
-    ).astype(jnp.bfloat16)
-    out_ref[...] = matmul(pick, normed, ((0,), (0,))).astype(jnp.bfloat16)
+def tagged_kernel(tokens_ref, gain_ref, route_ref, slot_ref, out_ref):
+    tokens, features = tokens_ref.shape
+    choices = route_ref.shape[1]
+    out_ref[:, :features] = normed_of(tokens_ref, gain_ref)
+    lanes = lax.broadcasted_iota(jnp.int32, (tokens, out_ref.shape[1] - features), 1)
+    tags = jnp.zeros(lanes.shape, jnp.int32)
+    for k in range(choices):
+        tags = jnp.where(lanes == k, route_ref[:, k : k + 1], tags)
+        tags = jnp.where(lanes == choices + k, slot_ref[:, k : k + 1], tags)
+    out_ref[:, features:] = tags.astype(jnp.float32).astype(jnp.bfloat16)
+
+
+def picked_rows_kernel(choices, own_ref, left_ref, right_ref, top_ref, bottom_ref, out_ref):
+    experts, _, cap_rows, features = out_ref.shape
+    for c, pieces in enumerate(((own_ref,), (left_ref,), (right_ref,), (top_ref, bottom_ref))):
+        rows = None
+        for ref in pieces:
+            tags = ref[:, features:].astype(jnp.float32).astype(jnp.int32)
+            pick = None
+            for k in range(choices):
+                target = tags[:, k : k + 1] * cap_rows + tags[:, choices + k : choices + k + 1]
+                hit = hits_of(target, experts * cap_rows).astype(jnp.float32)
+                pick = hit if pick is None else pick + hit
+            part = matmul(pick.astype(jnp.bfloat16), ref[:, :features], ((0,), (0,)))
+            rows = part if rows is None else rows + part
+        out_ref[:, c] = rows.astype(jnp.bfloat16).reshape(experts, cap_rows, features)
+
+
+def cut_kernel(left_ref, right_ref, top_ref, bottom_ref, sems):
+    half = top_ref.shape[0]
+    copies = [
+        pltpu.make_async_copy(left_ref.at[:half], top_ref, sems.at[0]),
+        pltpu.make_async_copy(right_ref.at[half:], bottom_ref, sems.at[1]),
+    ]
+    for copy in copies:
+        copy.start()
+    for copy in copies:
+        copy.wait()
+
+
+def cut_halves(left, right):
+    anywhere = pl.BlockSpec(memory_space=pl.ANY)
+    return call(
+        cut_kernel,
+        [jax.ShapeDtypeStruct((left.shape[0] // 2, left.shape[1]), left.dtype)] * 2,
+        [left, right],
+        0,
+        in_specs=[anywhere] * 2,
+        out_specs=[anywhere] * 2,
+        scratch_shapes=[pltpu.SemaphoreType.DMA((2,))],
+    )
 
 
 def pick_grad_kernel(cap_rows, cot_ref, gate_ref, route_ref, slot_ref, out_ref):
@@ -325,41 +369,6 @@
     )[0]
 
 
-def assemble_kernel(own_ref, left_ref, right_ref, top_ref, bottom_ref, out_ref, sems):
-    upper = top_ref.shape[0]
-    copies = [
-        (own_ref, out_ref.at[:, 0]),
-        (left_ref, out_ref.at[:, 1]),
-        (right_ref, out_ref.at[:, 2]),
-        (top_ref, out_ref.at[:upper, 3]),
-        (bottom_ref, out_ref.at[upper:, 3]),
-    ]
-    started = [
-        pltpu.make_async_copy(source, target, sems.at[n])
-        for n, (source, target) in enumerate(copies)
-    ]
-    for copy in started:
-        copy.start()
-    for copy in started:
-        copy.wait()
-
-
-def assemble(pieces, cap_rows):
-    features = pieces[0].shape[1]
-    shaped = [p.reshape(-1, cap_rows, features) for p in pieces]
-    experts = shaped[0].shape[0]
-    anywhere = pl.BlockSpec(memory_space=pl.ANY)
-    return call(
-        assemble_kernel,
-        [jax.ShapeDtypeStruct((experts, 4, cap_rows, features), jnp.bfloat16)],
-        shaped,
-        0,
-        in_specs=[anywhere] * 5,
-        out_specs=[pl.BlockSpec(memory_space=pltpu.HBM)],
-        scratch_shapes=[pltpu.SemaphoreType.DMA((5,))],
-    )[0]
-
-
 def add_kernel(into_ref, more_ref, out_ref):
     out_ref[...] = (
         into_ref[...].astype(jnp.float32) + more_ref[...].astype(jnp.float32)
@@ -454,34 +463,31 @@
     def send(values):
         return exchange(values.reshape(EXPERTS, -1, features), groups).reshape(-1, features)
 
-    def halves_of(chunk):
-        return chunk[:half], chunk[half:]
-
     cotangent = shifted(grad_handoff, "section", -1)
     arrival = shifted(after(fwd_handoff, cotangent), "section", 1)[0]
     cotangent = cotangent[0]
 
-    rows_bwd = call(
-        functools.partial(pick_backward_kernel, cap_rows),
-        rows_shape,
+    tagged = call(
+        tagged_kernel,
+        [jax.ShapeDtypeStruct((tok_rows, features + 128), jnp.bfloat16)],
         [saved_input[0], gain, route_bwd[0], slot_bwd[0]],
-        pick_flops,
-    )[0]
-    rows_left, rows_right = turned(rows_bwd, groups, 1), turned(rows_bwd, groups, -1)
-    rows_left_top, rows_right_bottom = rows_left[:half], rows_right[half:]
-    rows_top = turned(rows_left_top, groups, 1)
-    rows_bottom = turned(rows_right_bottom, groups, -1)
+        0,
+    )[0]
+    tagged_left, tagged_right = turned(tagged, groups, 1), turned(tagged, groups, -1)
+    tagged_left_top, tagged_right_bottom = cut_halves(tagged_left, tagged_right)
+    tagged_top = turned(tagged_left_top, groups, 1)
+    tagged_bottom = turned(tagged_right_bottom, groups, -1)
 
     grad_rows = call(
         functools.partial(pick_grad_kernel, cap_rows),
         rows_shape,
-        [after(cotangent, rows_bwd), gate_bwd[0], route_bwd[0], slot_bwd[0]],
+        [after(cotangent, tagged), gate_bwd[0], route_bwd[0], slot_bwd[0]],
         2 * pick_flops,
     )[0]
     rows_fwd = call(
         functools.partial(pick_forward_kernel, cap_rows),
         rows_shape,
-        [after(arrival, rows_left_top, rows_right_bottom), gain, route_fwd[0]],
+        [after(arrival, tagged_top, tagged_bottom), gain, route_fwd[0]],
         pick_flops,
     )[0]
 
@@ -490,17 +496,20 @@
     sent_fwd = send(after(rows_fwd, grads))
     whole, halves = (all_rows,), (half, half)
     hidden_0, pre_grad_0, back_0 = backward_chunks(
-        mine, [after(grads, rows_top, rows_bottom)], pre_blocks, w_in_local, w_out_local, [whole], (0,)
-    )
-    grads_left_top, grads_right_bottom = grads_left[:half], grads_right[half:]
+        mine, [grads], pre_blocks, w_in_local, w_out_local, [whole], (0,)
+    )
+    rows_bwd = call(
+        functools.partial(picked_rows_kernel, choices),
+        [jax.ShapeDtypeStruct((EXPERTS, groups, cap_rows, features), jnp.bfloat16)],
+        [after(tagged, rows_fwd, *back_0), tagged_left, tagged_right, tagged_top, tagged_bottom],
+        groups * pick_flops,
+    )[0]
+    grads_left_top, grads_right_bottom = cut_halves(after(grads_left, rows_bwd), grads_right)
     grads_top = turned(grads_left_top, groups, 1)
     grads_bottom = turned(grads_right_bottom, groups, -1)
-    assembled = assemble(
-        [after(rows_bwd, grads_left_top, grads_right_bottom, *back_0), rows_left, rows_right, rows_top, rows_bottom], cap_rows
-    )
     ready = after(sent_fwd, grads_left, grads_right)
     left, right = turned(ready, groups, 1), turned(ready, groups, -1)
-    sent_rows = send(after(assembled, sent_fwd))
+    sent_rows = send(after(rows_bwd, sent_fwd, grads_left_top, grads_right_bottom))
 
     hidden_1, pre_grad_1, back_1 = backward_chunks(
         mine,
@@ -524,7 +533,7 @@
     back_top = turned(back_2[0], groups, 1)
     back_bottom = turned(back_2[1], groups, -1)
 
-    left_top, right_bottom = left[:half], right[half:]
+    left_top, right_bottom = cut_halves(left, right)
     opposite_top = turned(left_top, groups, 1)
     opposite_bottom = turned(right_bottom, groups, -1)
     grad_w_out = weight_grad(
@@ -553,7 +562,7 @@
     fwd_to_right = add_half(fwd_1[0], fwd_bottom, 1)
     return_bwd = send(after(back_sum, sent_rows, fwd_to_left, fwd_to_right))
     grad_w_in = exchanged_grad(
-        sent_rows.reshape(assembled.shape), [*pre_grad_0, *pre_grad_1, *pre_grad_2], 256
+        sent_rows.reshape(rows_bwd.shape), [*pre_grad_0, *pre_grad_1, *pre_grad_2], 256
     )
 
     fwd_left = turned(fwd_to_left, groups, 1)

time: 237 us -> 236 us (level)
  Pallas kernels: 43 us -> 68 us
  waiting for transfers between devices: 101 us -> 77.2 us
  local copies, waits for them, and re-layouts: 27.4 us -> 23.2 us
  starting transfers between devices: 63.1 us -> 65.9 us
    pallas_call x20 -> x23, Pallas kernels: 43 us -> 68 us  [call(): pl.pallas_call(kernel, out_shape=out_shapes, cost_estimate=pl.CostEstimat...]
    ppermute x20, waiting for transfers between devices: 83.2 us -> 63.3 us  [turned(): return lax.ppermute(block, 'expert', route)]
    slice x6 -> x0, local copies, waits for them, and re-layouts: 7.43 us -> none  [the longest x2 3.84 us: body(): grads_left_top, grads_right_bottom = (grads_left[:half], grads_right[half:])]
    all_to_all x5, waiting for transfers between devices: 17.9 us -> 13.4 us  [exchange(): lax.all_to_all(block, 'expert', split_axis=0, concat_axis=0, tiled=True,...]
    unnamed x81 -> x95, local copies, waits for them, and re-layouts: 20 us -> 23.2 us
    ppermute x20, starting transfers between devices: 26.2 us -> 28.8 us  [turned(): return lax.ppermute(block, 'expert', route)]
  transfers between devices with their start and end apart: 27 -> 27, of which waited for: 11 -> 12; matrix products, arithmetic and copies ran while one was open for 5% -> 1% of each run, Pallas kernels for 17% -> 28%
where the time goes in v2:
time: 236 us; the launch traced here: 235 us
  waiting for transfers between devices  77.2 us (33%)
  Pallas kernels  68 us (29%)
  starting transfers between devices  65.9 us (28%)
  local copies, waits for them, and re-layouts  23.2 us (10%)
    pallas_call x23, Pallas kernels, call(): pl.pallas_call(kernel, out_shape=out_shapes, cost_estimate=pl.CostEstimat...  68 us
    ppermute x20, waiting for transfers between devices, turned(): return lax.ppermute(block, 'expert', route)  63.3 us
    all_to_all x5, starting transfers between devices, exchange(): lax.all_to_all(block, 'expert', split_axis=0, concat_axis=0, tiled=True,...  34.8 us
    ppermute x20, starting transfers between devices, turned(): return lax.ppermute(block, 'expert', route)  28.8 us
    unnamed x95, local copies, waits for them, and re-layouts  23.2 us
    all_to_all x5, waiting for transfers between devices, exchange(): lax.all_to_all(block, 'expert', split_axis=0, concat_axis=0, tiled=True,...  13.4 us
  transfers between devices with their start and end apart: 27, of which 12 were waited for; matrix products, arithmetic and copies ran while one was open for 1% of the time, Pallas kernels for 28%

profile of v2, /device:TPU:6, one launch (start us, length us, event | category | flops | bytes accessed | tf_op | source)
XLA Modules:
  0.0 235.3 jit_solution(1097628780706986335)
XLA Ops:
  8.1 8.6 %all-to-all-start = ((bf16[8,32,1536]{2,1,0:T(8,128)(2,1)}), bf16[8,32,1536]{2,1,0:T(8,128)(2,1)S(1)}, u32[]{:S(2)}, u32[]{:S(2)}) async-start(bf16[8,32,1536]{2,1,0:T(8,128)(2,1)} %bitcast.48), calls=%async_computation | async-start | bytes 1572864 | tf_op jit(solution)/shard_map/all_to_all | solution.py:35
  16.7 3.0 %collective-permute-start.3 = (bf16[128,1664]{1,0:T(8,128)(2,1)}, bf16[128,1664]{1,0:T(8,128)(2,1)S(1)}, u32[]{:S(2)}, u32[]{:S(2)}) collective-permute-start(bf16[128,1664]{1,0:T(8,128)(2,1)} %copy-done.11), channel_id=1, source_target_pairs={{0,3},{1,0},{2,1},{3,2},{4,7},{5,4},{6,5},{7,6},{8,11},{9,8},{10,9... | collective-permute-start | bytes 1277960 | tf_op jit(solution)/shard_map/ppermute | solution.py:30
  21.8 7.1 %collective-permute-done.3.right_ref = bf16[128,1664]{1,0:T(8,128)(2,1)S(1)} collective-permute-done((bf16[128,1664]{1,0:T(8,128)(2,1)}, bf16[128,1664]{1,0:T(8,128)(2,1)S(1)}, u32[]{:S(2)}, u32[]{:S(2)}) %collective-permute-start.3) | collective-permute-done | bytes 426016 | tf_op jit(solution)/shard_map/ppermute | solution.py:30
  28.9 3.9 %collective-permute-done.2.left_ref = bf16[128,1664]{1,0:T(8,128)(2,1)S(1)} collective-permute-done((bf16[128,1664]{1,0:T(8,128)(2,1)}, bf16[128,1664]{1,0:T(8,128)(2,1)S(1)}, u32[]{:S(2)}, u32[]{:S(2)}) %collective-permute-start.2) | collective-permute-done | bytes 426016 | tf_op jit(solution)/shard_map/ppermute | solution.py:30
  34.5 3.2 %collective-permute-start.5 = (bf16[64,1664]{1,0:T(8,128)(2,1)}, bf16[64,1664]{1,0:T(8,128)(2,1)}, u32[]{:S(2)}, u32[]{:S(2)}) collective-permute-start(bf16[64,1664]{1,0:T(8,128)(2,1)} %get-tuple-element.49), channel_id=1, source_target_pairs={{0,3},{1,0},{2,1},{3,2},{4,7},{5,4},{6,5},{7,6},{8,11},{9,8},{10,9... | collective-permute-start | bytes 638984 | tf_op jit(solution)/shard_map/ppermute | solution.py:30
  38.5 5.6 %collective-permute-done.4.top_ref = bf16[64,1664]{1,0:T(8,128)(2,1)} collective-permute-done((bf16[64,1664]{1,0:T(8,128)(2,1)}, bf16[64,1664]{1,0:T(8,128)(2,1)}, u32[]{:S(2)}, u32[]{:S(2)}) %collective-permute-start.4) | collective-permute-done | bytes 213024 | tf_op jit(solution)/shard_map/ppermute | solution.py:30
  46.7 7.5 %all-to-all-start.1 = ((bf16[8,32,1536]{2,1,0:T(8,128)(2,1)}), bf16[8,32,1536]{2,1,0:T(8,128)(2,1)}, u32[]{:S(2)}, u32[]{:S(2)}) async-start(bf16[8,32,1536]{2,1,0:T(8,128)(2,1)} %bitcast.47), calls=%async_computation.1 | async-start | bytes 1572864 | tf_op jit(solution)/shard_map/all_to_all | solution.py:35
  54.2 3.2 %collective-permute-start.7 = (bf16[256,1536]{1,0:T(8,128)(2,1)S(1)}, bf16[256,1536]{1,0:T(8,128)(2,1)}, u32[]{:S(2)}, u32[]{:S(2)}) collective-permute-start(bf16[256,1536]{1,0:T(8,128)(2,1)S(1)} %bitcast.44), channel_id=1, source_target_pairs={{0,3},{1,0},{2,1},{3,2},{4,7},{5,4},{6,5},{7,6},{8,11},{9,8},{10,9... | collective-permute-start | bytes 2359304 | tf_op jit(solution)/shard_map/ppermute | solution.py:30
  68.4 6.2 %collective-permute-done.6.refs_0_.left_ref.refs_5_ = bf16[256,1536]{1,0:T(8,128)(2,1)} collective-permute-done((bf16[256,1536]{1,0:T(8,128)(2,1)S(1)}, bf16[256,1536]{1,0:T(8,128)(2,1)}, u32[]{:S(2)}, u32[]{:S(2)}) %collective-permute-start.6) | collective-permute-done | bytes 786464 | tf_op jit(solution)/shard_map/ppermute | solution.py:30
  74.7 24.9 %shard_map.156 = (bf16[128,1536]{1,0:T(8,128)(2,1)}, bf16[128,1536]{1,0:T(8,128)(2,1)}) custom-call(bf16[256,1536]{1,0:T(8,128)(2,1)} %collective-permute-done.6.refs_0_.left_ref.refs_5_, bf16[256,1536]{1,0:T(8,128)(2,1)} %collective-permute-done.7.refs_1_.right_ref.refs_6_), custom_call_target="tpu_custom_call" | custom-call | bytes 2359296 | tf_op jit(solution)/shard_map/pallas_call | solution.py:69
  99.6 6.9 %all-to-all-start.2 = ((bf16[8,128,1536]{2,1,0:T(8,128)(2,1)}), bf16[8,128,1536]{2,1,0:T(8,128)(2,1)}, u32[]{:S(2)}, u32[]{:S(2)}) async-start(bf16[8,128,1536]{2,1,0:T(8,128)(2,1)} %bitcast.42), calls=%async_computation.2 | async-start | bytes 6291456 | tf_op jit(solution)/shard_map/all_to_all | solution.py:35
  109.5 3.3 %collective-permute-start.11 = (bf16[128,1536]{1,0:T(8,128)(2,1)}, bf16[128,1536]{1,0:T(8,128)(2,1)S(1)}, u32[]{:S(2)}, u32[]{:S(2)}) collective-permute-start(bf16[128,1536]{1,0:T(8,128)(2,1)} %get-tuple-element.65), channel_id=1, source_target_pairs={{0,3},{1,0},{2,1},{3,2},{4,7},{5,4},{6,5},{7,6},{8,11},{9,8},{10,9... | collective-permute-start | bytes 1179656 | tf_op jit(solution)/shard_map/ppermute | solution.py:30
  115.9 4.7 %shard_map.153 = (bf16[256,768]{1,0:T(8,128)(2,1)S(1)}, bf16[256,768]{1,0:T(8,128)(2,1)S(1)}, bf16[256,768]{1,0:T(8,128)(2,1)S(1)}, bf16[256,768]{1,0:T(8,128)(2...) custom-call(s32[1]{0:T(128)} %bitcast.14.place_ref, bf16[1536,768]{1,0:T(8,128)(2,1)S(1)} %bitcast.27, ...), custom_call_target="tpu_custom_call" | custom-call | flops 2415919104 | bytes 12582916 | tf_op jit(solution)/shard_map/pallas_call | solution.py:69
  120.6 15.9 %collective-permute-done.10.refs_0_.refs_7_ = bf16[128,1536]{1,0:T(8,128)(2,1)S(1)} collective-permute-done((bf16[128,1536]{1,0:T(8,128)(2,1)}, bf16[128,1536]{1,0:T(8,128)(2,1)S(1)}, u32[]{:S(2)}, u32[]{:S(2)}) %collective-permute-start.10) | collective-permute-done | bytes 393248 | tf_op jit(solution)/shard_map/ppermute | solution.py:30
  136.5 3.2 %shard_map.157 = (bf16[256,768]{1,0:T(8,128)(2,1)S(1)}, bf16[256,768]{1,0:T(8,128)(2,1)S(1)}, bf16[128,1536]{1,0:T(8,128)(2,1)S(1)}, bf16[128,1536]{1,0:T(8,128)(2,1)S(1)}) custom-call(s32[1]{0:T(128)} %bitcast.14.place_ref, bf16[1536,768]{1,0:T(8,128)(2,1)S(1)} %bitcast.28, bf16[768,1536]{1,0:T(8,128)(2,1)S(1)} %bitcast.34, ...), custom_call_target="tpu_custom_call" | custom-call | flops 1207959552 | bytes 8650756 | tf_op jit(solution)/shard_map/pallas_call | solution.py:69
  148.1 6.0 %shard_map.158 = bf16[768,1536]{1,0:T(8,128)(2,1)} custom-call(bf16[256,768]{1,0:T(8,128)(2,1)S(1)} %copy-done.42, bf16[256,768]{1,0:T(8,128)(2,1)S(1)} %get-tuple-element.68.refs_1_, bf16[256,768]{1,0:T(8,128)(2,1)S(1)} %get-tuple-element.69.refs_2_, bf16[256,768]{1,0:T(8,128)(2,1)S(1)} %get-tuple-element.70.refs_3_, bf16[256,1536]{1,0:T(8,128)(2,1)S(1)} %bitcast.46, ...), custom_call_target="tpu_custom_call" | custom-call | flops 2415919104 | bytes 7077888 | tf_op jit(solution)/shard_map/pallas_call | solution.py:69
  160.7 3.0 %shard_map.161 = (bf16[256,1536]{1,0:T(8,128)(2,1)S(1)}, bf16[256,1536]{1,0:T(8,128)(2,1)S(1)}) custom-call(bf16[1536,768]{1,0:T(8,128)(2,1)S(1)} %bitcast.30, bf16[768,1536]{1,0:T(8,128)(2,1)S(1)} %bitcast.36, bf16[256,1536]{1,0:T(8,128)(2,1)S(1)} %collective-permute-done.8.left_ref.refs_0_, bf16[256,1536]{1,0:T(8,128)(2,1)S(1)} %collective-permute-done.9.right_ref.refs_1_), custom_call_target="tpu_custom_call" | custom-call | flops 2415919104 | bytes 7864320 | tf_op jit(solution)/shard_map/pallas_call | solution.py:69
  165.5 3.0 %collective-permute-start.18 = (bf16[128,1536]{1,0:T(8,128)(2,1)S(1)}, bf16[128,1536]{1,0:T(8,128)(2,1)S(1)}, u32[]{:S(2)}, u32[]{:S(2)}) collective-permute-start(bf16[128,1536]{1,0:T(8,128)(2,1)S(1)} %get-tuple-element.86), channel_id=1, source_target_pairs={{0,3},{1,0},{2,1},{3,2},{4,7},{5,4},{6,5},{7,6},{8,11},{9,8},{10,9... | collective-permute-start | bytes 1179656 | tf_op jit(solution)/shard_map/ppermute | solution.py:30
  168.5 15.5 %collective-permute-done.16.more_ref = bf16[128,1536]{1,0:T(8,128)(2,1)S(1)} collective-permute-done((bf16[128,1536]{1,0:T(8,128)(2,1)S(1)}, bf16[128,1536]{1,0:T(8,128)(2,1)S(1)}, u32[]{:S(2)}, u32[]{:S(2)}) %collective-permute-start.16) | collective-permute-done | bytes 393248 | tf_op jit(solution)/shard_map/ppermute | solution.py:30
  186.8 6.3 %all-to-all-start.3 = ((bf16[8,32,1536]{2,1,0:T(8,128)(2,1)}), bf16[8,32,1536]{2,1,0:T(8,128)(2,1)}, u32[]{:S(2)}, u32[]{:S(2)}) async-start(bf16[8,32,1536]{2,1,0:T(8,128)(2,1)} %bitcast.18), calls=%async_computation.3 | async-start | bytes 1572864 | tf_op jit(solution)/shard_map/all_to_all | solution.py:35
  196.3 6.8 %shard_map.164 = bf16[1536,768]{1,0:T(8,128)(2,1)} custom-call(bf16[8,4,32,1536]{3,2,1,0:T(8,128)(2,1)} %bitcast.17.rows_ref, bf16[256,768]{1,0:T(8,128)(2,1)S(1)} %copy-done.36, bf16[256,768]{1,0:T(8,128)(2,1)S(1)} %get-tuple-element.82.refs_1_, bf16[256,768]{1,0:T(8,128)(2,1)S(1)} %copy-done.38, bf16[256,768]{1,0:T(8,128)(2,1)S(1)} %copy-done.40), custom_call_target="tpu_custom_call" | custom-call | flops 2415919104 | bytes 7077888 | tf_op jit(solution)/shard_map/pallas_call | solution.py:69
  203.1 5.3 %collective-permute-done.17.two_ref = bf16[256,1536]{1,0:T(8,128)(2,1)S(1)} collective-permute-done((bf16[256,1536]{1,0:T(8,128)(2,1)}, bf16[256,1536]{1,0:T(8,128)(2,1)S(1)}, u32[]{:S(2)}, u32[]{:S(2)}) %collective-permute-start.17) | collective-permute-done | bytes 786464 | tf_op jit(solution)/shard_map/ppermute | solution.py:30
  211.3 5.4 %all-to-all-start.4 = ((bf16[8,32,1536]{2,1,0:T(8,128)(2,1)}), bf16[8,32,1536]{2,1,0:T(8,128)(2,1)S(1)}, u32[]{:S(2)}, u32[]{:S(2)}) async-start(bf16[8,32,1536]{2,1,0:T(8,128)(2,1)} %bitcast.20), calls=%async_computation.4 | async-start | bytes 1572864 | tf_op jit(solution)/shard_map/all_to_all | solution.py:35
  221.9 11.8 %all-to-all-done.4 = bf16[8,32,1536]{2,1,0:T(8,128)(2,1)S(1)} async-done(((bf16[8,32,1536]{2,1,0:T(8,128)(2,1)}), bf16[8,32,1536]{2,1,0:T(8,128)(2,1)S(1)}, u32[]{:S(2)}, u32[]{:S(2)}) %all-to-all-start.4) | async-done | bytes 786464 | tf_op jit(solution)/shard_map/all_to_all | solution.py:35
  (148 shorter events, 63.6 us)
Async XLA Ops:
  8.1 38.5 %all-to-all-start = ((bf16[8,32,1536]{2,1,0:T(8,128)(2,1)}), bf16[8,32,1536]{2,1,0:T(8,128)(2,1)S(1)}, u32[]{:S(2)}, u32[]{:S(2)}) async-start(bf16[8,32,1536]{2,1,0:T(8,128)(2,1)} %bitcast.48), calls=%async_computation | async-start | bytes 1572864 | tf_op jit(solution)/shard_map/all_to_all | solution.py:35
  16.7 12.2 %collective-permute-start.3 = (bf16[128,1664]{1,0:T(8,128)(2,1)}, bf16[128,1664]{1,0:T(8,128)(2,1)S(1)}, u32[]{:S(2)}, u32[]{:S(2)}) collective-permute-start(bf16[128,1664]{1,0:T(8,128)(2,1)} %copy-done.11), channel_id=1, source_target_pairs={{0,3},{1,0},{2,1},{3,2},{4,7},{5,4},{6,5},{7,6},{8,11},{9,8},{10,9... | collective-permute-start | bytes 1277960 | tf_op jit(solution)/shard_map/ppermute | solution.py:30
  19.8 13.1 %collective-permute-start.2 = (bf16[128,1664]{1,0:T(8,128)(2,1)}, bf16[128,1664]{1,0:T(8,128)(2,1)S(1)}, u32[]{:S(2)}, u32[]{:S(2)}) collective-permute-start(bf16[128,1664]{1,0:T(8,128)(2,1)} %copy-done.11), channel_id=1, source_target_pairs={{0,1},{1,2},{2,3},{3,0},{4,5},{5,6},{6,7},{7,4},{8,9},{9,10},{10,1... | collective-permute-start | bytes 1277960 | tf_op jit(solution)/shard_map/ppermute | solution.py:30
  19.8 24.3 %collective-permute-start.1 = (bf16[1,128,1536]{2,1,0:T(8,128)(2,1)}, bf16[1,128,1536]{2,1,0:T(8,128)(2,1)S(1)}, u32[]{:S(2)}, u32[]{:S(2)}) collective-permute-start(bf16[1,128,1536]{2,1,0:T(8,128)(2,1)} %param.12), channel_id=1, source_target_pairs={{224,0},{0,32},{32,64},{64,96},{96,128},{128,160},{160,192},{192,2... | collective-permute-start | bytes 1179656 | tf_op jit(solution)/shard_map/ppermute | solution.py:21
  46.7 52.9 %all-to-all-start.1 = ((bf16[8,32,1536]{2,1,0:T(8,128)(2,1)}), bf16[8,32,1536]{2,1,0:T(8,128)(2,1)}, u32[]{:S(2)}, u32[]{:S(2)}) async-start(bf16[8,32,1536]{2,1,0:T(8,128)(2,1)} %bitcast.47), calls=%async_computation.1 | async-start | bytes 1572864 | tf_op jit(solution)/shard_map/all_to_all | solution.py:35
  54.2 20.5 %collective-permute-start.6 = (bf16[256,1536]{1,0:T(8,128)(2,1)S(1)}, bf16[256,1536]{1,0:T(8,128)(2,1)}, u32[]{:S(2)}, u32[]{:S(2)}) collective-permute-start(bf16[256,1536]{1,0:T(8,128)(2,1)S(1)} %bitcast.43), channel_id=1, source_target_pairs={{0,1},{1,2},{2,3},{3,0},{4,5},{5,6},{6,7},{7,4},{8,9},{9,10},{10,1... | collective-permute-start | bytes 2359304 | tf_op jit(solution)/shard_map/ppermute | solution.py:30
  54.2 20.5 %collective-permute-start.7 = (bf16[256,1536]{1,0:T(8,128)(2,1)S(1)}, bf16[256,1536]{1,0:T(8,128)(2,1)}, u32[]{:S(2)}, u32[]{:S(2)}) collective-permute-start(bf16[256,1536]{1,0:T(8,128)(2,1)S(1)} %bitcast.44), channel_id=1, source_target_pairs={{0,3},{1,0},{2,1},{3,2},{4,7},{5,4},{6,5},{7,6},{8,11},{9,8},{10,9... | collective-permute-start | bytes 2359304 | tf_op jit(solution)/shard_map/ppermute | solution.py:30
  99.6 87.1 %all-to-all-start.2 = ((bf16[8,128,1536]{2,1,0:T(8,128)(2,1)}), bf16[8,128,1536]{2,1,0:T(8,128)(2,1)}, u32[]{:S(2)}, u32[]{:S(2)}) async-start(bf16[8,128,1536]{2,1,0:T(8,128)(2,1)} %bitcast.42), calls=%async_computation.2 | async-start | bytes 6291456 | tf_op jit(solution)/shard_map/all_to_all | solution.py:35
  106.6 33.5 %collective-permute-start.9 = (bf16[256,1536]{1,0:T(8,128)(2,1)}, bf16[256,1536]{1,0:T(8,128)(2,1)S(1)}, u32[]{:S(2)}, u32[]{:S(2)}) collective-permute-start(bf16[256,1536]{1,0:T(8,128)(2,1)} %bitcast.13.refs_0_), channel_id=1, source_target_pairs={{0,3},{1,0},{2,1},{3,2},{4,7},{5,4},{6,5},{7,6},{8,11},{9,8},{10,9... | collective-permute-start | bytes 2359304 | tf_op jit(solution)/shard_map/ppermute | solution.py:30
  109.5 30.6 %collective-permute-start.8 = (bf16[256,1536]{1,0:T(8,128)(2,1)}, bf16[256,1536]{1,0:T(8,128)(2,1)S(1)}, u32[]{:S(2)}, u32[]{:S(2)}) collective-permute-start(bf16[256,1536]{1,0:T(8,128)(2,1)} %bitcast.13.refs_0_), channel_id=1, source_target_pairs={{0,1},{1,2},{2,3},{3,0},{4,5},{5,6},{6,7},{7,4},{8,9},{9,10},{10,1... | collective-permute-start | bytes 2359304 | tf_op jit(solution)/shard_map/ppermute | solution.py:30
  109.5 27.0 %collective-permute-start.10 = (bf16[128,1536]{1,0:T(8,128)(2,1)}, bf16[128,1536]{1,0:T(8,128)(2,1)S(1)}, u32[]{:S(2)}, u32[]{:S(2)}) collective-permute-start(bf16[128,1536]{1,0:T(8,128)(2,1)} %get-tuple-element.62), channel_id=1, source_target_pairs={{0,1},{1,2},{2,3},{3,0},{4,5},{5,6},{6,7},{7,4},{8,9},{9,10},{10,1... | collective-permute-start | bytes 1179656 | tf_op jit(solution)/shard_map/ppermute | solution.py:30
  109.5 27.0 %collective-permute-start.11 = (bf16[128,1536]{1,0:T(8,128)(2,1)}, bf16[128,1536]{1,0:T(8,128)(2,1)S(1)}, u32[]{:S(2)}, u32[]{:S(2)}) collective-permute-start(bf16[128,1536]{1,0:T(8,128)(2,1)} %get-tuple-element.65), channel_id=1, source_target_pairs={{0,3},{1,0},{2,1},{3,2},{4,7},{5,4},{6,5},{7,6},{8,11},{9,8},{10,9... | collective-permute-start | bytes 1179656 | tf_op jit(solution)/shard_map/ppermute | solution.py:30
  139.8 14.4 %collective-permute-start.15 = (bf16[128,1536]{1,0:T(8,128)(2,1)S(1)}, bf16[128,1536]{1,0:T(8,128)(2,1)S(1)}, u32[]{:S(2)}, u32[]{:S(2)}) collective-permute-start(bf16[128,1536]{1,0:T(8,128)(2,1)S(1)} %get-tuple-element.73), channel_id=1, source_target_pairs={{0,3},{1,0},{2,1},{3,2},{4,7},{5,4},{6,5},{7,6},{8,11},{9,8},{10,9... | collective-permute-start | bytes 1179656 | tf_op jit(solution)/shard_map/ppermute | solution.py:30
  140.5 13.6 %collective-permute-start.13 = (bf16[128,1536]{1,0:T(8,128)(2,1)S(1)}, bf16[128,1536]{1,0:T(8,128)(2,1)S(1)}, u32[]{:S(2)}, u32[]{:S(2)}) collective-permute-start(bf16[128,1536]{1,0:T(8,128)(2,1)S(1)} %get-tuple-element.54), channel_id=1, source_target_pairs={{0,1},{1,2},{2,3},{3,0},{4,5},{5,6},{6,7},{7,4},{8,9},{9,10},{10,1... | collective-permute-start | bytes 1179656 | tf_op jit(solution)/shard_map/ppermute | solution.py:30
  142.3 13.8 %collective-permute-start.14 = (bf16[128,1536]{1,0:T(8,128)(2,1)S(1)}, bf16[128,1536]{1,0:T(8,128)(2,1)S(1)}, u32[]{:S(2)}, u32[]{:S(2)}) collective-permute-start(bf16[128,1536]{1,0:T(8,128)(2,1)S(1)} %get-tuple-element.55), channel_id=1, source_target_pairs={{0,3},{1,0},{2,1},{3,2},{4,7},{5,4},{6,5},{7,6},{8,11},{9,8},{10,9... | collective-permute-start | bytes 1179656 | tf_op jit(solution)/shard_map/ppermute | solution.py:30
  143.8 14.3 %collective-permute-start.12 = (bf16[128,1536]{1,0:T(8,128)(2,1)S(1)}, bf16[128,1536]{1,0:T(8,128)(2,1)S(1)}, u32[]{:S(2)}, u32[]{:S(2)}) collective-permute-start(bf16[128,1536]{1,0:T(8,128)(2,1)S(1)} %get-tuple-element.66), channel_id=1, source_target_pairs={{0,1},{1,2},{2,3},{3,0},{4,5},{5,6},{6,7},{7,4},{8,9},{9,10},{10,1... | collective-permute-start | bytes 1179656 | tf_op jit(solution)/shard_map/ppermute | solution.py:30
  158.1 26.6 %collective-permute-start.21 = (bf16[256,1536]{1,0:T(8,128)(2,1)S(1)}, bf16[256,1536]{1,0:T(8,128)(2,1)S(1)}, u32[]{:S(2)}, u32[]{:S(2)}) collective-permute-start(bf16[256,1536]{1,0:T(8,128)(2,1)S(1)} %shard_map.160), channel_id=1, source_target_pairs={{0,3},{1,0},{2,1},{3,2},{4,7},{5,4},{6,5},{7,6},{8,11},{9,8},{10,9... | collective-permute-start | bytes 2359304 | tf_op jit(solution)/shard_map/ppermute | solution.py:30
  158.6 26.1 %collective-permute-start.20 = (bf16[256,1536]{1,0:T(8,128)(2,1)S(1)}, bf16[256,1536]{1,0:T(8,128)(2,1)S(1)}, u32[]{:S(2)}, u32[]{:S(2)}) collective-permute-start(bf16[256,1536]{1,0:T(8,128)(2,1)S(1)} %shard_map.159), channel_id=1, source_target_pairs={{0,1},{1,2},{2,3},{3,0},{4,5},{5,6},{6,7},{7,4},{8,9},{9,10},{10,1... | collective-permute-start | bytes 2359304 | tf_op jit(solution)/shard_map/ppermute | solution.py:30
  165.2 18.9 %collective-permute-start.16 = (bf16[128,1536]{1,0:T(8,128)(2,1)S(1)}, bf16[128,1536]{1,0:T(8,128)(2,1)S(1)}, u32[]{:S(2)}, u32[]{:S(2)}) collective-permute-start(bf16[128,1536]{1,0:T(8,128)(2,1)S(1)} %get-tuple-element.79), channel_id=1, source_target_pairs={{0,1},{1,2},{2,3},{3,0},{4,5},{5,6},{6,7},{7,4},{8,9},{9,10},{10,1... | collective-permute-start | bytes 1179656 | tf_op jit(solution)/shard_map/ppermute | solution.py:30
  165.5 18.8 %collective-permute-start.18 = (bf16[128,1536]{1,0:T(8,128)(2,1)S(1)}, bf16[128,1536]{1,0:T(8,128)(2,1)S(1)}, u32[]{:S(2)}, u32[]{:S(2)}) collective-permute-start(bf16[128,1536]{1,0:T(8,128)(2,1)S(1)} %get-tuple-element.86), channel_id=1, source_target_pairs={{0,3},{1,0},{2,1},{3,2},{4,7},{5,4},{6,5},{7,6},{8,11},{9,8},{10,9... | collective-permute-start | bytes 1179656 | tf_op jit(solution)/shard_map/ppermute | solution.py:30
  186.8 24.5 %all-to-all-start.3 = ((bf16[8,32,1536]{2,1,0:T(8,128)(2,1)}), bf16[8,32,1536]{2,1,0:T(8,128)(2,1)}, u32[]{:S(2)}, u32[]{:S(2)}) async-start(bf16[8,32,1536]{2,1,0:T(8,128)(2,1)} %bitcast.18), calls=%async_computation.3 | async-start | bytes 1572864 | tf_op jit(solution)/shard_map/all_to_all | solution.py:35
  193.1 15.4 %collective-permute-start.17 = (bf16[256,1536]{1,0:T(8,128)(2,1)}, bf16[256,1536]{1,0:T(8,128)(2,1)S(1)}, u32[]{:S(2)}, u32[]{:S(2)}) collective-permute-start(bf16[256,1536]{1,0:T(8,128)(2,1)} %copy-done.30), channel_id=1, source_target_pairs={{0,1},{1,2},{2,3},{3,0},{4,5},{5,6},{6,7},{7,4},{8,9},{9,10},{10,1... | collective-permute-start | bytes 2359304 | tf_op jit(solution)/shard_map/ppermute | solution.py:30
  193.4 15.1 %collective-permute-start.19 = (bf16[256,1536]{1,0:T(8,128)(2,1)}, bf16[256,1536]{1,0:T(8,128)(2,1)S(1)}, u32[]{:S(2)}, u32[]{:S(2)}) collective-permute-start(bf16[256,1536]{1,0:T(8,128)(2,1)} %copy-done.29), channel_id=1, source_target_pairs={{0,3},{1,0},{2,1},{3,2},{4,7},{5,4},{6,5},{7,6},{8,11},{9,8},{10,9... | collective-permute-start | bytes 2359304 | tf_op jit(solution)/shard_map/ppermute | solution.py:30
  211.3 22.4 %all-to-all-start.4 = ((bf16[8,32,1536]{2,1,0:T(8,128)(2,1)}), bf16[8,32,1536]{2,1,0:T(8,128)(2,1)S(1)}, u32[]{:S(2)}, u32[]{:S(2)}) async-start(bf16[8,32,1536]{2,1,0:T(8,128)(2,1)} %bitcast.20), calls=%async_computation.4 | async-start | bytes 1572864 | tf_op jit(solution)/shard_map/all_to_all | solution.py:35
  (48 other events, 392.4 us)

commit v3 on v2

--- a/solution.py
+++ b/solution.py
@@ -171,7 +171,7 @@
         [left, right],
         0,
         in_specs=[anywhere] * 2,
-        out_specs=[anywhere] * 2,
+        out_specs=[pl.BlockSpec(memory_space=pltpu.VMEM)] * 2,
         scratch_shapes=[pltpu.SemaphoreType.DMA((2,))],
     )
 

time: 236 us -> 215 us (0.911)
  Pallas kernels: 68 us -> 45.6 us
    pallas_call x23, Pallas kernels: 68 us -> 45.6 us  [call(): pl.pallas_call(kernel, out_shape=out_shapes, cost_estimate=pl.CostEstimat...]
  transfers between devices with their start and end apart: 27 -> 27, of which waited for: 12 -> 13; matrix products, arithmetic and copies ran while one was open for 1% -> 2% of each run, Pallas kernels for 28% -> 20%
where the time goes in v3:
time: 215 us; the launch traced here: 213 us
  waiting for transfers between devices  79.3 us (37%)
  starting transfers between devices  64.5 us (30%)
  Pallas kernels  45.6 us (21%)
  local copies, waits for them, and re-layouts  23 us (11%)
    ppermute x20, waiting for transfers between devices, turned(): return lax.ppermute(block, 'expert', route)  64.5 us
    pallas_call x23, Pallas kernels, call(): pl.pallas_call(kernel, out_shape=out_shapes, cost_estimate=pl.CostEstimat...  45.6 us
    all_to_all x5, starting transfers between devices, exchange(): lax.all_to_all(block, 'expert', split_axis=0, concat_axis=0, tiled=True,...  33.4 us
    ppermute x20, starting transfers between devices, turned(): return lax.ppermute(block, 'expert', route)  28.8 us
    unnamed x95, local copies, waits for them, and re-layouts  23 us
    all_to_all x5, waiting for transfers between devices, exchange(): lax.all_to_all(block, 'expert', split_axis=0, concat_axis=0, tiled=True,...  14.3 us
  transfers between devices with their start and end apart: 27, of which 13 were waited for; matrix products, arithmetic and copies ran while one was open for 2% of the time, Pallas kernels for 20%

profile of v3, /device:TPU:6, one launch (start us, length us, event | category | flops | bytes accessed | tf_op | source)
XLA Modules:
  0.0 213.5 jit_solution(10615157165062689557)
XLA Ops:
  8.1 8.6 %all-to-all-start = ((bf16[8,32,1536]{2,1,0:T(8,128)(2,1)}), bf16[8,32,1536]{2,1,0:T(8,128)(2,1)S(1)}, u32[]{:S(2)}, u32[]{:S(2)}) async-start(bf16[8,32,1536]{2,1,0:T(8,128)(2,1)} %bitcast.48), calls=%async_computation | async-start | bytes 1572864 | tf_op jit(solution)/shard_map/all_to_all | solution.py:35
  16.7 3.0 %collective-permute-start.3 = (bf16[128,1664]{1,0:T(8,128)(2,1)}, bf16[128,1664]{1,0:T(8,128)(2,1)S(1)}, u32[]{:S(2)}, u32[]{:S(2)}) collective-permute-start(bf16[128,1664]{1,0:T(8,128)(2,1)} %copy-done.11), channel_id=1, source_target_pairs={{0,3},{1,0},{2,1},{3,2},{4,7},{5,4},{6,5},{7,6},{8,11},{9,8},{10,9... | collective-permute-start | bytes 1277960 | tf_op jit(solution)/shard_map/ppermute | solution.py:30
  21.8 7.1 %collective-permute-done.3.right_ref = bf16[128,1664]{1,0:T(8,128)(2,1)S(1)} collective-permute-done((bf16[128,1664]{1,0:T(8,128)(2,1)}, bf16[128,1664]{1,0:T(8,128)(2,1)S(1)}, u32[]{:S(2)}, u32[]{:S(2)}) %collective-permute-start.3) | collective-permute-done | bytes 426016 | tf_op jit(solution)/shard_map/ppermute | solution.py:30
  28.9 3.9 %collective-permute-done.2.left_ref = bf16[128,1664]{1,0:T(8,128)(2,1)S(1)} collective-permute-done((bf16[128,1664]{1,0:T(8,128)(2,1)}, bf16[128,1664]{1,0:T(8,128)(2,1)S(1)}, u32[]{:S(2)}, u32[]{:S(2)}) %collective-permute-start.2) | collective-permute-done | bytes 426016 | tf_op jit(solution)/shard_map/ppermute | solution.py:30
  34.9 3.2 %collective-permute-start.5 = (bf16[64,1664]{1,0:T(8,128)(2,1)}, bf16[64,1664]{1,0:T(8,128)(2,1)}, u32[]{:S(2)}, u32[]{:S(2)}) collective-permute-start(bf16[64,1664]{1,0:T(8,128)(2,1)} %get-tuple-element.49), channel_id=1, source_target_pairs={{0,3},{1,0},{2,1},{3,2},{4,7},{5,4},{6,5},{7,6},{8,11},{9,8},{10,9... | collective-permute-start | bytes 638984 | tf_op jit(solution)/shard_map/ppermute | solution.py:30
  38.9 5.6 %collective-permute-done.4.top_ref = bf16[64,1664]{1,0:T(8,128)(2,1)} collective-permute-done((bf16[64,1664]{1,0:T(8,128)(2,1)}, bf16[64,1664]{1,0:T(8,128)(2,1)}, u32[]{:S(2)}, u32[]{:S(2)}) %collective-permute-start.4) | collective-permute-done | bytes 213024 | tf_op jit(solution)/shard_map/ppermute | solution.py:30
  47.1 7.5 %all-to-all-start.1 = ((bf16[8,32,1536]{2,1,0:T(8,128)(2,1)}), bf16[8,32,1536]{2,1,0:T(8,128)(2,1)}, u32[]{:S(2)}, u32[]{:S(2)}) async-start(bf16[8,32,1536]{2,1,0:T(8,128)(2,1)} %bitcast.47), calls=%async_computation.1 | async-start | bytes 1572864 | tf_op jit(solution)/shard_map/all_to_all | solution.py:35
  54.6 3.2 %collective-permute-start.7 = (bf16[256,1536]{1,0:T(8,128)(2,1)S(1)}, bf16[256,1536]{1,0:T(8,128)(2,1)}, u32[]{:S(2)}, u32[]{:S(2)}) collective-permute-start(bf16[256,1536]{1,0:T(8,128)(2,1)S(1)} %bitcast.44), channel_id=1, source_target_pairs={{0,3},{1,0},{2,1},{3,2},{4,7},{5,4},{6,5},{7,6},{8,11},{9,8},{10,9... | collective-permute-start | bytes 2359304 | tf_op jit(solution)/shard_map/ppermute | solution.py:30
  68.9 6.3 %collective-permute-done.6.refs_0_.left_ref.refs_5_ = bf16[256,1536]{1,0:T(8,128)(2,1)} collective-permute-done((bf16[256,1536]{1,0:T(8,128)(2,1)S(1)}, bf16[256,1536]{1,0:T(8,128)(2,1)}, u32[]{:S(2)}, u32[]{:S(2)}) %collective-permute-start.6) | collective-permute-done | bytes 786464 | tf_op jit(solution)/shard_map/ppermute | solution.py:30
  78.0 6.1 %all-to-all-start.2 = ((bf16[8,128,1536]{2,1,0:T(8,128)(2,1)}), bf16[8,128,1536]{2,1,0:T(8,128)(2,1)}, u32[]{:S(2)}, u32[]{:S(2)}) async-start(bf16[8,128,1536]{2,1,0:T(8,128)(2,1)} %bitcast.42), calls=%async_computation.2 | async-start | bytes 6291456 | tf_op jit(solution)/shard_map/all_to_all | solution.py:35
  84.1 3.0 %collective-permute-start.9 = (bf16[256,1536]{1,0:T(8,128)(2,1)}, bf16[256,1536]{1,0:T(8,128)(2,1)S(1)}, u32[]{:S(2)}, u32[]{:S(2)}) collective-permute-start(bf16[256,1536]{1,0:T(8,128)(2,1)} %bitcast.13.refs_0_), channel_id=1, source_target_pairs={{0,3},{1,0},{2,1},{3,2},{4,7},{5,4},{6,5},{7,6},{8,11},{9,8},{10,9... | collective-permute-start | bytes 2359304 | tf_op jit(solution)/shard_map/ppermute | solution.py:30
  87.0 3.3 %collective-permute-start.11 = (bf16[128,1536]{1,0:T(8,128)(2,1)}, bf16[128,1536]{1,0:T(8,128)(2,1)S(1)}, u32[]{:S(2)}, u32[]{:S(2)}) collective-permute-start(bf16[128,1536]{1,0:T(8,128)(2,1)} %get-tuple-element.65), channel_id=1, source_target_pairs={{0,3},{1,0},{2,1},{3,2},{4,7},{5,4},{6,5},{7,6},{8,11},{9,8},{10,9... | collective-permute-start | bytes 1179656 | tf_op jit(solution)/shard_map/ppermute | solution.py:30
  93.4 4.7 %shard_map.153 = (bf16[256,768]{1,0:T(8,128)(2,1)S(1)}, bf16[256,768]{1,0:T(8,128)(2,1)S(1)}, bf16[256,768]{1,0:T(8,128)(2,1)S(1)}, bf16[256,768]{1,0:T(8,128)(2...) custom-call(s32[1]{0:T(128)} %bitcast.14.place_ref, bf16[1536,768]{1,0:T(8,128)(2,1)S(1)} %bitcast.27, ...), custom_call_target="tpu_custom_call" | custom-call | flops 2415919104 | bytes 12582916 | tf_op jit(solution)/shard_map/pallas_call | solution.py:69
  98.1 16.2 %collective-permute-done.10.refs_0_.refs_7_ = bf16[128,1536]{1,0:T(8,128)(2,1)S(1)} collective-permute-done((bf16[128,1536]{1,0:T(8,128)(2,1)}, bf16[128,1536]{1,0:T(8,128)(2,1)S(1)}, u32[]{:S(2)}, u32[]{:S(2)}) %collective-permute-start.10) | collective-permute-done | bytes 393248 | tf_op jit(solution)/shard_map/ppermute | solution.py:30
  114.3 3.2 %shard_map.157 = (bf16[256,768]{1,0:T(8,128)(2,1)S(1)}, bf16[256,768]{1,0:T(8,128)(2,1)S(1)}, bf16[128,1536]{1,0:T(8,128)(2,1)S(1)}, bf16[128,1536]{1,0:T(8,128)(2,1)S(1)}) custom-call(s32[1]{0:T(128)} %bitcast.14.place_ref, bf16[1536,768]{1,0:T(8,128)(2,1)S(1)} %bitcast.28, bf16[768,1536]{1,0:T(8,128)(2,1)S(1)} %bitcast.34, ...), custom_call_target="tpu_custom_call" | custom-call | flops 1207959552 | bytes 8650756 | tf_op jit(solution)/shard_map/pallas_call | solution.py:69
  126.0 6.0 %shard_map.158 = bf16[768,1536]{1,0:T(8,128)(2,1)} custom-call(bf16[256,768]{1,0:T(8,128)(2,1)S(1)} %copy-done.42, bf16[256,768]{1,0:T(8,128)(2,1)S(1)} %get-tuple-element.68.refs_1_, bf16[256,768]{1,0:T(8,128)(2,1)S(1)} %get-tuple-element.69.refs_2_, bf16[256,768]{1,0:T(8,128)(2,1)S(1)} %get-tuple-element.70.refs_3_, bf16[256,1536]{1,0:T(8,128)(2,1)S(1)} %bitcast.46, ...), custom_call_target="tpu_custom_call" | custom-call | flops 2415919104 | bytes 7077888 | tf_op jit(solution)/shard_map/pallas_call | solution.py:69
  138.9 3.0 %shard_map.161 = (bf16[256,1536]{1,0:T(8,128)(2,1)S(1)}, bf16[256,1536]{1,0:T(8,128)(2,1)S(1)}) custom-call(bf16[1536,768]{1,0:T(8,128)(2,1)S(1)} %bitcast.30, bf16[768,1536]{1,0:T(8,128)(2,1)S(1)} %bitcast.36, bf16[256,1536]{1,0:T(8,128)(2,1)S(1)} %collective-permute-done.8.left_ref.refs_0_, bf16[256,1536]{1,0:T(8,128)(2,1)S(1)} %collective-permute-done.9.right_ref.refs_1_), custom_call_target="tpu_custom_call" | custom-call | flops 2415919104 | bytes 7864320 | tf_op jit(solution)/shard_map/pallas_call | solution.py:69
  143.7 3.0 %collective-permute-start.18 = (bf16[128,1536]{1,0:T(8,128)(2,1)S(1)}, bf16[128,1536]{1,0:T(8,128)(2,1)S(1)}, u32[]{:S(2)}, u32[]{:S(2)}) collective-permute-start(bf16[128,1536]{1,0:T(8,128)(2,1)S(1)} %get-tuple-element.86), channel_id=1, source_target_pairs={{0,3},{1,0},{2,1},{3,2},{4,7},{5,4},{6,5},{7,6},{8,11},{9,8},{10,9... | collective-permute-start | bytes 1179656 | tf_op jit(solution)/shard_map/ppermute | solution.py:30
  146.6 15.9 %collective-permute-done.16.more_ref = bf16[128,1536]{1,0:T(8,128)(2,1)S(1)} collective-permute-done((bf16[128,1536]{1,0:T(8,128)(2,1)S(1)}, bf16[128,1536]{1,0:T(8,128)(2,1)S(1)}, u32[]{:S(2)}, u32[]{:S(2)}) %collective-permute-start.16) | collective-permute-done | bytes 393248 | tf_op jit(solution)/shard_map/ppermute | solution.py:30
  165.2 5.8 %all-to-all-start.3 = ((bf16[8,32,1536]{2,1,0:T(8,128)(2,1)}), bf16[8,32,1536]{2,1,0:T(8,128)(2,1)}, u32[]{:S(2)}, u32[]{:S(2)}) async-start(bf16[8,32,1536]{2,1,0:T(8,128)(2,1)} %bitcast.18), calls=%async_computation.3 | async-start | bytes 1572864 | tf_op jit(solution)/shard_map/all_to_all | solution.py:35
  174.3 6.8 %shard_map.164 = bf16[1536,768]{1,0:T(8,128)(2,1)} custom-call(bf16[8,4,32,1536]{3,2,1,0:T(8,128)(2,1)} %bitcast.17.rows_ref, bf16[256,768]{1,0:T(8,128)(2,1)S(1)} %copy-done.36, bf16[256,768]{1,0:T(8,128)(2,1)S(1)} %get-tuple-element.82.refs_1_, bf16[256,768]{1,0:T(8,128)(2,1)S(1)} %copy-done.38, bf16[256,768]{1,0:T(8,128)(2,1)S(1)} %copy-done.40), custom_call_target="tpu_custom_call" | custom-call | flops 2415919104 | bytes 7077888 | tf_op jit(solution)/shard_map/pallas_call | solution.py:69
  181.1 5.5 %collective-permute-done.17.two_ref = bf16[256,1536]{1,0:T(8,128)(2,1)S(1)} collective-permute-done((bf16[256,1536]{1,0:T(8,128)(2,1)}, bf16[256,1536]{1,0:T(8,128)(2,1)S(1)}, u32[]{:S(2)}, u32[]{:S(2)}) %collective-permute-start.17) | collective-permute-done | bytes 786464 | tf_op jit(solution)/shard_map/ppermute | solution.py:30
  189.5 5.4 %all-to-all-start.4 = ((bf16[8,32,1536]{2,1,0:T(8,128)(2,1)}), bf16[8,32,1536]{2,1,0:T(8,128)(2,1)S(1)}, u32[]{:S(2)}, u32[]{:S(2)}) async-start(bf16[8,32,1536]{2,1,0:T(8,128)(2,1)} %bitcast.20), calls=%async_computation.4 | async-start | bytes 1572864 | tf_op jit(solution)/shard_map/all_to_all | solution.py:35
  200.1 11.8 %all-to-all-done.4 = bf16[8,32,1536]{2,1,0:T(8,128)(2,1)S(1)} async-done(((bf16[8,32,1536]{2,1,0:T(8,128)(2,1)}), bf16[8,32,1536]{2,1,0:T(8,128)(2,1)S(1)}, u32[]{:S(2)}, u32[]{:S(2)}) %all-to-all-start.4) | async-done | bytes 786464 | tf_op jit(solution)/shard_map/all_to_all | solution.py:35
  (148 shorter events, 64.3 us)
Async XLA Ops:
  8.1 39.0 %all-to-all-start = ((bf16[8,32,1536]{2,1,0:T(8,128)(2,1)}), bf16[8,32,1536]{2,1,0:T(8,128)(2,1)S(1)}, u32[]{:S(2)}, u32[]{:S(2)}) async-start(bf16[8,32,1536]{2,1,0:T(8,128)(2,1)} %bitcast.48), calls=%async_computation | async-start | bytes 1572864 | tf_op jit(solution)/shard_map/all_to_all | solution.py:35
  16.7 12.2 %collective-permute-start.3 = (bf16[128,1664]{1,0:T(8,128)(2,1)}, bf16[128,1664]{1,0:T(8,128)(2,1)S(1)}, u32[]{:S(2)}, u32[]{:S(2)}) collective-permute-start(bf16[128,1664]{1,0:T(8,128)(2,1)} %copy-done.11), channel_id=1, source_target_pairs={{0,3},{1,0},{2,1},{3,2},{4,7},{5,4},{6,5},{7,6},{8,11},{9,8},{10,9... | collective-permute-start | bytes 1277960 | tf_op jit(solution)/shard_map/ppermute | solution.py:30
  19.8 13.1 %collective-permute-start.2 = (bf16[128,1664]{1,0:T(8,128)(2,1)}, bf16[128,1664]{1,0:T(8,128)(2,1)S(1)}, u32[]{:S(2)}, u32[]{:S(2)}) collective-permute-start(bf16[128,1664]{1,0:T(8,128)(2,1)} %copy-done.11), channel_id=1, source_target_pairs={{0,1},{1,2},{2,3},{3,0},{4,5},{5,6},{6,7},{7,4},{8,9},{9,10},{10,1... | collective-permute-start | bytes 1277960 | tf_op jit(solution)/shard_map/ppermute | solution.py:30
  19.8 24.7 %collective-permute-start.1 = (bf16[1,128,1536]{2,1,0:T(8,128)(2,1)}, bf16[1,128,1536]{2,1,0:T(8,128)(2,1)S(1)}, u32[]{:S(2)}, u32[]{:S(2)}) collective-permute-start(bf16[1,128,1536]{2,1,0:T(8,128)(2,1)} %param.12), channel_id=1, source_target_pairs={{224,0},{0,32},{32,64},{64,96},{96,128},{128,160},{160,192},{192,2... | collective-permute-start | bytes 1179656 | tf_op jit(solution)/shard_map/ppermute | solution.py:21
  47.1 30.9 %all-to-all-start.1 = ((bf16[8,32,1536]{2,1,0:T(8,128)(2,1)}), bf16[8,32,1536]{2,1,0:T(8,128)(2,1)}, u32[]{:S(2)}, u32[]{:S(2)}) async-start(bf16[8,32,1536]{2,1,0:T(8,128)(2,1)} %bitcast.47), calls=%async_computation.1 | async-start | bytes 1572864 | tf_op jit(solution)/shard_map/all_to_all | solution.py:35
  54.6 20.5 %collective-permute-start.6 = (bf16[256,1536]{1,0:T(8,128)(2,1)S(1)}, bf16[256,1536]{1,0:T(8,128)(2,1)}, u32[]{:S(2)}, u32[]{:S(2)}) collective-permute-start(bf16[256,1536]{1,0:T(8,128)(2,1)S(1)} %bitcast.43), channel_id=1, source_target_pairs={{0,1},{1,2},{2,3},{3,0},{4,5},{5,6},{6,7},{7,4},{8,9},{9,10},{10,1... | collective-permute-start | bytes 2359304 | tf_op jit(solution)/shard_map/ppermute | solution.py:30
  54.6 20.5 %collective-permute-start.7 = (bf16[256,1536]{1,0:T(8,128)(2,1)S(1)}, bf16[256,1536]{1,0:T(8,128)(2,1)}, u32[]{:S(2)}, u32[]{:S(2)}) collective-permute-start(bf16[256,1536]{1,0:T(8,128)(2,1)S(1)} %bitcast.44), channel_id=1, source_target_pairs={{0,3},{1,0},{2,1},{3,2},{4,7},{5,4},{6,5},{7,6},{8,11},{9,8},{10,9... | collective-permute-start | bytes 2359304 | tf_op jit(solution)/shard_map/ppermute | solution.py:30
  78.0 87.2 %all-to-all-start.2 = ((bf16[8,128,1536]{2,1,0:T(8,128)(2,1)}), bf16[8,128,1536]{2,1,0:T(8,128)(2,1)}, u32[]{:S(2)}, u32[]{:S(2)}) async-start(bf16[8,128,1536]{2,1,0:T(8,128)(2,1)} %bitcast.42), calls=%async_computation.2 | async-start | bytes 6291456 | tf_op jit(solution)/shard_map/all_to_all | solution.py:35
  84.1 33.9 %collective-permute-start.9 = (bf16[256,1536]{1,0:T(8,128)(2,1)}, bf16[256,1536]{1,0:T(8,128)(2,1)S(1)}, u32[]{:S(2)}, u32[]{:S(2)}) collective-permute-start(bf16[256,1536]{1,0:T(8,128)(2,1)} %bitcast.13.refs_0_), channel_id=1, source_target_pairs={{0,3},{1,0},{2,1},{3,2},{4,7},{5,4},{6,5},{7,6},{8,11},{9,8},{10,9... | collective-permute-start | bytes 2359304 | tf_op jit(solution)/shard_map/ppermute | solution.py:30
  87.0 30.9 %collective-permute-start.8 = (bf16[256,1536]{1,0:T(8,128)(2,1)}, bf16[256,1536]{1,0:T(8,128)(2,1)S(1)}, u32[]{:S(2)}, u32[]{:S(2)}) collective-permute-start(bf16[256,1536]{1,0:T(8,128)(2,1)} %bitcast.13.refs_0_), channel_id=1, source_target_pairs={{0,1},{1,2},{2,3},{3,0},{4,5},{5,6},{6,7},{7,4},{8,9},{9,10},{10,1... | collective-permute-start | bytes 2359304 | tf_op jit(solution)/shard_map/ppermute | solution.py:30
  87.0 27.3 %collective-permute-start.10 = (bf16[128,1536]{1,0:T(8,128)(2,1)}, bf16[128,1536]{1,0:T(8,128)(2,1)S(1)}, u32[]{:S(2)}, u32[]{:S(2)}) collective-permute-start(bf16[128,1536]{1,0:T(8,128)(2,1)} %get-tuple-element.62), channel_id=1, source_target_pairs={{0,1},{1,2},{2,3},{3,0},{4,5},{5,6},{6,7},{7,4},{8,9},{9,10},{10,1... | collective-permute-start | bytes 1179656 | tf_op jit(solution)/shard_map/ppermute | solution.py:30
  87.0 27.3 %collective-permute-start.11 = (bf16[128,1536]{1,0:T(8,128)(2,1)}, bf16[128,1536]{1,0:T(8,128)(2,1)S(1)}, u32[]{:S(2)}, u32[]{:S(2)}) collective-permute-start(bf16[128,1536]{1,0:T(8,128)(2,1)} %get-tuple-element.65), channel_id=1, source_target_pairs={{0,3},{1,0},{2,1},{3,2},{4,7},{5,4},{6,5},{7,6},{8,11},{9,8},{10,9... | collective-permute-start | bytes 1179656 | tf_op jit(solution)/shard_map/ppermute | solution.py:30
  117.6 14.4 %collective-permute-start.15 = (bf16[128,1536]{1,0:T(8,128)(2,1)S(1)}, bf16[128,1536]{1,0:T(8,128)(2,1)S(1)}, u32[]{:S(2)}, u32[]{:S(2)}) collective-permute-start(bf16[128,1536]{1,0:T(8,128)(2,1)S(1)} %get-tuple-element.73), channel_id=1, source_target_pairs={{0,3},{1,0},{2,1},{3,2},{4,7},{5,4},{6,5},{7,6},{8,11},{9,8},{10,9... | collective-permute-start | bytes 1179656 | tf_op jit(solution)/shard_map/ppermute | solution.py:30
  118.3 13.6 %collective-permute-start.13 = (bf16[128,1536]{1,0:T(8,128)(2,1)S(1)}, bf16[128,1536]{1,0:T(8,128)(2,1)S(1)}, u32[]{:S(2)}, u32[]{:S(2)}) collective-permute-start(bf16[128,1536]{1,0:T(8,128)(2,1)S(1)} %get-tuple-element.54), channel_id=1, source_target_pairs={{0,1},{1,2},{2,3},{3,0},{4,5},{5,6},{6,7},{7,4},{8,9},{9,10},{10,1... | collective-permute-start | bytes 1179656 | tf_op jit(solution)/shard_map/ppermute | solution.py:30
  120.2 14.1 %collective-permute-start.14 = (bf16[128,1536]{1,0:T(8,128)(2,1)S(1)}, bf16[128,1536]{1,0:T(8,128)(2,1)S(1)}, u32[]{:S(2)}, u32[]{:S(2)}) collective-permute-start(bf16[128,1536]{1,0:T(8,128)(2,1)S(1)} %get-tuple-element.55), channel_id=1, source_target_pairs={{0,3},{1,0},{2,1},{3,2},{4,7},{5,4},{6,5},{7,6},{8,11},{9,8},{10,9... | collective-permute-start | bytes 1179656 | tf_op jit(solution)/shard_map/ppermute | solution.py:30
  121.6 14.6 %collective-permute-start.12 = (bf16[128,1536]{1,0:T(8,128)(2,1)S(1)}, bf16[128,1536]{1,0:T(8,128)(2,1)S(1)}, u32[]{:S(2)}, u32[]{:S(2)}) collective-permute-start(bf16[128,1536]{1,0:T(8,128)(2,1)S(1)} %get-tuple-element.66), channel_id=1, source_target_pairs={{0,1},{1,2},{2,3},{3,0},{4,5},{5,6},{6,7},{7,4},{8,9},{9,10},{10,1... | collective-permute-start | bytes 1179656 | tf_op jit(solution)/shard_map/ppermute | solution.py:30
  136.3 26.9 %collective-permute-start.21 = (bf16[256,1536]{1,0:T(8,128)(2,1)S(1)}, bf16[256,1536]{1,0:T(8,128)(2,1)S(1)}, u32[]{:S(2)}, u32[]{:S(2)}) collective-permute-start(bf16[256,1536]{1,0:T(8,128)(2,1)S(1)} %shard_map.160), channel_id=1, source_target_pairs={{0,3},{1,0},{2,1},{3,2},{4,7},{5,4},{6,5},{7,6},{8,11},{9,8},{10,9... | collective-permute-start | bytes 2359304 | tf_op jit(solution)/shard_map/ppermute | solution.py:30
  136.8 26.4 %collective-permute-start.20 = (bf16[256,1536]{1,0:T(8,128)(2,1)S(1)}, bf16[256,1536]{1,0:T(8,128)(2,1)S(1)}, u32[]{:S(2)}, u32[]{:S(2)}) collective-permute-start(bf16[256,1536]{1,0:T(8,128)(2,1)S(1)} %shard_map.159), channel_id=1, source_target_pairs={{0,1},{1,2},{2,3},{3,0},{4,5},{5,6},{6,7},{7,4},{8,9},{9,10},{10,1... | collective-permute-start | bytes 2359304 | tf_op jit(solution)/shard_map/ppermute | solution.py:30
  143.3 19.2 %collective-permute-start.16 = (bf16[128,1536]{1,0:T(8,128)(2,1)S(1)}, bf16[128,1536]{1,0:T(8,128)(2,1)S(1)}, u32[]{:S(2)}, u32[]{:S(2)}) collective-permute-start(bf16[128,1536]{1,0:T(8,128)(2,1)S(1)} %get-tuple-element.79), channel_id=1, source_target_pairs={{0,1},{1,2},{2,3},{3,0},{4,5},{5,6},{6,7},{7,4},{8,9},{9,10},{10,1... | collective-permute-start | bytes 1179656 | tf_op jit(solution)/shard_map/ppermute | solution.py:30
  143.7 19.2 %collective-permute-start.18 = (bf16[128,1536]{1,0:T(8,128)(2,1)S(1)}, bf16[128,1536]{1,0:T(8,128)(2,1)S(1)}, u32[]{:S(2)}, u32[]{:S(2)}) collective-permute-start(bf16[128,1536]{1,0:T(8,128)(2,1)S(1)} %get-tuple-element.86), channel_id=1, source_target_pairs={{0,3},{1,0},{2,1},{3,2},{4,7},{5,4},{6,5},{7,6},{8,11},{9,8},{10,9... | collective-permute-start | bytes 1179656 | tf_op jit(solution)/shard_map/ppermute | solution.py:30
  165.2 24.3 %all-to-all-start.3 = ((bf16[8,32,1536]{2,1,0:T(8,128)(2,1)}), bf16[8,32,1536]{2,1,0:T(8,128)(2,1)}, u32[]{:S(2)}, u32[]{:S(2)}) async-start(bf16[8,32,1536]{2,1,0:T(8,128)(2,1)} %bitcast.18), calls=%async_computation.3 | async-start | bytes 1572864 | tf_op jit(solution)/shard_map/all_to_all | solution.py:35
  171.1 15.6 %collective-permute-start.17 = (bf16[256,1536]{1,0:T(8,128)(2,1)}, bf16[256,1536]{1,0:T(8,128)(2,1)S(1)}, u32[]{:S(2)}, u32[]{:S(2)}) collective-permute-start(bf16[256,1536]{1,0:T(8,128)(2,1)} %copy-done.30), channel_id=1, source_target_pairs={{0,1},{1,2},{2,3},{3,0},{4,5},{5,6},{6,7},{7,4},{8,9},{9,10},{10,1... | collective-permute-start | bytes 2359304 | tf_op jit(solution)/shard_map/ppermute | solution.py:30
  171.4 15.2 %collective-permute-start.19 = (bf16[256,1536]{1,0:T(8,128)(2,1)}, bf16[256,1536]{1,0:T(8,128)(2,1)S(1)}, u32[]{:S(2)}, u32[]{:S(2)}) collective-permute-start(bf16[256,1536]{1,0:T(8,128)(2,1)} %copy-done.29), channel_id=1, source_target_pairs={{0,3},{1,0},{2,1},{3,2},{4,7},{5,4},{6,5},{7,6},{8,11},{9,8},{10,9... | collective-permute-start | bytes 2359304 | tf_op jit(solution)/shard_map/ppermute | solution.py:30
  189.5 22.5 %all-to-all-start.4 = ((bf16[8,32,1536]{2,1,0:T(8,128)(2,1)}), bf16[8,32,1536]{2,1,0:T(8,128)(2,1)S(1)}, u32[]{:S(2)}, u32[]{:S(2)}) async-start(bf16[8,32,1536]{2,1,0:T(8,128)(2,1)} %bitcast.20), calls=%async_computation.4 | async-start | bytes 1572864 | tf_op jit(solution)/shard_map/all_to_all | solution.py:35
  (48 other events, 393.9 us)

commit v4 on v3

--- a/solution.py
+++ b/solution.py
@@ -52,27 +52,40 @@
     return lax.dot_general(left, right, (dims, ((), ())), preferred_element_type=jnp.float32)
 
 
-def call(kernel, out_shapes, operands, flops, in_specs=None, out_specs=None, **more):
+ANYWHERE = pl.BlockSpec(memory_space=pl.ANY)
+IN_VMEM = pl.BlockSpec(memory_space=pltpu.VMEM)
+TOKEN = jax.ShapeDtypeStruct((8, 128), jnp.float32)
+
+
+def call(kernel, out_shapes, operands, flops, in_specs=None, out_specs=None, waits=(), **more):
     moved = sum(a.size * a.dtype.itemsize for a in operands)
     moved += sum(o.size * o.dtype.itemsize for o in out_shapes)
+    taken, extra, given = len(operands), len(waits), len(out_shapes)
+
+    def run(*refs):
+        rest = refs[taken + extra :]
+        kernel(*refs[:taken], *rest[:given], *rest[given + 1 :])
+        rest[given][...] = jnp.zeros(TOKEN.shape, TOKEN.dtype)
+
     if in_specs is None and "grid_spec" not in more:
 
         def whole(array):
             return pl.BlockSpec(array.shape, lambda i: (0,) * len(array.shape))
 
         more["grid"] = (1,)
-        more["in_specs"] = [whole(a) for a in operands]
-        more["out_specs"] = [whole(o) for o in out_shapes]
-    elif in_specs is not None:
-        more["in_specs"] = in_specs
-        more["out_specs"] = out_specs
-    return pl.pallas_call(
-        kernel,
-        out_shape=out_shapes,
+        in_specs = [whole(a) for a in operands]
+        out_specs = [whole(o) for o in out_shapes]
+    if in_specs is not None:
+        more["in_specs"] = [*in_specs, *[ANYWHERE] * extra]
+        more["out_specs"] = [*out_specs, IN_VMEM]
+    *outs, token = pl.pallas_call(
+        run,
+        out_shape=[*out_shapes, TOKEN],
         cost_estimate=pl.CostEstimate(flops=flops, bytes_accessed=moved, transcendentals=0),
         compiler_params=pltpu.CompilerParams(vmem_limit_bytes=VMEM_BYTES),
         **more,
-    )(*operands)
+    )(*operands, *waits)
+    return outs, token
 
 
 def rms_scale(widened):
@@ -135,19 +148,16 @@
     out_ref[:, features:] = tags.astype(jnp.float32).astype(jnp.bfloat16)
 
 
-def picked_rows_kernel(choices, own_ref, left_ref, right_ref, top_ref, bottom_ref, out_ref):
+def picked_rows_kernel(choices, own_ref, left_ref, out_ref):
     experts, _, cap_rows, features = out_ref.shape
-    for c, pieces in enumerate(((own_ref,), (left_ref,), (right_ref,), (top_ref, bottom_ref))):
-        rows = None
-        for ref in pieces:
-            tags = ref[:, features:].astype(jnp.float32).astype(jnp.int32)
-            pick = None
-            for k in range(choices):
-                target = tags[:, k : k + 1] * cap_rows + tags[:, choices + k : choices + k + 1]
-                hit = hits_of(target, experts * cap_rows).astype(jnp.float32)
-                pick = hit if pick is None else pick + hit
-            part = matmul(pick.astype(jnp.bfloat16), ref[:, :features], ((0,), (0,)))
-            rows = part if rows is None else rows + part
+    for c, ref in enumerate((own_ref, left_ref)):
+        tags = ref[:, features:].astype(jnp.float32).astype(jnp.int32)
+        pick = None
+        for k in range(choices):
+            target = tags[:, k : k + 1] * cap_rows + tags[:, choices + k : choices + k + 1]
+            hit = hits_of(target, experts * cap_rows).astype(jnp.float32)
+            pick = hit if pick is None else pick + hit
+        rows = matmul(pick.astype(jnp.bfloat16), ref[:, :features], ((0,), (0,)))
         out_ref[:, c] = rows.astype(jnp.bfloat16).reshape(experts, cap_rows, features)
 
 
@@ -163,17 +173,18 @@
         copy.wait()
 
 
-def cut_halves(left, right):
-    anywhere = pl.BlockSpec(memory_space=pl.ANY)
-    return call(
+def cut_halves(left, right, waits=()):
+    outs, token = call(
         cut_kernel,
         [jax.ShapeDtypeStruct((left.shape[0] // 2, left.shape[1]), left.dtype)] * 2,
         [left, right],
         0,
-        in_specs=[anywhere] * 2,
-        out_specs=[pl.BlockSpec(memory_space=pltpu.VMEM)] * 2,
+        in_specs=[ANYWHERE] * 2,
+        out_specs=[IN_VMEM] * 2,
         scratch_shapes=[pltpu.SemaphoreType.DMA((2,))],
-    )
+        waits=waits,
+    )
+    return outs[0], outs[1], token
 
 
 def pick_grad_kernel(cap_rows, cot_ref, gate_ref, route_ref, slot_ref, out_ref):
@@ -246,7 +257,7 @@
             ).astype(jnp.bfloat16)
 
 
-def backward_chunks(place, grads, pre_blocks, w_in, w_out, sizes, shifts, split=False):
+def backward_chunks(place, grads, pre_blocks, w_in, w_out, sizes, shifts, split=False, waits=()):
     experts, groups, cap_rows, hidden = pre_blocks.shape
     features = w_in.shape[0]
     rows = experts * cap_rows
@@ -265,7 +276,7 @@
     out_shapes = [jax.ShapeDtypeStruct((rows, hidden), jnp.bfloat16)] * (2 * chunks) + [
         jax.ShapeDtypeStruct((rows // parts, features), jnp.bfloat16)
     ] * (parts * chunks)
-    outs = call(
+    outs, token = call(
         functools.partial(backward_kernel, sizes, split),
         out_shapes,
         [place, w_in, w_out, *grads] + [pre_blocks] * chunks,
@@ -275,15 +286,17 @@
             grid=(1,),
             in_specs=[whole(w_in.shape), whole(w_out.shape)]
             + [whole(g.shape) for g in grads]
-            + [shared(s) for s in shifts],
-            out_specs=[whole(o.shape) for o in out_shapes],
+            + [shared(s) for s in shifts]
+            + [ANYWHERE] * len(waits),
+            out_specs=[*[whole(o.shape) for o in out_shapes], IN_VMEM],
             scratch_shapes=[pltpu.VMEM((rows, hidden), jnp.float32)],
         ),
-    )
-    return outs[:chunks], outs[chunks : 2 * chunks], outs[2 * chunks :]
-
-
-def forward_chunks(rows_list, w_in, w_out, sizes, split=False):
+        waits=waits,
+    )
+    return outs[:chunks], outs[chunks : 2 * chunks], outs[2 * chunks :], token
+
+
+def forward_chunks(rows_list, w_in, w_out, sizes, split=False, waits=()):
     features, hidden = w_in.shape
     rows = sum(sizes[0])
     parts = 2 if split else 1
@@ -296,6 +309,7 @@
             pltpu.VMEM((rows, hidden), jnp.float32),
             pltpu.VMEM((rows, hidden), jnp.bfloat16),
         ],
+        waits=waits,
     )
 
 
@@ -326,10 +340,10 @@
     out_ref[...] = total.astype(jnp.bfloat16)
 
 
-def weight_grad(lefts, rights, tile):
+def weight_grad(lefts, rights, tile, waits=()):
     left_cols, right_cols = lefts[0].shape[1], rights[0].shape[1]
     rows = sum(a.shape[0] for a in lefts)
-    return call(
+    outs, token = call(
         functools.partial(
             weight_grad_kernel, [a.shape[0] for a in lefts], [a.shape[0] for a in rights]
         ),
@@ -340,33 +354,59 @@
         + [pl.BlockSpec(a.shape, lambda i: (0, 0)) for a in rights],
         out_specs=[pl.BlockSpec((tile, right_cols), lambda i: (i, 0))],
         grid=(left_cols // tile,),
-    )[0]
-
-
-def exchanged_grad_kernel(rows_ref, *refs):
-    out_ref = refs[-1]
-    blocks, chunks, slots, tile = rows_ref.shape
+        waits=waits,
+    )
+    return outs[0], token
+
+
+def first_grad_kernel(rows_ref, own_ref, left_ref, out_ref):
+    blocks, _, slots, tile = rows_ref.shape
     total = None
-    for c in range(chunks):
+    for c, right in enumerate((own_ref, left_ref)):
         rows = rows_ref[:, c].reshape(blocks * slots, tile)
-        part = matmul(rows, refs[c][...], ((0,), (0,)))
+        part = matmul(rows, right[...], ((0,), (0,)))
         total = part if total is None else total + part
-    out_ref[...] = total.astype(jnp.bfloat16)
-
-
-def exchanged_grad(rows, rights, tile):
+    out_ref[...] = total
+
+
+def first_grad(rows, rights, tile, waits):
     blocks, chunks, slots, features = rows.shape
     hidden = rights[0].shape[1]
-    return call(
-        exchanged_grad_kernel,
-        [jax.ShapeDtypeStruct((features, hidden), jnp.bfloat16)],
+    outs, token = call(
+        first_grad_kernel,
+        [jax.ShapeDtypeStruct((features, hidden), jnp.float32)],
         [rows, *rights],
         2 * blocks * chunks * slots * features * hidden,
         in_specs=[pl.BlockSpec((blocks, chunks, slots, tile), lambda i: (0, 0, 0, i))]
         + [pl.BlockSpec(a.shape, lambda i: (0, 0)) for a in rights],
         out_specs=[pl.BlockSpec((tile, hidden), lambda i: (i, 0))],
         grid=(features // tile,),
-    )[0]
+        waits=waits,
+    )
+    return outs[0], token
+
+
+def last_grad_kernel(first_ref, one_ref, two_ref, right_one_ref, right_two_ref, out_ref):
+    total = first_ref[...] + matmul(one_ref[...], right_one_ref[...], ((0,), (0,)))
+    total = total + matmul(two_ref[...], right_two_ref[...], ((0,), (0,)))
+    out_ref[...] = total.astype(jnp.bfloat16)
+
+
+def last_grad(first, lefts, rights, tile):
+    features, hidden = first.shape
+    rows = lefts[0].shape[0]
+    place = pl.BlockSpec((tile, hidden), lambda i: (i, 0))
+    return call(
+        last_grad_kernel,
+        [jax.ShapeDtypeStruct((features, hidden), jnp.bfloat16)],
+        [first, *lefts, *rights],
+        4 * rows * features * hidden,
+        in_specs=[place]
+        + [pl.BlockSpec((rows, tile), lambda i: (0, i))] * 2
+        + [pl.BlockSpec((rows, hidden), lambda i: (0, 0))] * 2,
+        out_specs=[place],
+        grid=(features // tile,),
+    )[0][0]
 
 
 def add_kernel(into_ref, more_ref, out_ref):
@@ -375,10 +415,10 @@
     ).astype(jnp.bfloat16)
 
 
-def add_half(into, more, which):
+def add_half(into, more, which, waits=()):
     half, features = more.shape
     place = pl.BlockSpec((half, features), lambda i: (which, 0))
-    return call(
+    outs, token = call(
         add_kernel,
         [jax.ShapeDtypeStruct(into.shape, into.dtype)],
         [into, more],
@@ -387,7 +427,9 @@
         out_specs=[place],
         grid=(1,),
         input_output_aliases={0: 0},
-    )[0]
+        waits=waits,
+    )
+    return outs[0], token
 
 
 def sum_kernel(one_ref, two_ref, three_ref, out_ref):
@@ -398,10 +440,45 @@
     ).astype(jnp.bfloat16)
 
 
-def sum_three(one, two, three):
-    return call(
-        sum_kernel, [jax.ShapeDtypeStruct(one.shape, one.dtype)], [one, two, three], 2 * one.size
-    )[0]
+def sum_three(one, two, three, waits=()):
+    outs, token = call(
+        sum_kernel,
+        [jax.ShapeDtypeStruct(one.shape, one.dtype)],
+        [one, two, three],
+        2 * one.size,
+        waits=waits,
+    )
+    return outs[0], token
+
+
+def sum_split_kernel(one_ref, two_ref, three_ref, both_ref, out_ref, own_ref, left_ref, sems):
+    copies = [
+        pltpu.make_async_copy(both_ref.at[:, 0], own_ref, sems.at[0]),
+        pltpu.make_async_copy(both_ref.at[:, 1], left_ref, sems.at[1]),
+    ]
+    for copy in copies:
+        copy.start()
+    sum_kernel(one_ref, two_ref, three_ref, out_ref)
+    for copy in copies:
+        copy.wait()
+
+
+def sum_and_split(one, two, three, both, waits):
+    experts, _, slots, features = both.shape
+    whole = pl.BlockSpec(one.shape, lambda i: (0, 0))
+    outs, _ = call(
+        sum_split_kernel,
+        [jax.ShapeDtypeStruct(one.shape, one.dtype)]
+        + [jax.ShapeDtypeStruct((experts, slots, features), both.dtype)] * 2,
+        [one, two, three, both],
+        2 * one.size,
+        in_specs=[whole, whole, whole, ANYWHERE],
+        out_specs=[whole, IN_VMEM, IN_VMEM],
+        grid=(1,),
+        scratch_shapes=[pltpu.SemaphoreType.DMA((2,))],
+        waits=waits,
+    )
+    return [o.reshape(one.shape) for o in outs]
 
 
 def forward_out_kernel(cap_rows, arrival_ref, gate_ref, route_ref, returned_ref, out_ref):
@@ -467,121 +544,133 @@
     arrival = shifted(after(fwd_handoff, cotangent), "section", 1)[0]
     cotangent = cotangent[0]
 
-    tagged = call(
+    (tagged,), tagged_token = call(
         tagged_kernel,
         [jax.ShapeDtypeStruct((tok_rows, features + 128), jnp.bfloat16)],
         [saved_input[0], gain, route_bwd[0], slot_bwd[0]],
         0,
-    )[0]
-    tagged_left, tagged_right = turned(tagged, groups, 1), turned(tagged, groups, -1)
-    tagged_left_top, tagged_right_bottom = cut_halves(tagged_left, tagged_right)
-    tagged_top = turned(tagged_left_top, groups, 1)
-    tagged_bottom = turned(tagged_right_bottom, groups, -1)
-
-    grad_rows = call(
+    )
+    tagged_left = turned(tagged, groups, 1)
+
+    (grad_rows,), _ = call(
         functools.partial(pick_grad_kernel, cap_rows),
         rows_shape,
-        [after(cotangent, tagged), gate_bwd[0], route_bwd[0], slot_bwd[0]],
+        [cotangent, gate_bwd[0], route_bwd[0], slot_bwd[0]],
         2 * pick_flops,
-    )[0]
-    rows_fwd = call(
+        waits=[tagged_token],
+    )
+    (rows_fwd,), _ = call(
         functools.partial(pick_forward_kernel, cap_rows),
         rows_shape,
-        [after(arrival, tagged_top, tagged_bottom), gain, route_fwd[0]],
+        [arrival, gain, route_fwd[0]],
         pick_flops,
-    )[0]
-
+        waits=[tagged_left],
+    )
+
+    whole, halves = (all_rows,), (half, half)
     grads = send(grad_rows)
     grads_left, grads_right = turned(grads, groups, 1), turned(grads, groups, -1)
     sent_fwd = send(after(rows_fwd, grads))
-    whole, halves = (all_rows,), (half, half)
-    hidden_0, pre_grad_0, back_0 = backward_chunks(
+    hidden_0, pre_grad_0, back_0, token_0 = backward_chunks(
         mine, [grads], pre_blocks, w_in_local, w_out_local, [whole], (0,)
     )
-    rows_bwd = call(
-        functools.partial(picked_rows_kernel, choices),
-        [jax.ShapeDtypeStruct((EXPERTS, groups, cap_rows, features), jnp.bfloat16)],
-        [after(tagged, rows_fwd, *back_0), tagged_left, tagged_right, tagged_top, tagged_bottom],
-        groups * pick_flops,
-    )[0]
-    grads_left_top, grads_right_bottom = cut_halves(after(grads_left, rows_bwd), grads_right)
+    grads_left_top, grads_right_bottom, cut_token = cut_halves(grads_left, grads_right, [token_0])
     grads_top = turned(grads_left_top, groups, 1)
     grads_bottom = turned(grads_right_bottom, groups, -1)
-    ready = after(sent_fwd, grads_left, grads_right)
-    left, right = turned(ready, groups, 1), turned(ready, groups, -1)
-    sent_rows = send(after(rows_bwd, sent_fwd, grads_left_top, grads_right_bottom))
-
-    hidden_1, pre_grad_1, back_1 = backward_chunks(
+    (rows_bwd,), rows_token = call(
+        functools.partial(picked_rows_kernel, choices),
+        [jax.ShapeDtypeStruct((EXPERTS, 2, cap_rows, features), jnp.bfloat16)],
+        [tagged, tagged_left],
+        2 * pick_flops,
+        waits=[cut_token],
+    )
+    sent_rows = send(rows_bwd).reshape(rows_bwd.shape)
+    left, right = turned(sent_fwd, groups, 1), turned(sent_fwd, groups, -1)
+
+    hidden_1, pre_grad_1, back_1, token_1 = backward_chunks(
         mine,
-        [after(grads_left, sent_fwd), grads_right],
+        [grads_left, grads_right],
         pre_blocks,
         w_in_local,
         w_out_local,
         [whole] * 2,
         (groups - 1, 1),
-    )
-    hidden_2, pre_grad_2, back_2 = backward_chunks(
+        waits=[cut_token, rows_token],
+    )
+    left_top, right_bottom, cut_token = cut_halves(left, right, [token_1])
+    opposite_top = turned(left_top, groups, 1)
+    opposite_bottom = turned(right_bottom, groups, -1)
+    hidden_2, pre_grad_2, back_2, token_2 = backward_chunks(
         mine,
-        [after(grads_top, *back_1), grads_bottom],
+        [grads_top, grads_bottom],
         pre_blocks,
         w_in_local,
         w_out_local,
         [halves],
         (2,),
         split=True,
+        waits=[token_1, cut_token],
     )
     back_top = turned(back_2[0], groups, 1)
     back_bottom = turned(back_2[1], groups, -1)
 
-    left_top, right_bottom = cut_halves(left, right)
-    opposite_top = turned(left_top, groups, 1)
-    opposite_bottom = turned(right_bottom, groups, -1)
-    grad_w_out = weight_grad(
+    fwd_0, token_3 = forward_chunks([sent_fwd], w_in_local, w_out_local, [whole], waits=[token_2])
+    grad_w_out, token_4 = weight_grad(
         [*hidden_0, *hidden_1, *hidden_2],
-        [after(grads, left_top, right_bottom), grads_left, grads_right, grads_top, grads_bottom],
+        [grads, grads_left, grads_right, grads_top, grads_bottom],
         256,
-    )
-    fwd_0 = forward_chunks([after(sent_fwd, left_top, right_bottom)], w_in_local, w_out_local, [whole])
-
-    arrived = (grad_w_out, *fwd_0, opposite_top, opposite_bottom)
-    back_to_left = add_half(back_1[1], after(back_top, *arrived), 0)
-    back_to_right = add_half(back_1[0], after(back_bottom, *arrived), 1)
+        waits=[token_2],
+    )
+    back_to_left, token_5 = add_half(back_1[1], back_top, 0, [token_3, token_4])
+    back_to_right, token_6 = add_half(back_1[0], back_bottom, 1, [token_3, token_4])
     back_left = turned(back_to_left, groups, 1)
     back_right = turned(back_to_right, groups, -1)
-    fwd_1 = forward_chunks(
-        [after(left, back_to_left, back_to_right), right], w_in_local, w_out_local, [whole] * 2
-    )
-    fwd_2 = forward_chunks(
-        [after(opposite_top, *fwd_1), opposite_bottom], w_in_local, w_out_local, [halves], split=True
+    fwd_1, token_7 = forward_chunks(
+        [left, right], w_in_local, w_out_local, [whole] * 2, waits=[token_5, token_6]
+    )
+    fwd_2, _ = forward_chunks(
+        [opposite_top, opposite_bottom],
+        w_in_local,
+        w_out_local,
+        [halves],
+        split=True,
+        waits=[token_7],
     )
     fwd_top = turned(fwd_2[0], groups, 1)
     fwd_bottom = turned(fwd_2[1], groups, -1)
 
-    back_sum = sum_three(after(back_0[0], *fwd_2), back_left, back_right)
-    fwd_to_left = add_half(fwd_1[1], fwd_top, 0)
-    fwd_to_right = add_half(fwd_1[0], fwd_bottom, 1)
-    return_bwd = send(after(back_sum, sent_rows, fwd_to_left, fwd_to_right))
-    grad_w_in = exchanged_grad(
-        sent_rows.reshape(rows_bwd.shape), [*pre_grad_0, *pre_grad_1, *pre_grad_2], 256
-    )
-
+    fwd_to_left, token_8 = add_half(fwd_1[1], fwd_top, 0)
+    fwd_to_right, token_9 = add_half(fwd_1[0], fwd_bottom, 1)
+    back_sum, _ = sum_three(back_0[0], back_left, back_right, [token_8, token_9])
+    return_bwd = send(back_sum)
     fwd_left = turned(fwd_to_left, groups, 1)
     fwd_right = turned(fwd_to_right, groups, -1)
-    fwd_sum = sum_three(fwd_0[0], after(fwd_left, grad_w_in), fwd_right)
+    first, token_10 = first_grad(
+        sent_rows, [pre_grad_0[0], pre_grad_1[0]], 256, [token_8, token_9]
+    )
+    fwd_sum, own_rows, left_rows = sum_and_split(
+        fwd_0[0], fwd_left, fwd_right, sent_rows, [token_10]
+    )
     return_fwd = send(after(fwd_sum, return_bwd))
+
+    right_rows = turned(own_rows, groups, -1)
+    opposite_rows = turned(left_rows, groups, 1)
+    grad_w_in = last_grad(
+        first, [right_rows, opposite_rows], [pre_grad_1[1], pre_grad_2[0]], 256
+    )
 
     section_out = call(
         functools.partial(forward_out_kernel, cap_rows),
         token_shape,
         [arrival, gate_fwd[0], route_fwd[0], return_fwd],
         2 * pick_flops,
-    )[0]
+    )[0][0]
     input_grad = call(
         functools.partial(backward_out_kernel, cap_rows),
         token_shape,
         [saved_input[0], gain, cotangent, route_bwd[0], slot_bwd[0], return_bwd],
         pick_flops,
-    )[0]
+    )[0][0]
     return (section_out[None], input_grad[None], grad_w_in[None], grad_w_out[None])
 
 

time: 215 us -> 224 us (1.042)
  local copies, waits for them, and re-layouts: 23 us -> 29.6 us
  waiting for transfers between devices: 79.3 us -> 85.2 us
  starting transfers between devices: 64.5 us -> 61.3 us
    ppermute x20 -> x19, waiting for transfers between devices: 64.5 us -> 75.7 us  [turned(): return lax.ppermute(block, 'expert', route)]
    unnamed x95 -> x99, local copies, waits for them, and re-layouts: 23 us -> 29.6 us
    all_to_all x5, waiting for transfers between devices: 14.3 us -> 9 us  [exchange(): lax.all_to_all(block, 'expert', split_axis=0, concat_axis=0, tiled=True,...]
    ppermute x20 -> x19, starting transfers between devices: 28.8 us -> 26.1 us  [turned(): return lax.ppermute(block, 'expert', route)]
  transfers between devices with their start and end apart: 27 -> 26, of which waited for: 13 -> 14; matrix products, arithmetic and copies ran while one was open for 2% -> 2% of each run, Pallas kernels for 20% -> 19%
where the time goes in v4:
time: 224 us; the launch traced here: 222 us
  waiting for transfers between devices  85.2 us (38%)
  starting transfers between devices  61.3 us (27%)
  Pallas kernels  45.3 us (20%)
  local copies, waits for them, and re-layouts  29.6 us (13%)
    ppermute x19, waiting for transfers between devices, turned(): return lax.ppermute(block, 'expert', route)  75.7 us
    pallas_call x23, Pallas kernels, call(): pl.pallas_call(run, out_shape=[*out_shapes, TOKEN], cost_estimate=pl.Cost...  45.3 us
    all_to_all x5, starting transfers between devices, exchange(): lax.all_to_all(block, 'expert', split_axis=0, concat_axis=0, tiled=True,...  32.9 us
    unnamed x99, local copies, waits for them, and re-layouts  29.6 us
    ppermute x19, starting transfers between devices, turned(): return lax.ppermute(block, 'expert', route)  26.1 us
    all_to_all x5, waiting for transfers between devices, exchange(): lax.all_to_all(block, 'expert', split_axis=0, concat_axis=0, tiled=True,...  9 us
  transfers between devices with their start and end apart: 26, of which 14 were waited for; matrix products, arithmetic and copies ran while one was open for 2% of the time, Pallas kernels for 19%

profile of v4, /device:TPU:6, one launch (start us, length us, event | category | flops | bytes accessed | tf_op | source)
XLA Modules:
  0.0 222.4 jit_solution(9444685355200537966)
XLA Ops:
  8.1 8.5 %all-to-all-start = ((bf16[8,32,1536]{2,1,0:T(8,128)(2,1)}), bf16[8,32,1536]{2,1,0:T(8,128)(2,1)S(1)}, u32[]{:S(2)}, u32[]{:S(2)}) async-start(bf16[8,32,1536]{2,1,0:T(8,128)(2,1)} %bitcast.56), calls=%async_computation | async-start | bytes 1572864 | tf_op jit(solution)/shard_map/all_to_all | solution.py:35
  21.0 8.4 %collective-permute-done.2.refs_3_.refs_1_ = bf16[128,1664]{1,0:T(8,128)(2,1)} collective-permute-done((bf16[128,1664]{1,0:T(8,128)(2,1)}, bf16[128,1664]{1,0:T(8,128)(2,1)}, u32[]{:S(2)}, u32[]{:S(2)}) %collective-permute-start.2) | collective-permute-done | bytes 426016 | tf_op jit(solution)/shard_map/ppermute | solution.py:30
  32.0 9.0 %all-to-all-done = bf16[8,32,1536]{2,1,0:T(8,128)(2,1)S(1)} async-done(((bf16[8,32,1536]{2,1,0:T(8,128)(2,1)}), bf16[8,32,1536]{2,1,0:T(8,128)(2,1)S(1)}, u32[]{:S(2)}, u32[]{:S(2)}) %all-to-all-start) | async-done | bytes 786464 | tf_op jit(solution)/shard_map/all_to_all | solution.py:35
  41.0 4.2 %all-to-all-start.1 = ((bf16[8,32,1536]{2,1,0:T(8,128)(2,1)}), bf16[8,32,1536]{2,1,0:T(8,128)(2,1)}, u32[]{:S(2)}, u32[]{:S(2)}) async-start(bf16[8,32,1536]{2,1,0:T(8,128)(2,1)} %bitcast.55), calls=%async_computation.1 | async-start | bytes 1572864 | tf_op jit(solution)/shard_map/all_to_all | solution.py:35
  53.6 12.6 %collective-permute-done.3.refs_0_.refs_3_.refs_5_ = bf16[256,1536]{1,0:T(8,128)(2,1)} collective-permute-done((bf16[256,1536]{1,0:T(8,128)(2,1)S(1)}, bf16[256,1536]{1,0:T(8,128)(2,1)}, u32[]{:S(2)}, u32[]{:S(2)}) %collective-permute-start.3) | collective-permute-done | bytes 786464 | tf_op jit(solution)/shard_map/ppermute | solution.py:30
  71.9 6.7 %all-to-all-start.2 = ((bf16[8,64,1536]{2,1,0:T(8,128)(2,1)}), bf16[8,64,1536]{2,1,0:T(8,128)(2,1)}, u32[]{:S(2)}, u32[]{:S(2)}) async-start(bf16[8,64,1536]{2,1,0:T(8,128)(2,1)} %bitcast.50), calls=%async_computation.2 | async-start | bytes 3145728 | tf_op jit(solution)/shard_map/all_to_all | solution.py:35
  82.2 2.9 %collective-permute-start.6 = (bf16[128,1536]{1,0:T(8,128)(2,1)}, bf16[128,1536]{1,0:T(8,128)(2,1)S(1)}, u32[]{:S(2)}, u32[]{:S(2)}) collective-permute-start(bf16[128,1536]{1,0:T(8,128)(2,1)} %copy-done.43), channel_id=1, source_target_pairs={{0,3},{1,0},{2,1},{3,2},{4,7},{5,4},{6,5},{7,6},{8,11},{9,8},{10,9... | collective-permute-start | bytes 1179656 | tf_op jit(solution)/shard_map/ppermute | solution.py:30
  88.2 4.9 %shard_map.153 = (bf16[256,768]{1,0:T(8,128)(2,1)S(1)}, bf16[256,768]{1,0:T(8,128)(2,1)S(1)}, bf16[256,768]{1,0:T(8,128)(2,1)S(1)}, bf16[256,768]{1,0:T(8,128)(2...) custom-call(s32[1]{0:T(128)} %bitcast.14.refs_0_, ...), custom_call_target="tpu_custom_call" | custom-call | flops 2415919104 | bytes 12582916 | tf_op jit(solution)/shard_map/pallas_call | solution.py:81
  93.1 7.4 %collective-permute-done.7.refs_0_.refs_2_ = bf16[256,1536]{1,0:T(8,128)(2,1)S(1)} collective-permute-done((bf16[256,1536]{1,0:T(8,128)(2,1)}, bf16[256,1536]{1,0:T(8,128)(2,1)S(1)}, u32[]{:S(2)}, u32[]{:S(2)}) %collective-permute-start.7) | collective-permute-done | bytes 786464 | tf_op jit(solution)/shard_map/ppermute | solution.py:30
  101.3 5.4 %collective-permute-done.5.refs_3_.refs_7_ = bf16[128,1536]{1,0:T(8,128)(2,1)S(1)} collective-permute-done((bf16[128,1536]{1,0:T(8,128)(2,1)}, bf16[128,1536]{1,0:T(8,128)(2,1)S(1)}, u32[]{:S(2)}, u32[]{:S(2)}) %collective-permute-start.5) | collective-permute-done | bytes 393248 | tf_op jit(solution)/shard_map/ppermute | solution.py:30
  106.7 3.2 %shard_map.155 = (bf16[256,768]{1,0:T(8,128)(2,1)S(1)}, bf16[256,768]{1,0:T(8,128)(2,1)S(1)}, bf16[128,1536]{1,0:T(8,128)(2,1)S(1)}, bf16[128,1536]{1,0:T(8,128)(2,1)S(1)}, f32[8,128]{1,0:T(8,128)S(1)}) custom-call(s32[1]{0:T(128)} %bitcast.14.refs_0_, bf16[1536,768]{1,0:T(8,128)(2,1)S(1)} %bitcast.30, bf16[768,1536]{1,0:T(8,128)(2,1)S(1)} %bitcast.36, ...), custom_call_target="tpu_custom_call" | custom-call | flops 1207959552 | bytes 8650756 | tf_op jit(solution)/shard_map/pallas_call | solution.py:81
  110.7 2.9 %collective-permute-start.10 = (bf16[128,1536]{1,0:T(8,128)(2,1)S(1)}, bf16[128,1536]{1,0:T(8,128)(2,1)S(1)}, u32[]{:S(2)}, u32[]{:S(2)}) collective-permute-start(bf16[128,1536]{1,0:T(8,128)(2,1)S(1)} %get-tuple-element.86), channel_id=1, source_target_pairs={{0,3},{1,0},{2,1},{3,2},{4,7},{5,4},{6,5},{7,6},{8,11},{9,8},{10,9... | collective-permute-start | bytes 1179656 | tf_op jit(solution)/shard_map/ppermute | solution.py:30
  113.7 3.2 %collective-permute-start.12 = (bf16[128,1536]{1,0:T(8,128)(2,1)S(1)}, bf16[128,1536]{1,0:T(8,128)(2,1)S(1)}, u32[]{:S(2)}, u32[]{:S(2)}) collective-permute-start(bf16[128,1536]{1,0:T(8,128)(2,1)S(1)} %get-tuple-element.90), channel_id=1, source_target_pairs={{0,3},{1,0},{2,1},{3,2},{4,7},{5,4},{6,5},{7,6},{8,11},{9,8},{10,9... | collective-permute-start | bytes 1179656 | tf_op jit(solution)/shard_map/ppermute | solution.py:30
  116.9 6.0 %shard_map.157 = (bf16[768,1536]{1,0:T(8,128)(2,1)}, f32[8,128]{1,0:T(8,128)S(1)}) custom-call(bf16[256,768]{1,0:T(8,128)(2,1)S(1)} %copy-done.42, bf16[256,768]{1,0:T(8,128)(2,1)S(1)} %get-tuple-element.80.refs_1_, bf16[256,768]{1,0:T(8,128)(2,1)S(1)} %get-tuple-element.81.refs_2_, bf16[256,768]{1,0:T(8,128)(2,1)S(1)} %get-tuple-element.82.refs_3_, ...), custom_call_target="tpu_custom_call" | custom-call | flops 2415919104 | bytes 7077888 | tf_op jit(solution)/shard_map/pallas_call | solution.py:81
  122.9 2.9 %shard_map.156 = (bf16[256,1536]{1,0:T(8,128)(2,1)S(1)}, f32[8,128]{1,0:T(8,128)S(1)}) custom-call(bf16[1536,768]{1,0:T(8,128)(2,1)S(1)} %bitcast.31, bf16[768,1536]{1,0:T(8,128)(2,1)S(1)} %bitcast.37, bf16[256,1536]{1,0:T(8,128)(2,1)} %bitcast.13.refs_2_, f32[8,128]{1,0:T(8,128)S(1)} %get-tuple-element.74.refs_3_.refs_9_), custom_call_target="tpu_custom_call" | custom-call | flops 1207959552 | bytes 6291456 | tf_op jit(solution)/shard_map/pallas_call | solution.py:81
  128.8 3.0 %shard_map.160 = (bf16[256,1536]{1,0:T(8,128)(2,1)S(1)}, bf16[256,1536]{1,0:T(8,128)(2,1)S(1)}, f32[8,128]{1,0:T(8,128)S(1)}) custom-call(bf16[1536,768]{1,0:T(8,128)(2,1)S(1)} %bitcast.32, bf16[768,1536]{1,0:T(8,128)(2,1)S(1)} %bitcast.38, bf16[256,1536]{1,0:T(8,128)(2,1)S(1)} %collective-permute-done.7.refs_0_.refs_2_, ...), custom_call_target="tpu_custom_call" | custom-call | flops 2415919104 | bytes 7864320 | tf_op jit(solution)/shard_map/pallas_call | solution.py:81
  138.3 15.2 %collective-permute-done.15.refs_1_ = bf16[128,1536]{1,0:T(8,128)(2,1)S(1)} collective-permute-done((bf16[128,1536]{1,0:T(8,128)(2,1)S(1)}, bf16[128,1536]{1,0:T(8,128)(2,1)S(1)}, u32[]{:S(2)}, u32[]{:S(2)}) %collective-permute-start.15) | collective-permute-done | bytes 393248 | tf_op jit(solution)/shard_map/ppermute | solution.py:30
  153.8 3.1 %collective-permute-done.13.refs_1_ = bf16[128,1536]{1,0:T(8,128)(2,1)S(1)} collective-permute-done((bf16[128,1536]{1,0:T(8,128)(2,1)S(1)}, bf16[128,1536]{1,0:T(8,128)(2,1)S(1)}, u32[]{:S(2)}, u32[]{:S(2)}) %collective-permute-start.13) | collective-permute-done | bytes 393248 | tf_op jit(solution)/shard_map/ppermute | solution.py:30
  158.5 6.6 %all-to-all-start.3 = ((bf16[8,32,1536]{2,1,0:T(8,128)(2,1)}), bf16[8,32,1536]{2,1,0:T(8,128)(2,1)S(1)}, u32[]{:S(2)}, u32[]{:S(2)}) async-start(bf16[8,32,1536]{2,1,0:T(8,128)(2,1)} %bitcast.18), calls=%async_computation.3 | async-start | bytes 1572864 | tf_op jit(solution)/shard_map/all_to_all | solution.py:35
  169.3 4.5 %shard_map.164 = (f32[1536,768]{1,0:T(8,128)S(1)}, f32[8,128]{1,0:T(8,128)S(1)}) custom-call(bf16[8,2,32,1536]{3,2,1,0:T(8,128)(2,1)} %bitcast.17.refs_0_.refs_3_, bf16[256,768]{1,0:T(8,128)(2,1)S(1)} %copy-done.38, bf16[256,768]{1,0:T(8,128)(2,1)S(1)} %copy-done.40, f32[8,128]{1,0:T(8,128)S(1)} %get-tuple-element.100.refs_3_, ...), custom_call_target="tpu_custom_call" | custom-call | flops 1207959552 | bytes 7077888 | tf_op jit(solution)/shard_map/pallas_call | solution.py:81
  175.9 6.0 %collective-permute-done.16.refs_2_ = bf16[256,1536]{1,0:T(8,128)(2,1)S(1)} collective-permute-done((bf16[256,1536]{1,0:T(8,128)(2,1)}, bf16[256,1536]{1,0:T(8,128)(2,1)S(1)}, u32[]{:S(2)}, u32[]{:S(2)}) %collective-permute-start.16) | collective-permute-done | bytes 786464 | tf_op jit(solution)/shard_map/ppermute | solution.py:30
  186.7 6.8 %all-to-all-start.4 = ((bf16[8,32,1536]{2,1,0:T(8,128)(2,1)}), bf16[8,32,1536]{2,1,0:T(8,128)(2,1)S(1)}, u32[]{:S(2)}, u32[]{:S(2)}) async-start(bf16[8,32,1536]{2,1,0:T(8,128)(2,1)} %bitcast.20), calls=%async_computation.4 | async-start | bytes 1572864 | tf_op jit(solution)/shard_map/all_to_all | solution.py:35
  196.3 11.6 %collective-permute-done.19.refs_1_ = bf16[256,1536]{1,0:T(8,128)(2,1)S(1)} collective-permute-done((bf16[256,1536]{1,0:T(8,128)(2,1)}, bf16[256,1536]{1,0:T(8,128)(2,1)S(1)}, u32[]{:S(2)}, u32[]{:S(2)}) %collective-permute-start.19) | collective-permute-done | bytes 786464 | tf_op jit(solution)/shard_map/ppermute | solution.py:30
  214.0 3.9 %shard_map.169 = (bf16[1536,768]{1,0:T(8,128)(2,1)}, f32[8,128]{1,0:T(8,128)}) custom-call(f32[1536,768]{1,0:T(8,128)S(1)} %copy-done.8, bf16[256,1536]{1,0:T(8,128)(2,1)S(1)} %collective-permute-done.19.refs_1_, bf16[256,1536]{1,0:T(8,128)(2,1)S(1)} %collective-permute-done.20.refs_2_, bf16[256,768]{1,0:T(8,128)(2,1)S(1)} %copy-done.28, ...), custom_call_target="tpu_custom_call" | custom-call | flops 1207959552 | bytes 9437184 | tf_op jit(solution)/shard_map/pallas_call | solution.py:81
  (150 shorter events, 72.3 us)
Async XLA Ops:
  8.1 32.9 %all-to-all-start = ((bf16[8,32,1536]{2,1,0:T(8,128)(2,1)}), bf16[8,32,1536]{2,1,0:T(8,128)(2,1)S(1)}, u32[]{:S(2)}, u32[]{:S(2)}) async-start(bf16[8,32,1536]{2,1,0:T(8,128)(2,1)} %bitcast.56), calls=%async_computation | async-start | bytes 1572864 | tf_op jit(solution)/shard_map/all_to_all | solution.py:35
  16.6 12.8 %collective-permute-start.2 = (bf16[128,1664]{1,0:T(8,128)(2,1)}, bf16[128,1664]{1,0:T(8,128)(2,1)}, u32[]{:S(2)}, u32[]{:S(2)}) collective-permute-start(bf16[128,1664]{1,0:T(8,128)(2,1)} %copy-done.25), channel_id=1, source_target_pairs={{0,1},{1,2},{2,3},{3,0},{4,5},{5,6},{6,7},{7,4},{8,9},{9,10},{10,1... | collective-permute-start | bytes 1277960 | tf_op jit(solution)/shard_map/ppermute | solution.py:30
  41.0 30.9 %all-to-all-start.1 = ((bf16[8,32,1536]{2,1,0:T(8,128)(2,1)}), bf16[8,32,1536]{2,1,0:T(8,128)(2,1)}, u32[]{:S(2)}, u32[]{:S(2)}) async-start(bf16[8,32,1536]{2,1,0:T(8,128)(2,1)} %bitcast.55), calls=%async_computation.1 | async-start | bytes 1572864 | tf_op jit(solution)/shard_map/all_to_all | solution.py:35
  45.3 21.0 %collective-permute-start.3 = (bf16[256,1536]{1,0:T(8,128)(2,1)S(1)}, bf16[256,1536]{1,0:T(8,128)(2,1)}, u32[]{:S(2)}, u32[]{:S(2)}) collective-permute-start(bf16[256,1536]{1,0:T(8,128)(2,1)S(1)} %bitcast.44), channel_id=1, source_target_pairs={{0,1},{1,2},{2,3},{3,0},{4,5},{5,6},{6,7},{7,4},{8,9},{9,10},{10,1... | collective-permute-start | bytes 2359304 | tf_op jit(solution)/shard_map/ppermute | solution.py:30
  46.9 19.4 %collective-permute-start.4 = (bf16[256,1536]{1,0:T(8,128)(2,1)S(1)}, bf16[256,1536]{1,0:T(8,128)(2,1)}, u32[]{:S(2)}, u32[]{:S(2)}) collective-permute-start(bf16[256,1536]{1,0:T(8,128)(2,1)S(1)} %bitcast.45), channel_id=1, source_target_pairs={{0,3},{1,0},{2,1},{3,2},{4,7},{5,4},{6,5},{7,6},{8,11},{9,8},{10,9... | collective-permute-start | bytes 2359304 | tf_op jit(solution)/shard_map/ppermute | solution.py:30
  71.9 86.6 %all-to-all-start.2 = ((bf16[8,64,1536]{2,1,0:T(8,128)(2,1)}), bf16[8,64,1536]{2,1,0:T(8,128)(2,1)}, u32[]{:S(2)}, u32[]{:S(2)}) async-start(bf16[8,64,1536]{2,1,0:T(8,128)(2,1)} %bitcast.50), calls=%async_computation.2 | async-start | bytes 3145728 | tf_op jit(solution)/shard_map/all_to_all | solution.py:35
  78.6 21.9 %collective-permute-start.7 = (bf16[256,1536]{1,0:T(8,128)(2,1)}, bf16[256,1536]{1,0:T(8,128)(2,1)S(1)}, u32[]{:S(2)}, u32[]{:S(2)}) collective-permute-start(bf16[256,1536]{1,0:T(8,128)(2,1)} %bitcast.13.refs_2_), channel_id=1, source_target_pairs={{0,1},{1,2},{2,3},{3,0},{4,5},{5,6},{6,7},{7,4},{8,9},{9,10},{10,1... | collective-permute-start | bytes 2359304 | tf_op jit(solution)/shard_map/ppermute | solution.py:30
  80.2 20.7 %collective-permute-start.8 = (bf16[256,1536]{1,0:T(8,128)(2,1)}, bf16[256,1536]{1,0:T(8,128)(2,1)S(1)}, u32[]{:S(2)}, u32[]{:S(2)}) collective-permute-start(bf16[256,1536]{1,0:T(8,128)(2,1)} %bitcast.13.refs_2_), channel_id=1, source_target_pairs={{0,3},{1,0},{2,1},{3,2},{4,7},{5,4},{6,5},{7,6},{8,11},{9,8},{10,9... | collective-permute-start | bytes 2359304 | tf_op jit(solution)/shard_map/ppermute | solution.py:30
  81.9 24.8 %collective-permute-start.5 = (bf16[128,1536]{1,0:T(8,128)(2,1)}, bf16[128,1536]{1,0:T(8,128)(2,1)S(1)}, u32[]{:S(2)}, u32[]{:S(2)}) collective-permute-start(bf16[128,1536]{1,0:T(8,128)(2,1)} %copy-done.44), channel_id=1, source_target_pairs={{0,1},{1,2},{2,3},{3,0},{4,5},{5,6},{6,7},{7,4},{8,9},{9,10},{10,1... | collective-permute-start | bytes 1179656 | tf_op jit(solution)/shard_map/ppermute | solution.py:30
  82.2 24.4 %collective-permute-start.6 = (bf16[128,1536]{1,0:T(8,128)(2,1)}, bf16[128,1536]{1,0:T(8,128)(2,1)S(1)}, u32[]{:S(2)}, u32[]{:S(2)}) collective-permute-start(bf16[128,1536]{1,0:T(8,128)(2,1)} %copy-done.43), channel_id=1, source_target_pairs={{0,3},{1,0},{2,1},{3,2},{4,7},{5,4},{6,5},{7,6},{8,11},{9,8},{10,9... | collective-permute-start | bytes 1179656 | tf_op jit(solution)/shard_map/ppermute | solution.py:30
  110.7 15.1 %collective-permute-start.10 = (bf16[128,1536]{1,0:T(8,128)(2,1)S(1)}, bf16[128,1536]{1,0:T(8,128)(2,1)S(1)}, u32[]{:S(2)}, u32[]{:S(2)}) collective-permute-start(bf16[128,1536]{1,0:T(8,128)(2,1)S(1)} %get-tuple-element.86), channel_id=1, source_target_pairs={{0,3},{1,0},{2,1},{3,2},{4,7},{5,4},{6,5},{7,6},{8,11},{9,8},{10,9... | collective-permute-start | bytes 1179656 | tf_op jit(solution)/shard_map/ppermute | solution.py:30
  113.6 14.5 %collective-permute-start.9 = (bf16[128,1536]{1,0:T(8,128)(2,1)S(1)}, bf16[128,1536]{1,0:T(8,128)(2,1)S(1)}, u32[]{:S(2)}, u32[]{:S(2)}) collective-permute-start(bf16[128,1536]{1,0:T(8,128)(2,1)S(1)} %get-tuple-element.77), channel_id=1, source_target_pairs={{0,1},{1,2},{2,3},{3,0},{4,5},{5,6},{6,7},{7,4},{8,9},{9,10},{10,1... | collective-permute-start | bytes 1179656 | tf_op jit(solution)/shard_map/ppermute | solution.py:30
  113.6 20.8 %collective-permute-start.11 = (bf16[128,1536]{1,0:T(8,128)(2,1)S(1)}, bf16[128,1536]{1,0:T(8,128)(2,1)S(1)}, u32[]{:S(2)}, u32[]{:S(2)}) collective-permute-start(bf16[128,1536]{1,0:T(8,128)(2,1)S(1)} %get-tuple-element.89), channel_id=1, source_target_pairs={{0,1},{1,2},{2,3},{3,0},{4,5},{5,6},{6,7},{7,4},{8,9},{9,10},{10,1... | collective-permute-start | bytes 1179656 | tf_op jit(solution)/shard_map/ppermute | solution.py:30
  113.7 20.7 %collective-permute-start.12 = (bf16[128,1536]{1,0:T(8,128)(2,1)S(1)}, bf16[128,1536]{1,0:T(8,128)(2,1)S(1)}, u32[]{:S(2)}, u32[]{:S(2)}) collective-permute-start(bf16[128,1536]{1,0:T(8,128)(2,1)S(1)} %get-tuple-element.90), channel_id=1, source_target_pairs={{0,3},{1,0},{2,1},{3,2},{4,7},{5,4},{6,5},{7,6},{8,11},{9,8},{10,9... | collective-permute-start | bytes 1179656 | tf_op jit(solution)/shard_map/ppermute | solution.py:30
  126.1 31.1 %collective-permute-start.18 = (bf16[256,1536]{1,0:T(8,128)(2,1)S(1)}, bf16[256,1536]{1,0:T(8,128)(2,1)S(1)}, u32[]{:S(2)}, u32[]{:S(2)}) collective-permute-start(bf16[256,1536]{1,0:T(8,128)(2,1)S(1)} %get-tuple-element.106), channel_id=1, source_target_pairs={{0,3},{1,0},{2,1},{3,2},{4,7},{5,4},{6,5},{7,6},{8,11},{9,8},{10,9... | collective-permute-start | bytes 2359304 | tf_op jit(solution)/shard_map/ppermute | solution.py:30
  128.5 28.8 %collective-permute-start.17 = (bf16[256,1536]{1,0:T(8,128)(2,1)S(1)}, bf16[256,1536]{1,0:T(8,128)(2,1)S(1)}, u32[]{:S(2)}, u32[]{:S(2)}) collective-permute-start(bf16[256,1536]{1,0:T(8,128)(2,1)S(1)} %get-tuple-element.105), channel_id=1, source_target_pairs={{0,1},{1,2},{2,3},{3,0},{4,5},{5,6},{6,7},{7,4},{8,9},{9,10},{10,1... | collective-permute-start | bytes 2359304 | tf_op jit(solution)/shard_map/ppermute | solution.py:30
  136.3 17.2 %collective-permute-start.15 = (bf16[128,1536]{1,0:T(8,128)(2,1)S(1)}, bf16[128,1536]{1,0:T(8,128)(2,1)S(1)}, u32[]{:S(2)}, u32[]{:S(2)}) collective-permute-start(bf16[128,1536]{1,0:T(8,128)(2,1)S(1)} %get-tuple-element.95), channel_id=1, source_target_pairs={{0,3},{1,0},{2,1},{3,2},{4,7},{5,4},{6,5},{7,6},{8,11},{9,8},{10,9... | collective-permute-start | bytes 1179656 | tf_op jit(solution)/shard_map/ppermute | solution.py:30
  137.2 19.7 %collective-permute-start.13 = (bf16[128,1536]{1,0:T(8,128)(2,1)S(1)}, bf16[128,1536]{1,0:T(8,128)(2,1)S(1)}, u32[]{:S(2)}, u32[]{:S(2)}) collective-permute-start(bf16[128,1536]{1,0:T(8,128)(2,1)S(1)} %get-tuple-element.92), channel_id=1, source_target_pairs={{0,1},{1,2},{2,3},{3,0},{4,5},{5,6},{6,7},{7,4},{8,9},{9,10},{10,1... | collective-permute-start | bytes 1179656 | tf_op jit(solution)/shard_map/ppermute | solution.py:30
  158.5 28.2 %all-to-all-start.3 = ((bf16[8,32,1536]{2,1,0:T(8,128)(2,1)}), bf16[8,32,1536]{2,1,0:T(8,128)(2,1)S(1)}, u32[]{:S(2)}, u32[]{:S(2)}) async-start(bf16[8,32,1536]{2,1,0:T(8,128)(2,1)} %bitcast.18), calls=%async_computation.3 | async-start | bytes 1572864 | tf_op jit(solution)/shard_map/all_to_all | solution.py:35
  165.2 16.8 %collective-permute-start.16 = (bf16[256,1536]{1,0:T(8,128)(2,1)}, bf16[256,1536]{1,0:T(8,128)(2,1)S(1)}, u32[]{:S(2)}, u32[]{:S(2)}) collective-permute-start(bf16[256,1536]{1,0:T(8,128)(2,1)} %copy-done.13), channel_id=1, source_target_pairs={{0,3},{1,0},{2,1},{3,2},{4,7},{5,4},{6,5},{7,6},{8,11},{9,8},{10,9... | collective-permute-start | bytes 2359304 | tf_op jit(solution)/shard_map/ppermute | solution.py:30
  166.4 16.8 %collective-permute-start.14 = (bf16[256,1536]{1,0:T(8,128)(2,1)S(1)}, bf16[256,1536]{1,0:T(8,128)(2,1)S(1)}, u32[]{:S(2)}, u32[]{:S(2)}) collective-permute-start(bf16[256,1536]{1,0:T(8,128)(2,1)S(1)} %get-tuple-element.93), channel_id=1, source_target_pairs={{0,1},{1,2},{2,3},{3,0},{4,5},{5,6},{6,7},{7,4},{8,9},{9,10},{10,1... | collective-permute-start | bytes 2359304 | tf_op jit(solution)/shard_map/ppermute | solution.py:30
  186.7 32.5 %all-to-all-start.4 = ((bf16[8,32,1536]{2,1,0:T(8,128)(2,1)}), bf16[8,32,1536]{2,1,0:T(8,128)(2,1)S(1)}, u32[]{:S(2)}, u32[]{:S(2)}) async-start(bf16[8,32,1536]{2,1,0:T(8,128)(2,1)} %bitcast.20), calls=%async_computation.4 | async-start | bytes 1572864 | tf_op jit(solution)/shard_map/all_to_all | solution.py:35
  193.6 14.4 %collective-permute-start.19 = (bf16[256,1536]{1,0:T(8,128)(2,1)}, bf16[256,1536]{1,0:T(8,128)(2,1)S(1)}, u32[]{:S(2)}, u32[]{:S(2)}) collective-permute-start(bf16[256,1536]{1,0:T(8,128)(2,1)} %bitcast.24), channel_id=1, source_target_pairs={{0,3},{1,0},{2,1},{3,2},{4,7},{5,4},{6,5},{7,6},{8,11},{9,8},{10,9... | collective-permute-start | bytes 2359304 | tf_op jit(solution)/shard_map/ppermute | solution.py:30
  194.1 15.6 %collective-permute-start.20 = (bf16[256,1536]{1,0:T(8,128)(2,1)}, bf16[256,1536]{1,0:T(8,128)(2,1)S(1)}, u32[]{:S(2)}, u32[]{:S(2)}) collective-permute-start(bf16[256,1536]{1,0:T(8,128)(2,1)} %bitcast.69), channel_id=1, source_target_pairs={{0,1},{1,2},{2,3},{3,0},{4,5},{5,6},{6,7},{7,4},{8,9},{9,10},{10,1... | collective-permute-start | bytes 2359304 | tf_op jit(solution)/shard_map/ppermute | solution.py:30
  (49 other events, 358.2 us)

commit v5 on v3

--- a/solution.py
+++ b/solution.py
@@ -487,7 +487,7 @@
     rows_fwd = call(
         functools.partial(pick_forward_kernel, cap_rows),
         rows_shape,
-        [after(arrival, tagged_top, tagged_bottom), gain, route_fwd[0]],
+        [after(arrival, tagged_left_top, tagged_right_bottom), gain, route_fwd[0]],
         pick_flops,
     )[0]
 

time: 215 us -> 218 us (1.014)
  waiting for transfers between devices: 79.3 us -> 84.4 us
    all_to_all x5, waiting for transfers between devices: 14.3 us -> 17.2 us  [exchange(): lax.all_to_all(block, 'expert', split_axis=0, concat_axis=0, tiled=True,...]
    unnamed x95 -> x91, local copies, waits for them, and re-layouts: 23 us -> 23.7 us
  transfers between devices with their start and end apart: 27 -> 27, of which waited for: 13 -> 12; matrix products, arithmetic and copies ran while one was open for 2% -> 1% of each run, Pallas kernels for 20% -> 20%
where the time goes in v5:
time: 218 us; the launch traced here: 217 us
  waiting for transfers between devices  84.4 us (39%)
  starting transfers between devices  62.8 us (29%)
  Pallas kernels  45.4 us (21%)
  local copies, waits for them, and re-layouts  23.7 us (11%)
    ppermute x20, waiting for transfers between devices, turned(): return lax.ppermute(block, 'expert', route)  66.7 us
    pallas_call x23, Pallas kernels, call(): pl.pallas_call(kernel, out_shape=out_shapes, cost_estimate=pl.CostEstimat...  45.4 us
    all_to_all x5, starting transfers between devices, exchange(): lax.all_to_all(block, 'expert', split_axis=0, concat_axis=0, tiled=True,...  31.6 us
    ppermute x20, starting transfers between devices, turned(): return lax.ppermute(block, 'expert', route)  28.8 us
    unnamed x91, local copies, waits for them, and re-layouts  23.7 us
    all_to_all x5, waiting for transfers between devices, exchange(): lax.all_to_all(block, 'expert', split_axis=0, concat_axis=0, tiled=True,...  17.2 us
  transfers between devices with their start and end apart: 27, of which 12 were waited for; matrix products, arithmetic and copies ran while one was open for 1% of the time, Pallas kernels for 20%

profile of v5, /device:TPU:6, one launch (start us, length us, event | category | flops | bytes accessed | tf_op | source)
XLA Modules:
  0.0 217.3 jit_solution(2795795926741866223)
XLA Ops:
  8.2 8.6 %all-to-all-start = ((bf16[8,32,1536]{2,1,0:T(8,128)(2,1)}), bf16[8,32,1536]{2,1,0:T(8,128)(2,1)S(1)}, u32[]{:S(2)}, u32[]{:S(2)}) async-start(bf16[8,32,1536]{2,1,0:T(8,128)(2,1)} %bitcast.48), calls=%async_computation | async-start | bytes 1572864 | tf_op jit(solution)/shard_map/all_to_all | solution.py:35
  16.8 3.0 %collective-permute-start.3 = (bf16[128,1664]{1,0:T(8,128)(2,1)}, bf16[128,1664]{1,0:T(8,128)(2,1)}, u32[]{:S(2)}, u32[]{:S(2)}) collective-permute-start(bf16[128,1664]{1,0:T(8,128)(2,1)} %copy-done.11), channel_id=1, source_target_pairs={{0,3},{1,0},{2,1},{3,2},{4,7},{5,4},{6,5},{7,6},{8,11},{9,8},{10,9... | collective-permute-start | bytes 1277960 | tf_op jit(solution)/shard_map/ppermute | solution.py:30
  22.5 6.4 %collective-permute-done.3.right_ref = bf16[128,1664]{1,0:T(8,128)(2,1)} collective-permute-done((bf16[128,1664]{1,0:T(8,128)(2,1)}, bf16[128,1664]{1,0:T(8,128)(2,1)}, u32[]{:S(2)}, u32[]{:S(2)}) %collective-permute-start.3) | collective-permute-done | bytes 426016 | tf_op jit(solution)/shard_map/ppermute | solution.py:30
  28.9 4.0 %collective-permute-done.2.left_ref = bf16[128,1664]{1,0:T(8,128)(2,1)} collective-permute-done((bf16[128,1664]{1,0:T(8,128)(2,1)}, bf16[128,1664]{1,0:T(8,128)(2,1)}, u32[]{:S(2)}, u32[]{:S(2)}) %collective-permute-start.2) | collective-permute-done | bytes 426016 | tf_op jit(solution)/shard_map/ppermute | solution.py:30
  38.0 3.2 %all-to-all-done = bf16[8,32,1536]{2,1,0:T(8,128)(2,1)S(1)} async-done(((bf16[8,32,1536]{2,1,0:T(8,128)(2,1)}), bf16[8,32,1536]{2,1,0:T(8,128)(2,1)S(1)}, u32[]{:S(2)}, u32[]{:S(2)}) %all-to-all-start) | async-done | bytes 786464 | tf_op jit(solution)/shard_map/all_to_all | solution.py:35
  41.2 4.3 %all-to-all-start.1 = ((bf16[8,32,1536]{2,1,0:T(8,128)(2,1)}), bf16[8,32,1536]{2,1,0:T(8,128)(2,1)}, u32[]{:S(2)}, u32[]{:S(2)}) async-start(bf16[8,32,1536]{2,1,0:T(8,128)(2,1)} %bitcast.47), calls=%async_computation.1 | async-start | bytes 1572864 | tf_op jit(solution)/shard_map/all_to_all | solution.py:35
  49.1 2.9 %collective-permute-start.9 = (bf16[64,1664]{1,0:T(8,128)(2,1)}, bf16[64,1664]{1,0:T(8,128)(2,1)}, u32[]{:S(2)}, u32[]{:S(2)}) collective-permute-start(bf16[64,1664]{1,0:T(8,128)(2,1)} %copy-done.39), channel_id=1, source_target_pairs={{0,3},{1,0},{2,1},{3,2},{4,7},{5,4},{6,5},{7,6},{8,11},{9,8},{10,9... | collective-permute-start | bytes 638984 | tf_op jit(solution)/shard_map/ppermute | solution.py:30
  58.7 12.6 %collective-permute-done.8.top_ref = bf16[64,1664]{1,0:T(8,128)(2,1)} collective-permute-done((bf16[64,1664]{1,0:T(8,128)(2,1)}, bf16[64,1664]{1,0:T(8,128)(2,1)}, u32[]{:S(2)}, u32[]{:S(2)}) %collective-permute-start.8) | collective-permute-done | bytes 213024 | tf_op jit(solution)/shard_map/ppermute | solution.py:30
  77.7 6.9 %all-to-all-start.2 = ((bf16[8,128,1536]{2,1,0:T(8,128)(2,1)}), bf16[8,128,1536]{2,1,0:T(8,128)(2,1)}, u32[]{:S(2)}, u32[]{:S(2)}) async-start(bf16[8,128,1536]{2,1,0:T(8,128)(2,1)} %bitcast.42), calls=%async_computation.2 | async-start | bytes 6291456 | tf_op jit(solution)/shard_map/all_to_all | solution.py:35
  84.7 3.0 %collective-permute-start.7 = (bf16[256,1536]{1,0:T(8,128)(2,1)}, bf16[256,1536]{1,0:T(8,128)(2,1)S(1)}, u32[]{:S(2)}, u32[]{:S(2)}) collective-permute-start(bf16[256,1536]{1,0:T(8,128)(2,1)} %bitcast.13.refs_0_), channel_id=1, source_target_pairs={{0,3},{1,0},{2,1},{3,2},{4,7},{5,4},{6,5},{7,6},{8,11},{9,8},{10,9... | collective-permute-start | bytes 2359304 | tf_op jit(solution)/shard_map/ppermute | solution.py:30
  87.8 3.1 %collective-permute-start.11 = (bf16[128,1536]{1,0:T(8,128)(2,1)}, bf16[128,1536]{1,0:T(8,128)(2,1)S(1)}, u32[]{:S(2)}, u32[]{:S(2)}) collective-permute-start(bf16[128,1536]{1,0:T(8,128)(2,1)} %get-tuple-element.65), channel_id=1, source_target_pairs={{0,3},{1,0},{2,1},{3,2},{4,7},{5,4},{6,5},{7,6},{8,11},{9,8},{10,9... | collective-permute-start | bytes 1179656 | tf_op jit(solution)/shard_map/ppermute | solution.py:30
  94.0 4.7 %shard_map.153 = (bf16[256,768]{1,0:T(8,128)(2,1)S(1)}, bf16[256,768]{1,0:T(8,128)(2,1)S(1)}, bf16[256,768]{1,0:T(8,128)(2,1)S(1)}, bf16[256,768]{1,0:T(8,128)(2...) custom-call(s32[1]{0:T(128)} %bitcast.14.place_ref, bf16[1536,768]{1,0:T(8,128)(2,1)S(1)} %bitcast.27, ...), custom_call_target="tpu_custom_call" | custom-call | flops 2415919104 | bytes 12582916 | tf_op jit(solution)/shard_map/pallas_call | solution.py:69
  98.7 16.7 %collective-permute-done.10.refs_0_.refs_7_ = bf16[128,1536]{1,0:T(8,128)(2,1)S(1)} collective-permute-done((bf16[128,1536]{1,0:T(8,128)(2,1)}, bf16[128,1536]{1,0:T(8,128)(2,1)S(1)}, u32[]{:S(2)}, u32[]{:S(2)}) %collective-permute-start.10) | collective-permute-done | bytes 393248 | tf_op jit(solution)/shard_map/ppermute | solution.py:30
  115.4 3.2 %shard_map.157 = (bf16[256,768]{1,0:T(8,128)(2,1)S(1)}, bf16[256,768]{1,0:T(8,128)(2,1)S(1)}, bf16[128,1536]{1,0:T(8,128)(2,1)S(1)}, bf16[128,1536]{1,0:T(8,128)(2,1)S(1)}) custom-call(s32[1]{0:T(128)} %bitcast.14.place_ref, bf16[1536,768]{1,0:T(8,128)(2,1)S(1)} %bitcast.28, bf16[768,1536]{1,0:T(8,128)(2,1)S(1)} %bitcast.34, ...), custom_call_target="tpu_custom_call" | custom-call | flops 1207959552 | bytes 8650756 | tf_op jit(solution)/shard_map/pallas_call | solution.py:69
  127.1 6.0 %shard_map.158 = bf16[768,1536]{1,0:T(8,128)(2,1)} custom-call(bf16[256,768]{1,0:T(8,128)(2,1)S(1)} %copy-done.38, bf16[256,768]{1,0:T(8,128)(2,1)S(1)} %get-tuple-element.68.refs_1_, bf16[256,768]{1,0:T(8,128)(2,1)S(1)} %get-tuple-element.69.refs_2_, bf16[256,768]{1,0:T(8,128)(2,1)S(1)} %get-tuple-element.70.refs_3_, bf16[256,1536]{1,0:T(8,128)(2,1)S(1)} %bitcast.46, ...), custom_call_target="tpu_custom_call" | custom-call | flops 2415919104 | bytes 7077888 | tf_op jit(solution)/shard_map/pallas_call | solution.py:69
  140.4 3.0 %shard_map.161 = (bf16[256,1536]{1,0:T(8,128)(2,1)S(1)}, bf16[256,1536]{1,0:T(8,128)(2,1)S(1)}) custom-call(bf16[1536,768]{1,0:T(8,128)(2,1)S(1)} %bitcast.30, bf16[768,1536]{1,0:T(8,128)(2,1)S(1)} %bitcast.36, bf16[256,1536]{1,0:T(8,128)(2,1)S(1)} %collective-permute-done.6.left_ref.refs_0_, bf16[256,1536]{1,0:T(8,128)(2,1)S(1)} %collective-permute-done.7.right_ref.refs_1_), custom_call_target="tpu_custom_call" | custom-call | flops 2415919104 | bytes 7864320 | tf_op jit(solution)/shard_map/pallas_call | solution.py:69
  145.2 3.0 %collective-permute-start.18 = (bf16[128,1536]{1,0:T(8,128)(2,1)S(1)}, bf16[128,1536]{1,0:T(8,128)(2,1)S(1)}, u32[]{:S(2)}, u32[]{:S(2)}) collective-permute-start(bf16[128,1536]{1,0:T(8,128)(2,1)S(1)} %get-tuple-element.86), channel_id=1, source_target_pairs={{0,3},{1,0},{2,1},{3,2},{4,7},{5,4},{6,5},{7,6},{8,11},{9,8},{10,9... | collective-permute-start | bytes 1179656 | tf_op jit(solution)/shard_map/ppermute | solution.py:30
  148.2 16.3 %collective-permute-done.16.more_ref = bf16[128,1536]{1,0:T(8,128)(2,1)S(1)} collective-permute-done((bf16[128,1536]{1,0:T(8,128)(2,1)S(1)}, bf16[128,1536]{1,0:T(8,128)(2,1)S(1)}, u32[]{:S(2)}, u32[]{:S(2)}) %collective-permute-start.16) | collective-permute-done | bytes 393248 | tf_op jit(solution)/shard_map/ppermute | solution.py:30
  167.2 6.4 %all-to-all-start.3 = ((bf16[8,32,1536]{2,1,0:T(8,128)(2,1)}), bf16[8,32,1536]{2,1,0:T(8,128)(2,1)}, u32[]{:S(2)}, u32[]{:S(2)}) async-start(bf16[8,32,1536]{2,1,0:T(8,128)(2,1)} %bitcast.18), calls=%async_computation.3 | async-start | bytes 1572864 | tf_op jit(solution)/shard_map/all_to_all | solution.py:35
  174.0 2.9 %collective-permute-start.19 = (bf16[256,1536]{1,0:T(8,128)(2,1)}, bf16[256,1536]{1,0:T(8,128)(2,1)S(1)}, u32[]{:S(2)}, u32[]{:S(2)}) collective-permute-start(bf16[256,1536]{1,0:T(8,128)(2,1)} %copy-done.25), channel_id=1, source_target_pairs={{0,3},{1,0},{2,1},{3,2},{4,7},{5,4},{6,5},{7,6},{8,11},{9,8},{10,9... | collective-permute-start | bytes 2359304 | tf_op jit(solution)/shard_map/ppermute | solution.py:30
  176.9 6.8 %shard_map.164 = bf16[1536,768]{1,0:T(8,128)(2,1)} custom-call(bf16[8,4,32,1536]{3,2,1,0:T(8,128)(2,1)} %bitcast.17.rows_ref, bf16[256,768]{1,0:T(8,128)(2,1)S(1)} %copy-done.32, bf16[256,768]{1,0:T(8,128)(2,1)S(1)} %get-tuple-element.82.refs_1_, bf16[256,768]{1,0:T(8,128)(2,1)S(1)} %copy-done.34, bf16[256,768]{1,0:T(8,128)(2,1)S(1)} %copy-done.36), custom_call_target="tpu_custom_call" | custom-call | flops 2415919104 | bytes 7077888 | tf_op jit(solution)/shard_map/pallas_call | solution.py:69
  183.7 6.2 %collective-permute-done.17.two_ref = bf16[256,1536]{1,0:T(8,128)(2,1)S(1)} collective-permute-done((bf16[256,1536]{1,0:T(8,128)(2,1)}, bf16[256,1536]{1,0:T(8,128)(2,1)S(1)}, u32[]{:S(2)}, u32[]{:S(2)}) %collective-permute-start.17) | collective-permute-done | bytes 786464 | tf_op jit(solution)/shard_map/ppermute | solution.py:30
  192.7 5.4 %all-to-all-start.4 = ((bf16[8,32,1536]{2,1,0:T(8,128)(2,1)}), bf16[8,32,1536]{2,1,0:T(8,128)(2,1)S(1)}, u32[]{:S(2)}, u32[]{:S(2)}) async-start(bf16[8,32,1536]{2,1,0:T(8,128)(2,1)} %bitcast.20), calls=%async_computation.4 | async-start | bytes 1572864 | tf_op jit(solution)/shard_map/all_to_all | solution.py:35
  203.3 12.4 %all-to-all-done.4 = bf16[8,32,1536]{2,1,0:T(8,128)(2,1)S(1)} async-done(((bf16[8,32,1536]{2,1,0:T(8,128)(2,1)}), bf16[8,32,1536]{2,1,0:T(8,128)(2,1)S(1)}, u32[]{:S(2)}, u32[]{:S(2)}) %all-to-all-start.4) | async-done | bytes 786464 | tf_op jit(solution)/shard_map/all_to_all | solution.py:35
  (144 shorter events, 65.3 us)
Async XLA Ops:
  8.2 33.0 %all-to-all-start = ((bf16[8,32,1536]{2,1,0:T(8,128)(2,1)}), bf16[8,32,1536]{2,1,0:T(8,128)(2,1)S(1)}, u32[]{:S(2)}, u32[]{:S(2)}) async-start(bf16[8,32,1536]{2,1,0:T(8,128)(2,1)} %bitcast.48), calls=%async_computation | async-start | bytes 1572864 | tf_op jit(solution)/shard_map/all_to_all | solution.py:35
  19.8 15.6 %collective-permute-start.1 = (bf16[1,128,1536]{2,1,0:T(8,128)(2,1)}, bf16[1,128,1536]{2,1,0:T(8,128)(2,1)S(1)}, u32[]{:S(2)}, u32[]{:S(2)}) collective-permute-start(bf16[1,128,1536]{2,1,0:T(8,128)(2,1)} %param.12), channel_id=1, source_target_pairs={{224,0},{0,32},{32,64},{64,96},{96,128},{128,160},{160,192},{192,2... | collective-permute-start | bytes 1179656 | tf_op jit(solution)/shard_map/ppermute | solution.py:21
  41.2 36.6 %all-to-all-start.1 = ((bf16[8,32,1536]{2,1,0:T(8,128)(2,1)}), bf16[8,32,1536]{2,1,0:T(8,128)(2,1)}, u32[]{:S(2)}, u32[]{:S(2)}) async-start(bf16[8,32,1536]{2,1,0:T(8,128)(2,1)} %bitcast.47), calls=%async_computation.1 | async-start | bytes 1572864 | tf_op jit(solution)/shard_map/all_to_all | solution.py:35
  45.5 30.2 %collective-permute-start.4 = (bf16[256,1536]{1,0:T(8,128)(2,1)S(1)}, bf16[256,1536]{1,0:T(8,128)(2,1)}, u32[]{:S(2)}, u32[]{:S(2)}) collective-permute-start(bf16[256,1536]{1,0:T(8,128)(2,1)S(1)} %bitcast.43), channel_id=1, source_target_pairs={{0,1},{1,2},{2,3},{3,0},{4,5},{5,6},{6,7},{7,4},{8,9},{9,10},{10,1... | collective-permute-start | bytes 2359304 | tf_op jit(solution)/shard_map/ppermute | solution.py:30
  47.1 28.6 %collective-permute-start.5 = (bf16[256,1536]{1,0:T(8,128)(2,1)S(1)}, bf16[256,1536]{1,0:T(8,128)(2,1)}, u32[]{:S(2)}, u32[]{:S(2)}) collective-permute-start(bf16[256,1536]{1,0:T(8,128)(2,1)S(1)} %bitcast.44), channel_id=1, source_target_pairs={{0,3},{1,0},{2,1},{3,2},{4,7},{5,4},{6,5},{7,6},{8,11},{9,8},{10,9... | collective-permute-start | bytes 2359304 | tf_op jit(solution)/shard_map/ppermute | solution.py:30
  48.8 22.5 %collective-permute-start.8 = (bf16[64,1664]{1,0:T(8,128)(2,1)}, bf16[64,1664]{1,0:T(8,128)(2,1)}, u32[]{:S(2)}, u32[]{:S(2)}) collective-permute-start(bf16[64,1664]{1,0:T(8,128)(2,1)} %copy-done.40), channel_id=1, source_target_pairs={{0,1},{1,2},{2,3},{3,0},{4,5},{5,6},{6,7},{7,4},{8,9},{9,10},{10,1... | collective-permute-start | bytes 638984 | tf_op jit(solution)/shard_map/ppermute | solution.py:30
  49.1 22.2 %collective-permute-start.9 = (bf16[64,1664]{1,0:T(8,128)(2,1)}, bf16[64,1664]{1,0:T(8,128)(2,1)}, u32[]{:S(2)}, u32[]{:S(2)}) collective-permute-start(bf16[64,1664]{1,0:T(8,128)(2,1)} %copy-done.39), channel_id=1, source_target_pairs={{0,3},{1,0},{2,1},{3,2},{4,7},{5,4},{6,5},{7,6},{8,11},{9,8},{10,9... | collective-permute-start | bytes 638984 | tf_op jit(solution)/shard_map/ppermute | solution.py:30
  77.7 89.5 %all-to-all-start.2 = ((bf16[8,128,1536]{2,1,0:T(8,128)(2,1)}), bf16[8,128,1536]{2,1,0:T(8,128)(2,1)}, u32[]{:S(2)}, u32[]{:S(2)}) async-start(bf16[8,128,1536]{2,1,0:T(8,128)(2,1)} %bitcast.42), calls=%async_computation.2 | async-start | bytes 6291456 | tf_op jit(solution)/shard_map/all_to_all | solution.py:35
  84.7 34.4 %collective-permute-start.7 = (bf16[256,1536]{1,0:T(8,128)(2,1)}, bf16[256,1536]{1,0:T(8,128)(2,1)S(1)}, u32[]{:S(2)}, u32[]{:S(2)}) collective-permute-start(bf16[256,1536]{1,0:T(8,128)(2,1)} %bitcast.13.refs_0_), channel_id=1, source_target_pairs={{0,3},{1,0},{2,1},{3,2},{4,7},{5,4},{6,5},{7,6},{8,11},{9,8},{10,9... | collective-permute-start | bytes 2359304 | tf_op jit(solution)/shard_map/ppermute | solution.py:30
  87.6 31.4 %collective-permute-start.6 = (bf16[256,1536]{1,0:T(8,128)(2,1)}, bf16[256,1536]{1,0:T(8,128)(2,1)S(1)}, u32[]{:S(2)}, u32[]{:S(2)}) collective-permute-start(bf16[256,1536]{1,0:T(8,128)(2,1)} %bitcast.13.refs_0_), channel_id=1, source_target_pairs={{0,1},{1,2},{2,3},{3,0},{4,5},{5,6},{6,7},{7,4},{8,9},{9,10},{10,1... | collective-permute-start | bytes 2359304 | tf_op jit(solution)/shard_map/ppermute | solution.py:30
  87.6 27.8 %collective-permute-start.10 = (bf16[128,1536]{1,0:T(8,128)(2,1)}, bf16[128,1536]{1,0:T(8,128)(2,1)S(1)}, u32[]{:S(2)}, u32[]{:S(2)}) collective-permute-start(bf16[128,1536]{1,0:T(8,128)(2,1)} %get-tuple-element.62), channel_id=1, source_target_pairs={{0,1},{1,2},{2,3},{3,0},{4,5},{5,6},{6,7},{7,4},{8,9},{9,10},{10,1... | collective-permute-start | bytes 1179656 | tf_op jit(solution)/shard_map/ppermute | solution.py:30
  87.8 27.6 %collective-permute-start.11 = (bf16[128,1536]{1,0:T(8,128)(2,1)}, bf16[128,1536]{1,0:T(8,128)(2,1)S(1)}, u32[]{:S(2)}, u32[]{:S(2)}) collective-permute-start(bf16[128,1536]{1,0:T(8,128)(2,1)} %get-tuple-element.65), channel_id=1, source_target_pairs={{0,3},{1,0},{2,1},{3,2},{4,7},{5,4},{6,5},{7,6},{8,11},{9,8},{10,9... | collective-permute-start | bytes 1179656 | tf_op jit(solution)/shard_map/ppermute | solution.py:30
  118.7 14.4 %collective-permute-start.15 = (bf16[128,1536]{1,0:T(8,128)(2,1)S(1)}, bf16[128,1536]{1,0:T(8,128)(2,1)S(1)}, u32[]{:S(2)}, u32[]{:S(2)}) collective-permute-start(bf16[128,1536]{1,0:T(8,128)(2,1)S(1)} %get-tuple-element.73), channel_id=1, source_target_pairs={{0,3},{1,0},{2,1},{3,2},{4,7},{5,4},{6,5},{7,6},{8,11},{9,8},{10,9... | collective-permute-start | bytes 1179656 | tf_op jit(solution)/shard_map/ppermute | solution.py:30
  119.4 13.6 %collective-permute-start.13 = (bf16[128,1536]{1,0:T(8,128)(2,1)S(1)}, bf16[128,1536]{1,0:T(8,128)(2,1)S(1)}, u32[]{:S(2)}, u32[]{:S(2)}) collective-permute-start(bf16[128,1536]{1,0:T(8,128)(2,1)S(1)} %get-tuple-element.54), channel_id=1, source_target_pairs={{0,1},{1,2},{2,3},{3,0},{4,5},{5,6},{6,7},{7,4},{8,9},{9,10},{10,1... | collective-permute-start | bytes 1179656 | tf_op jit(solution)/shard_map/ppermute | solution.py:30
  121.3 14.6 %collective-permute-start.14 = (bf16[128,1536]{1,0:T(8,128)(2,1)S(1)}, bf16[128,1536]{1,0:T(8,128)(2,1)S(1)}, u32[]{:S(2)}, u32[]{:S(2)}) collective-permute-start(bf16[128,1536]{1,0:T(8,128)(2,1)S(1)} %get-tuple-element.55), channel_id=1, source_target_pairs={{0,3},{1,0},{2,1},{3,2},{4,7},{5,4},{6,5},{7,6},{8,11},{9,8},{10,9... | collective-permute-start | bytes 1179656 | tf_op jit(solution)/shard_map/ppermute | solution.py:30
  122.7 15.1 %collective-permute-start.12 = (bf16[128,1536]{1,0:T(8,128)(2,1)S(1)}, bf16[128,1536]{1,0:T(8,128)(2,1)S(1)}, u32[]{:S(2)}, u32[]{:S(2)}) collective-permute-start(bf16[128,1536]{1,0:T(8,128)(2,1)S(1)} %get-tuple-element.66), channel_id=1, source_target_pairs={{0,1},{1,2},{2,3},{3,0},{4,5},{5,6},{6,7},{7,4},{8,9},{9,10},{10,1... | collective-permute-start | bytes 1179656 | tf_op jit(solution)/shard_map/ppermute | solution.py:30
  137.8 27.4 %collective-permute-start.21 = (bf16[256,1536]{1,0:T(8,128)(2,1)S(1)}, bf16[256,1536]{1,0:T(8,128)(2,1)S(1)}, u32[]{:S(2)}, u32[]{:S(2)}) collective-permute-start(bf16[256,1536]{1,0:T(8,128)(2,1)S(1)} %shard_map.160), channel_id=1, source_target_pairs={{0,3},{1,0},{2,1},{3,2},{4,7},{5,4},{6,5},{7,6},{8,11},{9,8},{10,9... | collective-permute-start | bytes 2359304 | tf_op jit(solution)/shard_map/ppermute | solution.py:30
  138.3 26.9 %collective-permute-start.20 = (bf16[256,1536]{1,0:T(8,128)(2,1)S(1)}, bf16[256,1536]{1,0:T(8,128)(2,1)S(1)}, u32[]{:S(2)}, u32[]{:S(2)}) collective-permute-start(bf16[256,1536]{1,0:T(8,128)(2,1)S(1)} %shard_map.159), channel_id=1, source_target_pairs={{0,1},{1,2},{2,3},{3,0},{4,5},{5,6},{6,7},{7,4},{8,9},{9,10},{10,1... | collective-permute-start | bytes 2359304 | tf_op jit(solution)/shard_map/ppermute | solution.py:30
  144.9 19.6 %collective-permute-start.16 = (bf16[128,1536]{1,0:T(8,128)(2,1)S(1)}, bf16[128,1536]{1,0:T(8,128)(2,1)S(1)}, u32[]{:S(2)}, u32[]{:S(2)}) collective-permute-start(bf16[128,1536]{1,0:T(8,128)(2,1)S(1)} %get-tuple-element.79), channel_id=1, source_target_pairs={{0,1},{1,2},{2,3},{3,0},{4,5},{5,6},{6,7},{7,4},{8,9},{9,10},{10,1... | collective-permute-start | bytes 1179656 | tf_op jit(solution)/shard_map/ppermute | solution.py:30
  145.2 19.6 %collective-permute-start.18 = (bf16[128,1536]{1,0:T(8,128)(2,1)S(1)}, bf16[128,1536]{1,0:T(8,128)(2,1)S(1)}, u32[]{:S(2)}, u32[]{:S(2)}) collective-permute-start(bf16[128,1536]{1,0:T(8,128)(2,1)S(1)} %get-tuple-element.86), channel_id=1, source_target_pairs={{0,3},{1,0},{2,1},{3,2},{4,7},{5,4},{6,5},{7,6},{8,11},{9,8},{10,9... | collective-permute-start | bytes 1179656 | tf_op jit(solution)/shard_map/ppermute | solution.py:30
  167.2 25.5 %all-to-all-start.3 = ((bf16[8,32,1536]{2,1,0:T(8,128)(2,1)}), bf16[8,32,1536]{2,1,0:T(8,128)(2,1)}, u32[]{:S(2)}, u32[]{:S(2)}) async-start(bf16[8,32,1536]{2,1,0:T(8,128)(2,1)} %bitcast.18), calls=%async_computation.3 | async-start | bytes 1572864 | tf_op jit(solution)/shard_map/all_to_all | solution.py:35
  173.6 16.2 %collective-permute-start.17 = (bf16[256,1536]{1,0:T(8,128)(2,1)}, bf16[256,1536]{1,0:T(8,128)(2,1)S(1)}, u32[]{:S(2)}, u32[]{:S(2)}) collective-permute-start(bf16[256,1536]{1,0:T(8,128)(2,1)} %copy-done.26), channel_id=1, source_target_pairs={{0,1},{1,2},{2,3},{3,0},{4,5},{5,6},{6,7},{7,4},{8,9},{9,10},{10,1... | collective-permute-start | bytes 2359304 | tf_op jit(solution)/shard_map/ppermute | solution.py:30
  174.0 15.9 %collective-permute-start.19 = (bf16[256,1536]{1,0:T(8,128)(2,1)}, bf16[256,1536]{1,0:T(8,128)(2,1)S(1)}, u32[]{:S(2)}, u32[]{:S(2)}) collective-permute-start(bf16[256,1536]{1,0:T(8,128)(2,1)} %copy-done.25), channel_id=1, source_target_pairs={{0,3},{1,0},{2,1},{3,2},{4,7},{5,4},{6,5},{7,6},{8,11},{9,8},{10,9... | collective-permute-start | bytes 2359304 | tf_op jit(solution)/shard_map/ppermute | solution.py:30
  192.7 23.0 %all-to-all-start.4 = ((bf16[8,32,1536]{2,1,0:T(8,128)(2,1)}), bf16[8,32,1536]{2,1,0:T(8,128)(2,1)S(1)}, u32[]{:S(2)}, u32[]{:S(2)}) async-start(bf16[8,32,1536]{2,1,0:T(8,128)(2,1)} %bitcast.20), calls=%async_computation.4 | async-start | bytes 1572864 | tf_op jit(solution)/shard_map/all_to_all | solution.py:35
  (46 other events, 399.4 us)

commit v6 on v3

--- a/solution.py
+++ b/solution.py
@@ -536,14 +536,9 @@
     left_top, right_bottom = cut_halves(left, right)
     opposite_top = turned(left_top, groups, 1)
     opposite_bottom = turned(right_bottom, groups, -1)
-    grad_w_out = weight_grad(
-        [*hidden_0, *hidden_1, *hidden_2],
-        [after(grads, left_top, right_bottom), grads_left, grads_right, grads_top, grads_bottom],
-        256,
-    )
     fwd_0 = forward_chunks([after(sent_fwd, left_top, right_bottom)], w_in_local, w_out_local, [whole])
 
-    arrived = (grad_w_out, *fwd_0, opposite_top, opposite_bottom)
+    arrived = tuple(fwd_0)
     back_to_left = add_half(back_1[1], after(back_top, *arrived), 0)
     back_to_right = add_half(back_1[0], after(back_bottom, *arrived), 1)
     back_left = turned(back_to_left, groups, 1)
@@ -553,6 +548,11 @@
     )
     fwd_2 = forward_chunks(
         [after(opposite_top, *fwd_1), opposite_bottom], w_in_local, w_out_local, [halves], split=True
+    )
+    grad_w_out = weight_grad(
+        [*hidden_0, *hidden_1, *hidden_2],
+        [after(grads, *fwd_2), grads_left, grads_right, grads_top, grads_bottom],
+        256,
     )
     fwd_top = turned(fwd_2[0], groups, 1)
     fwd_bottom = turned(fwd_2[1], groups, -1)

time: 215 us -> 220 us (1.023)
  local copies, waits for them, and re-layouts: 23 us -> 31.3 us
  waiting for transfers between devices: 79.3 us -> 71 us
  Pallas kernels: 45.6 us -> 48.5 us
  starting transfers between devices: 64.5 us -> 66.9 us
    unnamed x95 -> x117, local copies, waits for them, and re-layouts: 23 us -> 31.3 us
    all_to_all x5, waiting for transfers between devices: 14.3 us -> 7.07 us  [exchange(): lax.all_to_all(block, 'expert', split_axis=0, concat_axis=0, tiled=True,...]
    pallas_call x23, Pallas kernels: 45.6 us -> 48.5 us  [call(): pl.pallas_call(kernel, out_shape=out_shapes, cost_estimate=pl.CostEstimat...]
  transfers between devices with their start and end apart: 27 -> 27, of which waited for: 13 -> 16; matrix products, arithmetic and copies ran while one was open for 2% -> 2% of each run, Pallas kernels for 20% -> 21%
where the time goes in v6:
time: 220 us; the launch traced here: 219 us
  waiting for transfers between devices  71 us (32%)
  starting transfers between devices  66.9 us (30%)
  Pallas kernels  48.5 us (22%)
  local copies, waits for them, and re-layouts  31.3 us (14%)
    ppermute x20, waiting for transfers between devices, turned(): return lax.ppermute(block, 'expert', route)  63.4 us
    pallas_call x23, Pallas kernels, call(): pl.pallas_call(kernel, out_shape=out_shapes, cost_estimate=pl.CostEstimat...  48.5 us
    all_to_all x5, starting transfers between devices, exchange(): lax.all_to_all(block, 'expert', split_axis=0, concat_axis=0, tiled=True,...  34.6 us
    unnamed x117, local copies, waits for them, and re-layouts  31.3 us
    ppermute x20, starting transfers between devices, turned(): return lax.ppermute(block, 'expert', route)  30 us
    all_to_all x5, waiting for transfers between devices, exchange(): lax.all_to_all(block, 'expert', split_axis=0, concat_axis=0, tiled=True,...  7.07 us
  transfers between devices with their start and end apart: 27, of which 16 were waited for; matrix products, arithmetic and copies ran while one was open for 2% of the time, Pallas kernels for 21%

profile of v6, /device:TPU:6, one launch (start us, length us, event | category | flops | bytes accessed | tf_op | source)
XLA Modules:
  0.0 218.7 jit_solution(17452390748596193943)
XLA Ops:
  8.1 8.6 %all-to-all-start = ((bf16[8,32,1536]{2,1,0:T(8,128)(2,1)}), bf16[8,32,1536]{2,1,0:T(8,128)(2,1)S(1)}, u32[]{:S(2)}, u32[]{:S(2)}) async-start(bf16[8,32,1536]{2,1,0:T(8,128)(2,1)} %bitcast.48), calls=%async_computation | async-start | bytes 1572864 | tf_op jit(solution)/shard_map/all_to_all | solution.py:35
  16.7 3.0 %collective-permute-start.3 = (bf16[128,1664]{1,0:T(8,128)(2,1)}, bf16[128,1664]{1,0:T(8,128)(2,1)S(1)}, u32[]{:S(2)}, u32[]{:S(2)}) collective-permute-start(bf16[128,1664]{1,0:T(8,128)(2,1)} %copy-done.12), channel_id=1, source_target_pairs={{0,3},{1,0},{2,1},{3,2},{4,7},{5,4},{6,5},{7,6},{8,11},{9,8},{10,9... | collective-permute-start | bytes 1277960 | tf_op jit(solution)/shard_map/ppermute | solution.py:30
  21.8 7.1 %collective-permute-done.3.right_ref = bf16[128,1664]{1,0:T(8,128)(2,1)S(1)} collective-permute-done((bf16[128,1664]{1,0:T(8,128)(2,1)}, bf16[128,1664]{1,0:T(8,128)(2,1)S(1)}, u32[]{:S(2)}, u32[]{:S(2)}) %collective-permute-start.3) | collective-permute-done | bytes 426016 | tf_op jit(solution)/shard_map/ppermute | solution.py:30
  28.9 3.9 %collective-permute-done.2.left_ref = bf16[128,1664]{1,0:T(8,128)(2,1)S(1)} collective-permute-done((bf16[128,1664]{1,0:T(8,128)(2,1)}, bf16[128,1664]{1,0:T(8,128)(2,1)S(1)}, u32[]{:S(2)}, u32[]{:S(2)}) %collective-permute-start.2) | collective-permute-done | bytes 426016 | tf_op jit(solution)/shard_map/ppermute | solution.py:30
  34.9 3.2 %collective-permute-start.5 = (bf16[64,1664]{1,0:T(8,128)(2,1)}, bf16[64,1664]{1,0:T(8,128)(2,1)}, u32[]{:S(2)}, u32[]{:S(2)}) collective-permute-start(bf16[64,1664]{1,0:T(8,128)(2,1)} %get-tuple-element.49), channel_id=1, source_target_pairs={{0,3},{1,0},{2,1},{3,2},{4,7},{5,4},{6,5},{7,6},{8,11},{9,8},{10,9... | collective-permute-start | bytes 638984 | tf_op jit(solution)/shard_map/ppermute | solution.py:30
  38.8 5.6 %collective-permute-done.4.top_ref = bf16[64,1664]{1,0:T(8,128)(2,1)} collective-permute-done((bf16[64,1664]{1,0:T(8,128)(2,1)}, bf16[64,1664]{1,0:T(8,128)(2,1)}, u32[]{:S(2)}, u32[]{:S(2)}) %collective-permute-start.4) | collective-permute-done | bytes 213024 | tf_op jit(solution)/shard_map/ppermute | solution.py:30
  48.0 7.5 %all-to-all-start.1 = ((bf16[8,32,1536]{2,1,0:T(8,128)(2,1)}), bf16[8,32,1536]{2,1,0:T(8,128)(2,1)}, u32[]{:S(2)}, u32[]{:S(2)}) async-start(bf16[8,32,1536]{2,1,0:T(8,128)(2,1)} %bitcast.47), calls=%async_computation.1 | async-start | bytes 1572864 | tf_op jit(solution)/shard_map/all_to_all | solution.py:35
  55.5 3.2 %collective-permute-start.7 = (bf16[256,1536]{1,0:T(8,128)(2,1)S(1)}, bf16[256,1536]{1,0:T(8,128)(2,1)}, u32[]{:S(2)}, u32[]{:S(2)}) collective-permute-start(bf16[256,1536]{1,0:T(8,128)(2,1)S(1)} %bitcast.44), channel_id=1, source_target_pairs={{0,3},{1,0},{2,1},{3,2},{4,7},{5,4},{6,5},{7,6},{8,11},{9,8},{10,9... | collective-permute-start | bytes 2359304 | tf_op jit(solution)/shard_map/ppermute | solution.py:30
  69.7 6.3 %collective-permute-done.6.refs_0_.left_ref.refs_5_ = bf16[256,1536]{1,0:T(8,128)(2,1)} collective-permute-done((bf16[256,1536]{1,0:T(8,128)(2,1)S(1)}, bf16[256,1536]{1,0:T(8,128)(2,1)}, u32[]{:S(2)}, u32[]{:S(2)}) %collective-permute-start.6) | collective-permute-done | bytes 786464 | tf_op jit(solution)/shard_map/ppermute | solution.py:30
  78.9 6.7 %all-to-all-start.2 = ((bf16[8,128,1536]{2,1,0:T(8,128)(2,1)}), bf16[8,128,1536]{2,1,0:T(8,128)(2,1)}, u32[]{:S(2)}, u32[]{:S(2)}) async-start(bf16[8,128,1536]{2,1,0:T(8,128)(2,1)} %bitcast.42), calls=%async_computation.2 | async-start | bytes 6291456 | tf_op jit(solution)/shard_map/all_to_all | solution.py:35
  88.5 3.3 %collective-permute-start.11 = (bf16[128,1536]{1,0:T(8,128)(2,1)}, bf16[128,1536]{1,0:T(8,128)(2,1)S(1)}, u32[]{:S(2)}, u32[]{:S(2)}) collective-permute-start(bf16[128,1536]{1,0:T(8,128)(2,1)} %copy-done.52), channel_id=1, source_target_pairs={{0,3},{1,0},{2,1},{3,2},{4,7},{5,4},{6,5},{7,6},{8,11},{9,8},{10,9... | collective-permute-start | bytes 1179656 | tf_op jit(solution)/shard_map/ppermute | solution.py:30
  94.8 4.7 %shard_map.153 = (bf16[256,768]{1,0:T(8,128)(2,1)S(1)}, bf16[256,768]{1,0:T(8,128)(2,1)S(1)}, bf16[256,768]{1,0:T(8,128)(2,1)S(1)}, bf16[256,768]{1,0:T(8,128)(2...) custom-call(s32[1]{0:T(128)} %bitcast.14.place_ref, bf16[1536,768]{1,0:T(8,128)(2,1)S(1)} %bitcast.27, ...), custom_call_target="tpu_custom_call" | custom-call | flops 2415919104 | bytes 12582916 | tf_op jit(solution)/shard_map/pallas_call | solution.py:69
  101.9 13.6 %collective-permute-done.10.refs_0_.refs_7_ = bf16[128,1536]{1,0:T(8,128)(2,1)S(1)} collective-permute-done((bf16[128,1536]{1,0:T(8,128)(2,1)}, bf16[128,1536]{1,0:T(8,128)(2,1)S(1)}, u32[]{:S(2)}, u32[]{:S(2)}) %collective-permute-start.10) | collective-permute-done | bytes 393248 | tf_op jit(solution)/shard_map/ppermute | solution.py:30
  115.5 3.2 %shard_map.157 = (bf16[256,768]{1,0:T(8,128)(2,1)S(1)}, bf16[256,768]{1,0:T(8,128)(2,1)S(1)}, bf16[128,1536]{1,0:T(8,128)(2,1)S(1)}, bf16[128,1536]{1,0:T(8,128)(2,1)S(1)}) custom-call(s32[1]{0:T(128)} %bitcast.14.place_ref, bf16[1536,768]{1,0:T(8,128)(2,1)S(1)} %bitcast.28, bf16[768,1536]{1,0:T(8,128)(2,1)S(1)} %bitcast.34, ...), custom_call_target="tpu_custom_call" | custom-call | flops 1207959552 | bytes 8650756 | tf_op jit(solution)/shard_map/pallas_call | solution.py:69
  121.4 3.2 %collective-permute-start.15 = (bf16[128,1536]{1,0:T(8,128)(2,1)S(1)}, bf16[128,1536]{1,0:T(8,128)(2,1)S(1)}, u32[]{:S(2)}, u32[]{:S(2)}) collective-permute-start(bf16[128,1536]{1,0:T(8,128)(2,1)S(1)} %get-tuple-element.55), channel_id=1, source_target_pairs={{0,3},{1,0},{2,1},{3,2},{4,7},{5,4},{6,5},{7,6},{8,11},{9,8},{10,9... | collective-permute-start | bytes 1179656 | tf_op jit(solution)/shard_map/ppermute | solution.py:30
  135.0 3.9 %shard_map.160 = (bf16[256,1536]{1,0:T(8,128)(2,1)S(1)}, bf16[256,1536]{1,0:T(8,128)(2,1)}) custom-call(bf16[1536,768]{1,0:T(8,128)(2,1)S(1)} %bitcast.30, bf16[768,1536]{1,0:T(8,128)(2,1)S(1)} %bitcast.36, bf16[256,1536]{1,0:T(8,128)(2,1)S(1)} %collective-permute-done.8.left_ref.refs_0_, bf16[256,1536]{1,0:T(8,128)(2,1)S(1)} %collective-permute-done.9.right_ref.refs_1_), custom_call_target="tpu_custom_call" | custom-call | flops 2415919104 | bytes 7864320 | tf_op jit(solution)/shard_map/pallas_call | solution.py:69
  145.5 10.6 %collective-permute-done.21.three_ref = bf16[256,1536]{1,0:T(8,128)(2,1)S(1)} collective-permute-done((bf16[256,1536]{1,0:T(8,128)(2,1)S(1)}, bf16[256,1536]{1,0:T(8,128)(2,1)S(1)}, u32[]{:S(2)}, u32[]{:S(2)}) %collective-permute-start.21) | collective-permute-done | bytes 786464 | tf_op jit(solution)/shard_map/ppermute | solution.py:30
  158.8 3.1 %collective-permute-done.16.more_ref = bf16[128,1536]{1,0:T(8,128)(2,1)S(1)} collective-permute-done((bf16[128,1536]{1,0:T(8,128)(2,1)S(1)}, bf16[128,1536]{1,0:T(8,128)(2,1)S(1)}, u32[]{:S(2)}, u32[]{:S(2)}) %collective-permute-start.16) | collective-permute-done | bytes 393248 | tf_op jit(solution)/shard_map/ppermute | solution.py:30
  165.0 6.6 %all-to-all-start.3 = ((bf16[8,32,1536]{2,1,0:T(8,128)(2,1)}), bf16[8,32,1536]{2,1,0:T(8,128)(2,1)}, u32[]{:S(2)}, u32[]{:S(2)}) async-start(bf16[8,32,1536]{2,1,0:T(8,128)(2,1)} %bitcast.18), calls=%async_computation.3 | async-start | bytes 1572864 | tf_op jit(solution)/shard_map/all_to_all | solution.py:35
  174.9 6.8 %shard_map.163 = bf16[1536,768]{1,0:T(8,128)(2,1)} custom-call(bf16[8,4,32,1536]{3,2,1,0:T(8,128)(2,1)} %bitcast.17.rows_ref, bf16[256,768]{1,0:T(8,128)(2,1)S(1)} %copy-done.39, bf16[256,768]{1,0:T(8,128)(2,1)S(1)} %copy-done.47, bf16[256,768]{1,0:T(8,128)(2,1)S(1)} %copy-done.49, bf16[256,768]{1,0:T(8,128)(2,1)S(1)} %copy-done.51), custom_call_target="tpu_custom_call" | custom-call | flops 2415919104 | bytes 7077888 | tf_op jit(solution)/shard_map/pallas_call | solution.py:69
  181.7 6.1 %collective-permute-done.17.two_ref = bf16[256,1536]{1,0:T(8,128)(2,1)S(1)} collective-permute-done((bf16[256,1536]{1,0:T(8,128)(2,1)}, bf16[256,1536]{1,0:T(8,128)(2,1)S(1)}, u32[]{:S(2)}, u32[]{:S(2)}) %collective-permute-start.17) | collective-permute-done | bytes 786464 | tf_op jit(solution)/shard_map/ppermute | solution.py:30
  190.7 5.3 %all-to-all-start.4 = ((bf16[8,32,1536]{2,1,0:T(8,128)(2,1)}), bf16[8,32,1536]{2,1,0:T(8,128)(2,1)}, u32[]{:S(2)}, u32[]{:S(2)}) async-start(bf16[8,32,1536]{2,1,0:T(8,128)(2,1)} %bitcast.49), calls=%async_computation.4 | async-start | bytes 1572864 | tf_op jit(solution)/shard_map/all_to_all | solution.py:35
  200.7 6.0 %shard_map.169 = bf16[768,1536]{1,0:T(8,128)(2,1)} custom-call(bf16[256,768]{1,0:T(8,128)(2,1)S(1)} %copy-done.37, bf16[256,768]{1,0:T(8,128)(2,1)S(1)} %copy-done.41, bf16[256,768]{1,0:T(8,128)(2,1)S(1)} %copy-done.43, bf16[256,768]{1,0:T(8,128)(2,1)S(1)} %copy-done.45, bf16[256,1536]{1,0:T(8,128)(2,1)S(1)} %bitcast.46, ...), custom_call_target="tpu_custom_call" | custom-call | flops 2415919104 | bytes 7077888 | tf_op jit(solution)/shard_map/pallas_call | solution.py:69
  209.1 5.1 %all-to-all-done.4 = bf16[8,32,1536]{2,1,0:T(8,128)(2,1)} async-done(((bf16[8,32,1536]{2,1,0:T(8,128)(2,1)}), bf16[8,32,1536]{2,1,0:T(8,128)(2,1)}, u32[]{:S(2)}, u32[]{:S(2)}) %all-to-all-start.4) | async-done | bytes 786464 | tf_op jit(solution)/shard_map/all_to_all | solution.py:35
  (170 shorter events, 80.9 us)
Async XLA Ops:
  8.1 39.9 %all-to-all-start = ((bf16[8,32,1536]{2,1,0:T(8,128)(2,1)}), bf16[8,32,1536]{2,1,0:T(8,128)(2,1)S(1)}, u32[]{:S(2)}, u32[]{:S(2)}) async-start(bf16[8,32,1536]{2,1,0:T(8,128)(2,1)} %bitcast.48), calls=%async_computation | async-start | bytes 1572864 | tf_op jit(solution)/shard_map/all_to_all | solution.py:35
  16.7 12.2 %collective-permute-start.3 = (bf16[128,1664]{1,0:T(8,128)(2,1)}, bf16[128,1664]{1,0:T(8,128)(2,1)S(1)}, u32[]{:S(2)}, u32[]{:S(2)}) collective-permute-start(bf16[128,1664]{1,0:T(8,128)(2,1)} %copy-done.12), channel_id=1, source_target_pairs={{0,3},{1,0},{2,1},{3,2},{4,7},{5,4},{6,5},{7,6},{8,11},{9,8},{10,9... | collective-permute-start | bytes 1277960 | tf_op jit(solution)/shard_map/ppermute | solution.py:30
  19.7 13.1 %collective-permute-start.2 = (bf16[128,1664]{1,0:T(8,128)(2,1)}, bf16[128,1664]{1,0:T(8,128)(2,1)S(1)}, u32[]{:S(2)}, u32[]{:S(2)}) collective-permute-start(bf16[128,1664]{1,0:T(8,128)(2,1)} %copy-done.12), channel_id=1, source_target_pairs={{0,1},{1,2},{2,3},{3,0},{4,5},{5,6},{6,7},{7,4},{8,9},{9,10},{10,1... | collective-permute-start | bytes 1277960 | tf_op jit(solution)/shard_map/ppermute | solution.py:30
  19.7 24.7 %collective-permute-start.1 = (bf16[1,128,1536]{2,1,0:T(8,128)(2,1)}, bf16[1,128,1536]{2,1,0:T(8,128)(2,1)}, u32[]{:S(2)}, u32[]{:S(2)}) collective-permute-start(bf16[1,128,1536]{2,1,0:T(8,128)(2,1)} %param.12), channel_id=1, source_target_pairs={{224,0},{0,32},{32,64},{64,96},{96,128},{128,160},{160,192},{192,2... | collective-permute-start | bytes 1179656 | tf_op jit(solution)/shard_map/ppermute | solution.py:21
  48.0 30.9 %all-to-all-start.1 = ((bf16[8,32,1536]{2,1,0:T(8,128)(2,1)}), bf16[8,32,1536]{2,1,0:T(8,128)(2,1)}, u32[]{:S(2)}, u32[]{:S(2)}) async-start(bf16[8,32,1536]{2,1,0:T(8,128)(2,1)} %bitcast.47), calls=%async_computation.1 | async-start | bytes 1572864 | tf_op jit(solution)/shard_map/all_to_all | solution.py:35
  55.5 20.5 %collective-permute-start.6 = (bf16[256,1536]{1,0:T(8,128)(2,1)S(1)}, bf16[256,1536]{1,0:T(8,128)(2,1)}, u32[]{:S(2)}, u32[]{:S(2)}) collective-permute-start(bf16[256,1536]{1,0:T(8,128)(2,1)S(1)} %bitcast.43), channel_id=1, source_target_pairs={{0,1},{1,2},{2,3},{3,0},{4,5},{5,6},{6,7},{7,4},{8,9},{9,10},{10,1... | collective-permute-start | bytes 2359304 | tf_op jit(solution)/shard_map/ppermute | solution.py:30
  55.5 20.5 %collective-permute-start.7 = (bf16[256,1536]{1,0:T(8,128)(2,1)S(1)}, bf16[256,1536]{1,0:T(8,128)(2,1)}, u32[]{:S(2)}, u32[]{:S(2)}) collective-permute-start(bf16[256,1536]{1,0:T(8,128)(2,1)S(1)} %bitcast.44), channel_id=1, source_target_pairs={{0,3},{1,0},{2,1},{3,2},{4,7},{5,4},{6,5},{7,6},{8,11},{9,8},{10,9... | collective-permute-start | bytes 2359304 | tf_op jit(solution)/shard_map/ppermute | solution.py:30
  78.9 86.1 %all-to-all-start.2 = ((bf16[8,128,1536]{2,1,0:T(8,128)(2,1)}), bf16[8,128,1536]{2,1,0:T(8,128)(2,1)}, u32[]{:S(2)}, u32[]{:S(2)}) async-start(bf16[8,128,1536]{2,1,0:T(8,128)(2,1)} %bitcast.42), calls=%async_computation.2 | async-start | bytes 6291456 | tf_op jit(solution)/shard_map/all_to_all | solution.py:35
  85.5 35.3 %collective-permute-start.9 = (bf16[256,1536]{1,0:T(8,128)(2,1)}, bf16[256,1536]{1,0:T(8,128)(2,1)S(1)}, u32[]{:S(2)}, u32[]{:S(2)}) collective-permute-start(bf16[256,1536]{1,0:T(8,128)(2,1)} %bitcast.13.refs_0_), channel_id=1, source_target_pairs={{0,3},{1,0},{2,1},{3,2},{4,7},{5,4},{6,5},{7,6},{8,11},{9,8},{10,9... | collective-permute-start | bytes 2359304 | tf_op jit(solution)/shard_map/ppermute | solution.py:30
  88.5 32.4 %collective-permute-start.8 = (bf16[256,1536]{1,0:T(8,128)(2,1)}, bf16[256,1536]{1,0:T(8,128)(2,1)S(1)}, u32[]{:S(2)}, u32[]{:S(2)}) collective-permute-start(bf16[256,1536]{1,0:T(8,128)(2,1)} %bitcast.13.refs_0_), channel_id=1, source_target_pairs={{0,1},{1,2},{2,3},{3,0},{4,5},{5,6},{6,7},{7,4},{8,9},{9,10},{10,1... | collective-permute-start | bytes 2359304 | tf_op jit(solution)/shard_map/ppermute | solution.py:30
  88.5 27.0 %collective-permute-start.10 = (bf16[128,1536]{1,0:T(8,128)(2,1)}, bf16[128,1536]{1,0:T(8,128)(2,1)S(1)}, u32[]{:S(2)}, u32[]{:S(2)}) collective-permute-start(bf16[128,1536]{1,0:T(8,128)(2,1)} %copy-done.53), channel_id=1, source_target_pairs={{0,1},{1,2},{2,3},{3,0},{4,5},{5,6},{6,7},{7,4},{8,9},{9,10},{10,1... | collective-permute-start | bytes 1179656 | tf_op jit(solution)/shard_map/ppermute | solution.py:30
  88.5 27.0 %collective-permute-start.11 = (bf16[128,1536]{1,0:T(8,128)(2,1)}, bf16[128,1536]{1,0:T(8,128)(2,1)S(1)}, u32[]{:S(2)}, u32[]{:S(2)}) collective-permute-start(bf16[128,1536]{1,0:T(8,128)(2,1)} %copy-done.52), channel_id=1, source_target_pairs={{0,3},{1,0},{2,1},{3,2},{4,7},{5,4},{6,5},{7,6},{8,11},{9,8},{10,9... | collective-permute-start | bytes 1179656 | tf_op jit(solution)/shard_map/ppermute | solution.py:30
  118.8 12.1 %collective-permute-start.13 = (bf16[128,1536]{1,0:T(8,128)(2,1)S(1)}, bf16[128,1536]{1,0:T(8,128)(2,1)S(1)}, u32[]{:S(2)}, u32[]{:S(2)}) collective-permute-start(bf16[128,1536]{1,0:T(8,128)(2,1)S(1)} %get-tuple-element.68), channel_id=1, source_target_pairs={{0,3},{1,0},{2,1},{3,2},{4,7},{5,4},{6,5},{7,6},{8,11},{9,8},{10,9... | collective-permute-start | bytes 1179656 | tf_op jit(solution)/shard_map/ppermute | solution.py:30
  119.1 13.3 %collective-permute-start.12 = (bf16[128,1536]{1,0:T(8,128)(2,1)S(1)}, bf16[128,1536]{1,0:T(8,128)(2,1)S(1)}, u32[]{:S(2)}, u32[]{:S(2)}) collective-permute-start(bf16[128,1536]{1,0:T(8,128)(2,1)S(1)} %get-tuple-element.66), channel_id=1, source_target_pairs={{0,1},{1,2},{2,3},{3,0},{4,5},{5,6},{6,7},{7,4},{8,9},{9,10},{10,1... | collective-permute-start | bytes 1179656 | tf_op jit(solution)/shard_map/ppermute | solution.py:30
  121.3 19.5 %collective-permute-start.14 = (bf16[128,1536]{1,0:T(8,128)(2,1)S(1)}, bf16[128,1536]{1,0:T(8,128)(2,1)S(1)}, u32[]{:S(2)}, u32[]{:S(2)}) collective-permute-start(bf16[128,1536]{1,0:T(8,128)(2,1)S(1)} %get-tuple-element.54), channel_id=1, source_target_pairs={{0,1},{1,2},{2,3},{3,0},{4,5},{5,6},{6,7},{7,4},{8,9},{9,10},{10,1... | collective-permute-start | bytes 1179656 | tf_op jit(solution)/shard_map/ppermute | solution.py:30
  121.4 19.4 %collective-permute-start.15 = (bf16[128,1536]{1,0:T(8,128)(2,1)S(1)}, bf16[128,1536]{1,0:T(8,128)(2,1)S(1)}, u32[]{:S(2)}, u32[]{:S(2)}) collective-permute-start(bf16[128,1536]{1,0:T(8,128)(2,1)S(1)} %get-tuple-element.55), channel_id=1, source_target_pairs={{0,3},{1,0},{2,1},{3,2},{4,7},{5,4},{6,5},{7,6},{8,11},{9,8},{10,9... | collective-permute-start | bytes 1179656 | tf_op jit(solution)/shard_map/ppermute | solution.py:30
  132.4 23.8 %collective-permute-start.21 = (bf16[256,1536]{1,0:T(8,128)(2,1)S(1)}, bf16[256,1536]{1,0:T(8,128)(2,1)S(1)}, u32[]{:S(2)}, u32[]{:S(2)}) collective-permute-start(bf16[256,1536]{1,0:T(8,128)(2,1)S(1)} %shard_map.159), channel_id=1, source_target_pairs={{0,3},{1,0},{2,1},{3,2},{4,7},{5,4},{6,5},{7,6},{8,11},{9,8},{10,9... | collective-permute-start | bytes 2359304 | tf_op jit(solution)/shard_map/ppermute | solution.py:30
  133.1 24.6 %collective-permute-start.20 = (bf16[256,1536]{1,0:T(8,128)(2,1)S(1)}, bf16[256,1536]{1,0:T(8,128)(2,1)S(1)}, u32[]{:S(2)}, u32[]{:S(2)}) collective-permute-start(bf16[256,1536]{1,0:T(8,128)(2,1)S(1)} %shard_map.158), channel_id=1, source_target_pairs={{0,1},{1,2},{2,3},{3,0},{4,5},{5,6},{6,7},{7,4},{8,9},{9,10},{10,1... | collective-permute-start | bytes 2359304 | tf_op jit(solution)/shard_map/ppermute | solution.py:30
  142.2 19.7 %collective-permute-start.16 = (bf16[128,1536]{1,0:T(8,128)(2,1)S(1)}, bf16[128,1536]{1,0:T(8,128)(2,1)S(1)}, u32[]{:S(2)}, u32[]{:S(2)}) collective-permute-start(bf16[128,1536]{1,0:T(8,128)(2,1)S(1)} %get-tuple-element.74), channel_id=1, source_target_pairs={{0,1},{1,2},{2,3},{3,0},{4,5},{5,6},{6,7},{7,4},{8,9},{9,10},{10,1... | collective-permute-start | bytes 1179656 | tf_op jit(solution)/shard_map/ppermute | solution.py:30
  142.9 20.9 %collective-permute-start.18 = (bf16[128,1536]{1,0:T(8,128)(2,1)S(1)}, bf16[128,1536]{1,0:T(8,128)(2,1)S(1)}, u32[]{:S(2)}, u32[]{:S(2)}) collective-permute-start(bf16[128,1536]{1,0:T(8,128)(2,1)S(1)} %get-tuple-element.81), channel_id=1, source_target_pairs={{0,3},{1,0},{2,1},{3,2},{4,7},{5,4},{6,5},{7,6},{8,11},{9,8},{10,9... | collective-permute-start | bytes 1179656 | tf_op jit(solution)/shard_map/ppermute | solution.py:30
  165.0 25.7 %all-to-all-start.3 = ((bf16[8,32,1536]{2,1,0:T(8,128)(2,1)}), bf16[8,32,1536]{2,1,0:T(8,128)(2,1)}, u32[]{:S(2)}, u32[]{:S(2)}) async-start(bf16[8,32,1536]{2,1,0:T(8,128)(2,1)} %bitcast.18), calls=%async_computation.3 | async-start | bytes 1572864 | tf_op jit(solution)/shard_map/all_to_all | solution.py:35
  171.6 16.2 %collective-permute-start.17 = (bf16[256,1536]{1,0:T(8,128)(2,1)}, bf16[256,1536]{1,0:T(8,128)(2,1)S(1)}, u32[]{:S(2)}, u32[]{:S(2)}) collective-permute-start(bf16[256,1536]{1,0:T(8,128)(2,1)} %shard_map.162), channel_id=1, source_target_pairs={{0,1},{1,2},{2,3},{3,0},{4,5},{5,6},{6,7},{7,4},{8,9},{9,10},{10,1... | collective-permute-start | bytes 2359304 | tf_op jit(solution)/shard_map/ppermute | solution.py:30
  171.9 16.0 %collective-permute-start.19 = (bf16[256,1536]{1,0:T(8,128)(2,1)}, bf16[256,1536]{1,0:T(8,128)(2,1)S(1)}, u32[]{:S(2)}, u32[]{:S(2)}) collective-permute-start(bf16[256,1536]{1,0:T(8,128)(2,1)} %copy-done.26), channel_id=1, source_target_pairs={{0,3},{1,0},{2,1},{3,2},{4,7},{5,4},{6,5},{7,6},{8,11},{9,8},{10,9... | collective-permute-start | bytes 2359304 | tf_op jit(solution)/shard_map/ppermute | solution.py:30
  190.7 23.6 %all-to-all-start.4 = ((bf16[8,32,1536]{2,1,0:T(8,128)(2,1)}), bf16[8,32,1536]{2,1,0:T(8,128)(2,1)}, u32[]{:S(2)}, u32[]{:S(2)}) async-start(bf16[8,32,1536]{2,1,0:T(8,128)(2,1)} %bitcast.49), calls=%async_computation.4 | async-start | bytes 1572864 | tf_op jit(solution)/shard_map/all_to_all | solution.py:35
  (59 other events, 406.9 us)
